TPU v7x, 32 devices: a whole 2x2x4 slice. The times are simulated.
32 devices in a mesh: fsdp: 32 (over z, y, x, core).
Axes of the slice: x: 2, y: 2, z: 4, core: 2. Of those that a mesh axis runs over, the one named last changes fastest.
Arguments:
- latents_in: bfloat16 [128, 256, 384], P('fsdp'), may hold values from -6 to 6
- condition: bfloat16 [128, 384], P('fsdp'), may hold values from -6 to 6
- counts: int32 [32], P('fsdp'), may hold values from 3 to 4, as said below
- ada_weight: bfloat16 [2, 884736], P(None, 'fsdp'), may hold values from -0.3125 to 0.3125
- qkv_weight: bfloat16 [2, 442368], P(None, 'fsdp'), may hold values from -0.3125 to 0.3125
- proj_weight: bfloat16 [2, 147456], P(None, 'fsdp'), may hold values from -2.5 to 2.5
- fc1_weight: bfloat16 [2, 589824], P(None, 'fsdp'), may hold values from -0.3125 to 0.3125
- fc2_weight: bfloat16 [2, 589824], P(None, 'fsdp'), may hold values from -0.15625 to 0.15625
- biases: bfloat16 [2, 8192], P(None, 'fsdp'), may hold values from -3 to 3
- cotangent: bfloat16 [128, 256, 384], P('fsdp'), may hold values from -6 to 6
Outputs:
- latents_out: float32 [128, 256, 384], P('fsdp')
- latents_grad: float32 [128, 256, 384], P('fsdp')
- condition_grad: float32 [128, 384], P('fsdp')
- ada_grad: float32 [2, 884736], P(None, 'fsdp')
- qkv_grad: float32 [2, 442368], P(None, 'fsdp')
- proj_grad: float32 [2, 147456], P(None, 'fsdp')
- fc1_grad: float32 [2, 589824], P(None, 'fsdp')
- fc2_grad: float32 [2, 589824], P(None, 'fsdp')
- bias_grad: float32 [2, 8192], P(None, 'fsdp')
Inputs may be any that keep to these rules, and one draw needn't show every extreme that they name: Each device holds 3 or 4 latents, in its first slots; both counts occur in every draw.
All inputs are finite; a program needn't handle non-finite values.
Results may differ from a plain program's by a relative error of at most 0.022.
The roundings to bfloat16 on the way count: a program that leaves them out, or rounds other values in their place, can miss the bound.
Values may be sent and summed in bfloat16 or wider, within the bound.
No kernel may reach another device: no remote copies, remote signals or barrier semaphores. Data moves between devices by JAX's collectives and lax.ppermute only.
A program may use at most 192 MiB of HBM per device.

v0:
```python
import math

import jax
import jax.numpy as jnp
from jax import lax
from jax.sharding import PartitionSpec as P

D = 384
HEADS = 6
HEAD = 64
FF = 1536


EPSILON = 1e-06


def modulate_norm(values_in, shift_add, scale_mul):
    centred = values_in - jnp.mean(values_in, axis=-1, keepdims=True)
    variance = jnp.mean(centred * centred, axis=-1, keepdims=True)
    normed = centred * lax.rsqrt(variance + EPSILON)
    return normed * (1.0 + scale_mul[:, None, :]) + shift_add[:, None, :]


def gelu_tanh(values_in):
    return jax.nn.gelu(values_in, approximate=True)


def left_product(left, right):
    return lax.dot_general(
        left, right, (((0,), (0,)), ((), ())), preferred_element_type=jnp.float32
    )


def right_product(left, right):
    return lax.dot_general(
        left, right, (((1,), (1,)), ((), ())), preferred_element_type=jnp.float32
    )


def unpack(gathered):
    ada_flat, qkv_flat, proj_flat, fc1_flat, fc2_flat, bias_flat = gathered
    bias_wide = bias_flat.astype(jnp.float32)
    return (
        ada_flat.reshape(D, 6 * D),
        qkv_flat[: 3 * D * D].reshape(D, 3 * D),
        proj_flat[: D * D].reshape(D, D),
        fc1_flat.reshape(D, FF),
        fc2_flat.reshape(FF, D),
        bias_wide[: 6 * D],
        bias_wide[6 * D : 7 * D],
        bias_wide[7 * D : 8 * D],
        bias_wide[8 * D : 9 * D],
        bias_wide[9 * D : 9 * D + FF],
        bias_wide[9 * D + FF : 10 * D + FF],
    )


def split_modulation(modulation):
    return [modulation[:, part_index * D : (part_index + 1) * D] for part_index in range(6)]


def layer_forward(hidden, cond_act, params):
    w_ada, w_qkv, w_proj, w_fc1, w_fc2, b_ada, b_query, b_value, b_proj, b_fc1, b_fc2 = params
    slot_count, seq_len = (hidden.shape[0], hidden.shape[1])
    modulation = jnp.dot(cond_act, w_ada, preferred_element_type=jnp.float32) + b_ada
    shift_attn, scale_attn, gate_attn, shift_ffn, scale_ffn, gate_ffn = split_modulation(modulation)
    normed_attn = modulate_norm(hidden, shift_attn, scale_attn).astype(jnp.bfloat16).reshape(-1, D)
    mixed_qkv = jnp.dot(normed_attn, w_qkv, preferred_element_type=jnp.float32)
    queries = (
        (mixed_qkv[:, 0:D] + b_query).astype(jnp.bfloat16).reshape(slot_count, seq_len, HEADS, HEAD)
    )
    key_heads = (
        mixed_qkv[:, D : 2 * D].astype(jnp.bfloat16).reshape(slot_count, seq_len, HEADS, HEAD)
    )
    value_heads = (
        (mixed_qkv[:, 2 * D : 3 * D] + b_value)
        .astype(jnp.bfloat16)
        .reshape(slot_count, seq_len, HEADS, HEAD)
    )
    scores = jnp.einsum(
        "bqhd,bkhd->bhqk", queries, key_heads, preferred_element_type=jnp.float32
    ) * (1.0 / math.sqrt(HEAD))
    peak_score = jnp.max(scores, axis=-1, keepdims=True)
    exp_scores = jnp.exp(scores - peak_score)
    exp_total = jnp.sum(exp_scores, axis=-1, keepdims=True)
    logsum = peak_score + jnp.log(exp_total)
    attn_probs = (exp_scores / exp_total).astype(jnp.bfloat16)
    attended = jnp.einsum(
        "bhqk,bkhd->bqhd", attn_probs, value_heads, preferred_element_type=jnp.float32
    )
    attended = attended.astype(jnp.bfloat16).reshape(-1, D)
    projected = (jnp.dot(attended, w_proj, preferred_element_type=jnp.float32) + b_proj).reshape(
        slot_count, seq_len, D
    )
    middle = hidden + gate_attn[:, None, :] * projected
    normed_ffn = modulate_norm(middle, shift_ffn, scale_ffn).astype(jnp.bfloat16).reshape(-1, D)
    pre_act = jnp.dot(normed_ffn, w_fc1, preferred_element_type=jnp.float32) + b_fc1
    activation = gelu_tanh(pre_act).astype(jnp.bfloat16)
    branch = (jnp.dot(activation, w_fc2, preferred_element_type=jnp.float32) + b_fc2).reshape(
        slot_count, seq_len, D
    )
    result = middle + gate_ffn[:, None, :] * branch
    record = (
        hidden,
        modulation,
        normed_attn,
        queries,
        key_heads,
        value_heads,
        logsum,
        attended,
        projected,
        middle,
        normed_ffn,
        pre_act,
        activation,
        branch,
    )
    return (result, record)


def layer_backward(upstream, params, record):
    w_ada, w_qkv, w_proj, w_fc1, w_fc2, b_ada, b_query, b_value, b_proj, b_fc1, b_fc2 = params
    (
        hidden,
        modulation,
        normed_attn,
        queries,
        key_heads,
        value_heads,
        logsum,
        attended,
        projected,
        middle,
        normed_ffn,
        pre_act,
        activation,
        branch,
    ) = record
    slot_count, seq_len = (hidden.shape[0], hidden.shape[1])
    shift_attn, scale_attn, gate_attn, shift_ffn, scale_ffn, gate_ffn = split_modulation(modulation)
    d_branch = (upstream * gate_ffn[:, None, :]).reshape(-1, D)
    d_gate_ffn = jnp.sum(upstream * branch, axis=1)
    grad_b_fc2 = jnp.sum(d_branch, axis=0)
    branch_low = d_branch.astype(jnp.bfloat16)
    grad_w_fc2 = left_product(activation, branch_low)
    d_act = right_product(branch_low, w_fc2)
    gelu_out, gelu_pull = jax.vjp(gelu_tanh, pre_act)
    (d_pre,) = gelu_pull(d_act)
    grad_b_fc1 = jnp.sum(d_pre, axis=0)
    pre_low = d_pre.astype(jnp.bfloat16)
    grad_w_fc1 = left_product(normed_ffn, pre_low)
    d_normed_ffn = right_product(pre_low, w_fc1).reshape(slot_count, seq_len, D)
    norm_out, norm_pull = jax.vjp(modulate_norm, middle, shift_ffn, scale_ffn)
    middle_part, d_shift_ffn, d_scale_ffn = norm_pull(d_normed_ffn)
    d_middle = upstream + middle_part
    d_proj = (d_middle * gate_attn[:, None, :]).reshape(-1, D)
    d_gate_attn = jnp.sum(d_middle * projected, axis=1)
    grad_b_proj = jnp.sum(d_proj, axis=0)
    proj_low = d_proj.astype(jnp.bfloat16)
    grad_w_proj = left_product(attended, proj_low)
    d_attended = (
        right_product(proj_low, w_proj)
        .astype(jnp.bfloat16)
        .reshape(slot_count, seq_len, HEADS, HEAD)
    )
    scores = jnp.einsum(
        "bqhd,bkhd->bhqk", queries, key_heads, preferred_element_type=jnp.float32
    ) * (1.0 / math.sqrt(HEAD))
    attn_probs = jnp.exp(scores - logsum)
    d_probs = jnp.einsum(
        "bqhd,bkhd->bhqk", d_attended, value_heads, preferred_element_type=jnp.float32
    )
    d_values = jnp.einsum(
        "bhqk,bqhd->bkhd",
        attn_probs.astype(jnp.bfloat16),
        d_attended,
        preferred_element_type=jnp.float32,
    )
    row_inner = jnp.sum(attn_probs * d_probs, axis=-1, keepdims=True)
    d_scores = (attn_probs * (d_probs - row_inner) * (1.0 / math.sqrt(HEAD))).astype(jnp.bfloat16)
    d_query = jnp.einsum(
        "bhqk,bkhd->bqhd", d_scores, key_heads, preferred_element_type=jnp.float32
    ).reshape(-1, D)
    d_keys = jnp.einsum(
        "bhqk,bqhd->bkhd", d_scores, queries, preferred_element_type=jnp.float32
    ).reshape(-1, D)
    d_values = d_values.reshape(-1, D)
    grad_b_query = jnp.sum(d_query, axis=0)
    grad_b_value = jnp.sum(d_values, axis=0)
    mixed_low = jnp.concatenate([d_query, d_keys, d_values], axis=1).astype(jnp.bfloat16)
    grad_w_qkv = left_product(normed_attn, mixed_low)
    d_normed_attn = right_product(mixed_low, w_qkv).reshape(slot_count, seq_len, D)
    attn_out, attn_pull = jax.vjp(modulate_norm, hidden, shift_attn, scale_attn)
    hidden_part, d_shift_attn, d_scale_attn = attn_pull(d_normed_attn)
    d_hidden = d_middle + hidden_part
    d_mod = jnp.concatenate(
        [d_shift_attn, d_scale_attn, d_gate_attn, d_shift_ffn, d_scale_ffn, d_gate_ffn], axis=1
    )
    grad_b_ada = jnp.sum(d_mod, axis=0)
    mod_low = d_mod.astype(jnp.bfloat16)
    d_cond = right_product(mod_low, w_ada)
    grad_bias = jnp.concatenate(
        [grad_b_ada, grad_b_query, grad_b_value, grad_b_proj, grad_b_fc1, grad_b_fc2]
    )
    return (d_hidden, d_cond, mod_low, (grad_w_qkv, grad_w_proj, grad_w_fc1, grad_w_fc2, grad_bias))


def pad_flat(values_in, length):
    flat = values_in.reshape(-1)
    return jnp.pad(flat, (0, length - flat.shape[0]))


def body(
    latents_in,
    condition,
    counts,
    ada_weight,
    qkv_weight,
    proj_weight,
    fc1_weight,
    fc2_weight,
    biases,
    cotangent,
):
    slot_count = latents_in.shape[0]
    layer_total = ada_weight.shape[0]
    device_count = lax.axis_size("fsdp")
    rest_list = (qkv_weight, proj_weight, fc1_weight, fc2_weight, biases)
    rest_lengths = [piece.shape[1] * device_count for piece in rest_list]
    ada_shard = ada_weight.shape[1]
    occupied = (jnp.arange(slot_count) < counts[0]).astype(jnp.float32)
    cond_wide = condition.astype(jnp.float32)
    silu_out, silu_pull = jax.vjp(jax.nn.silu, cond_wide)
    cond_act = silu_out.astype(jnp.bfloat16)
    hidden = latents_in.astype(jnp.float32)
    records = []
    for layer_index in range(layer_total):
        gathered = (
            lax.all_gather(ada_weight[layer_index], "fsdp", axis=0, tiled=True),
            lax.all_gather(qkv_weight[layer_index], "fsdp", axis=0, tiled=True),
            lax.all_gather(proj_weight[layer_index], "fsdp", axis=0, tiled=True),
            lax.all_gather(fc1_weight[layer_index], "fsdp", axis=0, tiled=True),
            lax.all_gather(fc2_weight[layer_index], "fsdp", axis=0, tiled=True),
            lax.all_gather(biases[layer_index], "fsdp", axis=0, tiled=True),
        )
        params = unpack(gathered)
        hidden, record = layer_forward(hidden, cond_act, params)
        records.append(record)
    latents_out = hidden * occupied[:, None, None]
    upstream = cotangent.astype(jnp.float32) * occupied[:, None, None]
    cond_total = jnp.zeros(cond_wide.shape, jnp.float32)
    layer_sums = [None] * layer_total
    mod_lows = [None] * layer_total
    for layer_index in reversed(range(layer_total)):
        gathered = (
            lax.all_gather(ada_weight[layer_index], "fsdp", axis=0, tiled=True),
            lax.all_gather(qkv_weight[layer_index], "fsdp", axis=0, tiled=True),
            lax.all_gather(proj_weight[layer_index], "fsdp", axis=0, tiled=True),
            lax.all_gather(fc1_weight[layer_index], "fsdp", axis=0, tiled=True),
            lax.all_gather(fc2_weight[layer_index], "fsdp", axis=0, tiled=True),
            lax.all_gather(biases[layer_index], "fsdp", axis=0, tiled=True),
        )
        params = unpack(gathered)
        upstream, d_cond, mod_low, grad_parts = layer_backward(
            upstream, params, records[layer_index]
        )
        mod_lows[layer_index] = mod_low
        cond_total = cond_total + d_cond
        padded = [
            pad_flat(grad_parts[part_index], rest_lengths[part_index]) for part_index in range(5)
        ]
        layer_sums[layer_index] = (
            lax.psum_scatter(padded[0], "fsdp", scatter_dimension=0, tiled=True),
            lax.psum_scatter(padded[1], "fsdp", scatter_dimension=0, tiled=True),
            lax.psum_scatter(padded[2], "fsdp", scatter_dimension=0, tiled=True),
            lax.psum_scatter(padded[3], "fsdp", scatter_dimension=0, tiled=True),
            lax.psum_scatter(padded[4], "fsdp", scatter_dimension=0, tiled=True),
        )
    grad_rest = [
        jnp.stack([layer_sums[layer_index][part_index] for layer_index in range(layer_total)])
        for part_index in range(5)
    ]
    mod_joined = jnp.concatenate(mod_lows, axis=1)
    ada_full = left_product(
        lax.all_gather(cond_act, "fsdp", axis=0, tiled=True),
        lax.all_gather(mod_joined, "fsdp", axis=0, tiled=True),
    )
    own_start = lax.axis_index("fsdp") * ada_shard
    ada_rows = []
    for layer_index in range(layer_total):
        flat_layer = pad_flat(
            ada_full[:, layer_index * 6 * D : (layer_index + 1) * 6 * D], ada_shard * device_count
        )
        ada_rows.append(lax.dynamic_slice_in_dim(flat_layer, own_start, ada_shard))
    ada_grad = jnp.stack(ada_rows)
    (condition_grad,) = silu_pull(cond_total)
    return (
        latents_out,
        upstream,
        condition_grad,
        ada_grad,
        grad_rest[0],
        grad_rest[1],
        grad_rest[2],
        grad_rest[3],
        grad_rest[4],
    )


def solution(mesh):
    return jax.shard_map(
        body,
        mesh=mesh,
        in_specs=(
            P("fsdp", None, None),
            P("fsdp", None),
            P("fsdp"),
            P(None, "fsdp"),
            P(None, "fsdp"),
            P(None, "fsdp"),
            P(None, "fsdp"),
            P(None, "fsdp"),
            P(None, "fsdp"),
            P("fsdp", None, None),
        ),
        out_specs=(
            P("fsdp", None, None),
            P("fsdp", None, None),
            P("fsdp", None),
            P(None, "fsdp"),
            P(None, "fsdp"),
            P(None, "fsdp"),
            P(None, "fsdp"),
            P(None, "fsdp"),
            P(None, "fsdp"),
        ),
        check_vma=False,
    )
```

profile of v0, /device:TPU:0, one launch (start us, length us, event | category | flops | bytes accessed | tf_op | source)
XLA Modules:
  0.0 1176.4 jit_solution(3500207744249926017)
XLA Ops:
  15.7 50.3 %all-gather.8 = bf16[1,442368]{1,0:T(2,128)(2,1)S(1)} all-gather(bf16[1,13824]{1,0:T(2,128)(2,1)S(1)} %get-tuple-element.75), channel_id=10, replica_groups=mesh['fsdp'=32] {'fsdp'}, dimensions={1}, use_global_device_ids=true | all-gather | bytes 912384 | tf_op jit(solution)/shard_map/all_gather | solution.py:241
  66.0 18.3 %reduce.21 = bf16[442368]{0:T(1024)(128)(2,1)S(1)} reduce(bf16[1,442368]{1,0:T(2,128)(2,1)S(1)} %all-gather.8, bf16[]{:T(256)} %constant.93), dimensions={0}, to_apply=%all-gather.8.reduce_sub_computation | reduce | bytes 1769474 | tf_op jit(solution)/shard_map/all_gather | solution.py:241
  88.2 44.3 %all-gather.2 = bf16[1,442368]{1,0:T(2,128)(2,1)S(1)} all-gather(bf16[1,13824]{1,0:T(2,128)(2,1)S(1)} %get-tuple-element.76), channel_id=4, replica_groups=mesh['fsdp'=32] {'fsdp'}, dimensions={1}, use_global_device_ids=true | all-gather | bytes 912384 | tf_op jit(solution)/shard_map/all_gather | solution.py:241
  132.5 18.3 %reduce.10 = bf16[442368]{0:T(1024)(128)(2,1)S(1)} reduce(bf16[1,442368]{1,0:T(2,128)(2,1)S(1)} %all-gather.2, bf16[]{:T(256)} %constant.93), dimensions={0}, to_apply=%all-gather.2.reduce_sub_computation | reduce | bytes 1769474 | tf_op jit(solution)/shard_map/all_gather | solution.py:241
  154.5 39.7 %all-gather.7 = bf16[1,8192]{1,0:T(2,128)(2,1)S(1)} all-gather(bf16[1,256]{1,0:T(2,128)(2,1)S(1)} %get-tuple-element.95), channel_id=9, replica_groups=mesh['fsdp'=32] {'fsdp'}, dimensions={1}, use_global_device_ids=true | all-gather | bytes 16896 | tf_op jit(solution)/shard_map/all_gather | solution.py:245
  194.3 36.7 %all-gather.1 = bf16[1,8192]{1,0:T(2,128)(2,1)S(1)} all-gather(bf16[1,256]{1,0:T(2,128)(2,1)S(1)} %get-tuple-element.96), channel_id=3, replica_groups=mesh['fsdp'=32] {'fsdp'}, dimensions={1}, use_global_device_ids=true | all-gather | bytes 16896 | tf_op jit(solution)/shard_map/all_gather | solution.py:245
  231.0 40.2 %all-gather.9 = bf16[1,147456]{1,0:T(2,128)(2,1)S(1)} all-gather(bf16[1,4608]{1,0:T(2,128)(2,1)S(1)} %get-tuple-element.93), channel_id=11, replica_groups=mesh['fsdp'=32] {'fsdp'}, dimensions={1}, use_global_device_ids=true | all-gather | bytes 304128 | tf_op jit(solution)/shard_map/all_gather | solution.py:242
  278.3 39.3 %all-gather.3 = bf16[1,147456]{1,0:T(2,128)(2,1)S(1)} all-gather(bf16[1,4608]{1,0:T(2,128)(2,1)S(1)} %get-tuple-element.94), channel_id=5, replica_groups=mesh['fsdp'=32] {'fsdp'}, dimensions={1}, use_global_device_ids=true | all-gather | bytes 304128 | tf_op jit(solution)/shard_map/all_gather | solution.py:242
  328.3 25.6 %reduce.15 = bf16[589824]{0:T(1024)(128)(2,1)S(1)} reduce(bf16[1,589824]{1,0:T(2,128)(2,1)} %all-gather.24.cloned.1.call-done, bf16[]{:T(256)} %constant.93), dimensions={0}, to_apply=%all-gather.4.reduce_sub_computation | reduce | bytes 2359298 | tf_op jit(solution)/shard_map/all_gather | solution.py:243
  358.3 25.7 %reduce.26 = bf16[589824]{0:T(1024)(128)(2,1)S(1)} reduce(bf16[1,589824]{1,0:T(2,128)(2,1)} %all-gather.30.cloned.1.call-done, bf16[]{:T(256)} %constant.93), dimensions={0}, to_apply=%all-gather.10.reduce_sub_computation | reduce | bytes 2359298 | tf_op jit(solution)/shard_map/all_gather | solution.py:243
  388.3 25.5 %reduce.28 = bf16[589824]{0:T(1024)(128)(2,1)S(1)} reduce(bf16[1,589824]{1,0:T(2,128)(2,1)} %all-gather.32.cloned.1.call-done, bf16[]{:T(256)} %constant.93), dimensions={0}, to_apply=%all-gather.11.reduce_sub_computation | reduce | bytes 2359298 | tf_op jit(solution)/shard_map/all_gather | solution.py:244
  415.3 25.9 %reduce.17 = bf16[589824]{0:T(1024)(128)(2,1)S(1)} reduce(bf16[1,589824]{1,0:T(2,128)(2,1)} %all-gather.26.cloned.1.call-done, bf16[]{:T(256)} %constant.93), dimensions={0}, to_apply=%all-gather.5.reduce_sub_computation | reduce | bytes 2359298 | tf_op jit(solution)/shard_map/all_gather | solution.py:244
  442.7 39.1 %reduce.19 = bf16[884736]{0:T(1024)(128)(2,1)} reduce(bf16[1,884736]{1,0:T(2,128)(2,1)} %all-gather.28.cloned.1.call-done, bf16[]{:T(256)} %constant.93), dimensions={0}, to_apply=%all-gather.6.reduce_sub_computation | reduce | bytes 3538946 | tf_op jit(solution)/shard_map/all_gather | solution.py:240
  485.4 39.4 %reduce.8 = bf16[884736]{0:T(1024)(128)(2,1)} reduce(bf16[1,884736]{1,0:T(2,128)(2,1)} %all-gather.22.cloned.1.call-done, bf16[]{:T(256)} %constant.93), dimensions={0}, to_apply=%all-gather.reduce_sub_computation | reduce | bytes 3538946 | tf_op jit(solution)/shard_map/all_gather | solution.py:240
  589.7 6.6 fusion.176
  621.1 11.5 fusion.109
  632.7 13.0 %bitcast_convert_fusion.3 = (bf16[4,256,6,64]{1,3,2,0:T(8,128)(2,1)}, f32[4,6,64,256]{3,2,1,0:T(8,128)}) fusion(f32[4,6,256,256]{2,3,1,0:T(8,128)} %fusion.118, f32[4,6,256,256]{2,3,1,0:T(8,128)} %copy-done.1, f32[4,6,256]{2,1,0:T(8,128)S(1)} %log_add_fusion.1, bf16[4,256,6,64]{1,0,3,2:T(4,128)(2,1)S(1)} %copy-done.50), kind=kOutput, calls=%fused_computation.119 | convolution fusion | flops 215881984 | bytes 15753216 | tf_op jit(solution)/shard_map/bhqk,bkhd->bqhd/dot_general | solution.py:182
  658.1 7.0 fusion.175
  686.3 12.4 %fusion.106 = bf16[4,6,64,256]{3,2,1,0:T(8,128)(2,1)} fusion(f32[4,6,256,256]{2,3,1,0:T(8,128)} %fusion.115, f32[4,6,256,256]{2,3,1,0:T(8,128)} %copy-done, f32[4,6,256]{2,1,0:T(8,128)S(1)} %log_add_fusion, bf16[4,256,6,64]{1,0,3,2:T(4,128)(2,1)} %copy-done.49), kind=kOutput, calls=%fused_computation.159 | convolution fusion | flops 215881984 | bytes 14180352 | tf_op jit(solution)/shard_map/bhqk,bqhd->bkhd/dot_general | solution.py:185
  698.8 12.7 %bitcast_convert_fusion.1 = (bf16[4,256,6,64]{1,3,2,0:T(8,128)(2,1)}, f32[4,6,64,256]{3,2,1,0:T(8,128)}) fusion(f32[4,6,256,256]{2,3,1,0:T(8,128)} %fusion.115, f32[4,6,256,256]{2,3,1,0:T(8,128)} %copy-done, f32[4,6,256]{2,1,0:T(8,128)S(1)} %log_add_fusion, bf16[4,256,6,64]{1,0,3,2:T(4,128)(2,1)S(1)} %copy-done.47), kind=kOutput, calls=%fused_computation.115 | convolution fusion | flops 215881984 | bytes 15753216 | tf_op jit(solution)/shard_map/bhqk,bkhd->bqhd/dot_general | solution.py:182
  786.7 38.5 %all-gather.12 = bf16[32,4,384]{2,1,0:T(4,128)(2,1)S(1)} all-gather(bf16[1,4,384]{2,1,0:T(4,128)(2,1)S(1)} %fusion.168), channel_id=1, replica_groups=mesh['fsdp'=32] {'fsdp'}, dimensions={0}, use_global_device_ids=true | all-gather | bytes 101376 | tf_op jit(solution)/shard_map/all_gather | solution.py:286
  830.9 12.0 %all-reduce.17.cloned.1.call-done = (f32[8192]{0:T(1024)}, f32[8192]{0:T(1024)}) async-done(((f32[8192]{0:T(1024)}, f32[8192]{0:T(1024)}), (f32[8192]{0:T(1024)}, f32[8192]{0:T(1024)})) %all-reduce.17.cloned.1.call-update) | async-done | bytes 65552
  845.0 56.6 %all-gather.34.cloned.1.call-done = bf16[32,4,4608]{2,1,0:T(4,128)(2,1)} async-done(((bf16[1,4,4608]{2,1,0:T(4,128)(2,1)}), bf16[32,4,4608]{2,1,0:T(4,128)(2,1)}) %all-gather.34.cloned.1.call-update) | async-done | bytes 1179664 | tf_op jit(solution)/shard_map/all_gather | solution.py:287
  918.7 241.4 %all-reduce.19.cloned.1.call-done = (f32[442368]{0:T(1024)}, f32[442368]{0:T(1024)}, f32[147456]{0:T(1024)}, f32[147456]{0:T(1024)}, f32[589824]{0:T(1024)}, /*i...) async-done(((f32[442368]{0:T(1024)}, f32[442368]{0:T(1024)}, f32[147456]{0:T(1024)}, f32[147456]{0:T(1024)}, f32[589824]{0:T(1024)}, /*index=5*/f32[589824]{0:T(1024)}, ...) | async-done | bytes 14155792
  (499 shorter events, 279.7 us)
Async XLA Ops:
  7.2 321.1 %all-gather.24.cloned.1.call-start = ((), (), s32[]{:S(2)}) async-start(), calls=%async_computation.1 | async-start | bytes 2433024 | tf_op jit(solution)/shard_map/all_gather | solution.py:243
  9.0 349.3 %all-gather.30.cloned.1.call-start = ((), (), s32[]{:S(2)}) async-start(), calls=%async_computation.4 | async-start | bytes 2433024 | tf_op jit(solution)/shard_map/all_gather | solution.py:243
  9.7 378.6 %all-gather.32.cloned.1.call-start = ((), (), s32[]{:S(2)}) async-start(), calls=%async_computation.5 | async-start | bytes 2433024 | tf_op jit(solution)/shard_map/all_gather | solution.py:244
  11.6 403.7 %all-gather.26.cloned.1.call-start = ((), (), s32[]{:S(2)}) async-start(), calls=%async_computation.2 | async-start | bytes 2433024 | tf_op jit(solution)/shard_map/all_gather | solution.py:244
  12.1 430.5 %all-gather.28.cloned.1.call-start = ((), (), s32[]{:S(2)}) async-start(), calls=%async_computation.3 | async-start | bytes 3649536 | tf_op jit(solution)/shard_map/all_gather | solution.py:240
  14.1 471.3 %all-gather.22.cloned.1.call-start = ((), (), s32[]{:S(2)}) async-start(), calls=%async_computation | async-start | bytes 3649536 | tf_op jit(solution)/shard_map/all_gather | solution.py:240
  14.6 828.2 %all-reduce.17.cloned.1.call-start = ((), (), s32[]{:S(2)}) async-start(), calls=%async_computation.7 | async-start | bytes 131072
  150.8 80.2 %copy-start.74 = (bf16[2,4608]{1,0:T(2,128)(2,1)S(1)}, bf16[2,4608]{1,0:T(2,128)(2,1)}, u32[]{:S(2)}) copy-start(bf16[2,4608]{1,0:T(2,128)(2,1)} %param.15) | copy-start | bytes 55300
  271.3 56.3 %copy-start.6 = (bf16[4,256,384]{2,1,0:T(8,128)(2,1)S(1)}, bf16[4,256,384]{2,1,0:T(8,128)(2,1)}, u32[]{:S(2)}) copy-start(bf16[4,256,384]{2,1,0:T(8,128)(2,1)} %param.10) | copy-start | bytes 2359300
  328.3 25.6 %copy-start.82 = (f32[4,256]{1,0:T(4,128)}, f32[4,256]{1,0:T(4,128)S(1)}, u32[]{:S(2)}) copy-start(f32[4,256]{1,0:T(4,128)S(1)} %fusion.95) | copy-start | bytes 12292
  328.3 203.9 %copy-start.77 = (f32[4,256]{1,0:T(4,128)}, f32[4,256]{1,0:T(4,128)S(1)}, u32[]{:S(2)}) copy-start(f32[4,256]{1,0:T(4,128)S(1)} %fusion.144) | copy-start | bytes 12292
  485.3 45.9 %copy-start.7 = (bf16[384,2304]{1,0:T(8,128)(2,1)}, bf16[384,2304]{1,0:T(8,128)(2,1)S(1)}, u32[]{:S(2)}) copy-start(bf16[384,2304]{1,0:T(8,128)(2,1)S(1)} %reshape.396) | copy-start | bytes 5308420
  532.2 27.2 %copy-start.70 = (f32[4,384]{1,0:T(4,128)}, f32[4,384]{1,0:T(4,128)S(1)}, u32[]{:S(2)}) copy-start(f32[4,384]{1,0:T(4,128)S(1)} %get-tuple-element.85) | copy-start | bytes 18436
  559.0 24.9 %copy-start.4 = (f32[4,256,384]{2,1,0:T(8,128)}, f32[4,256,384]{2,1,0:T(8,128)S(1)}, u32[]{:S(2)}) copy-start(f32[4,256,384]{2,1,0:T(8,128)S(1)} %get-tuple-element.53) | copy-start | bytes 4718596
  606.7 11.7 slice-start.2
  621.1 11.6 copy-start.50
  632.7 14.2 %copy-start.38 = (bf16[4,6,64,256]{3,2,1,0:T(8,128)(2,1)}, bf16[4,6,64,256]{3,2,1,0:T(8,128)(2,1)S(1)}, u32[]{:S(2)}) copy-start(bf16[4,6,64,256]{3,2,1,0:T(8,128)(2,1)S(1)} %fusion.109) | copy-start | bytes 2359300
  632.7 13.0 %copy-start.18 = (bf16[4,256,6,64]{1,3,2,0:T(8,128)(2,1)S(1)}, bf16[4,256,6,64]{1,3,2,0:T(8,128)(2,1)}, u32[]{:S(2)}) copy-start(bf16[4,256,6,64]{1,3,2,0:T(8,128)(2,1)} %get-tuple-element.108) | copy-start | bytes 2359300
  671.9 11.7 slice-start
  686.3 12.5 %copy-start.47 = (bf16[4,256,6,64]{1,0,3,2:T(4,128)(2,1)S(1)}, bf16[4,256,6,64]{1,0,3,2:T(4,128)(2,1)}, u32[]{:S(2)}) copy-start(bf16[4,256,6,64]{1,0,3,2:T(4,128)(2,1)} %reshape.388) | copy-start | bytes 2359300
  698.8 12.7 %copy-start.30 = (f32[4,6,64,256]{3,2,1,0:T(8,128)S(1)}, f32[4,6,64,256]{3,2,1,0:T(8,128)}, u32[]{:S(2)}) copy-start(f32[4,6,64,256]{3,2,1,0:T(8,128)} %get-tuple-element.109) | copy-start | bytes 4718596
  726.8 174.8 %all-gather.34.cloned.1.call-start = ((), (), s32[]{:S(2)}) async-start(), calls=%async_computation.6 | async-start | bytes 1216512 | tf_op jit(solution)/shard_map/all_gather | solution.py:287
  732.9 427.2 %all-reduce.19.cloned.1.call-start = ((), (), s32[]{:S(2)}) async-start(), calls=%async_computation.8 | async-start | bytes 28311552
  786.0 39.3 %copy-start.8 = (bf16[384,2304]{1,0:T(8,128)(2,1)S(1)}, bf16[384,2304]{1,0:T(8,128)(2,1)}, u32[]{:S(2)}) copy-start(bf16[384,2304]{1,0:T(8,128)(2,1)} %copy-done.7) | copy-start | bytes 5308420
  (108 other events, 310.6 us)
Sparse Core Ops, SparseCore 0:
  11.5 61.3 all-gather.23
  76.4 58.8 all-gather.29
  138.8 56.9 all-gather.31
  198.5 56.8 all-gather.25
  258.7 60.2 all-gather.27
  322.4 59.5 all-gather.21
  726.9 115.9 all-reduce.16
  846.3 55.1 all-gather.33
  908.0 252.0 all-reduce.18
where the time goes:
time: 1180 us
  waiting for transfers between devices  312 us (26%)
  blocking collectives  289 us (24%)
  other arithmetic  264 us (22%)
  local copies, waits for them, and re-layouts  147 us (12%)
  matrix products  147 us (12%)
  between operations  16.5 us (1%)
    unnamed x11, waiting for transfers between devices  255 us
    all_gather x2, blocking collectives, body(): lax.all_gather(qkv_weight[layer_index], 'fsdp', axis=0, tiled=True)  94.6 us
    all_gather x2, blocking collectives, body(): lax.all_gather(proj_weight[layer_index], 'fsdp', axis=0, tiled=True)  79.6 us
    all_gather x2, other arithmetic, body(): lax.all_gather(ada_weight[layer_index], 'fsdp', axis=0, tiled=True)  78.5 us
    all_gather x2, blocking collectives, body(): lax.all_gather(biases[layer_index], 'fsdp', axis=0, tiled=True)  76.4 us
    all_gather x1, waiting for transfers between devices, body(): lax.all_gather(mod_joined, 'fsdp', axis=0, tiled=True)  56.6 us
    all_gather x2, other arithmetic, body(): lax.all_gather(fc2_weight[layer_index], 'fsdp', axis=0, tiled=True)  51.5 us
    all_gather x2, other arithmetic, body(): lax.all_gather(fc1_weight[layer_index], 'fsdp', axis=0, tiled=True)  51.3 us
  transfers between devices with their start and end apart: 9, of which 3 were waited for; matrix products, arithmetic and copies ran while one was open for 26% of the time, Pallas kernels for 0%

commit v1 on v0

--- a/solution.py
+++ b/solution.py
@@ -1,8 +1,11 @@
+import functools
 import math
 
 import jax
 import jax.numpy as jnp
 from jax import lax
+from jax.experimental import pallas as pl
+from jax.experimental.pallas import tpu as pltpu
 from jax.sharding import PartitionSpec as P
 
 D = 384
@@ -308,9 +311,589 @@
     )
 
 
+BF16 = jnp.bfloat16
+F32 = jnp.float32
+SLOT = 4
+SEQ = 256
+HALF = 7 * D
+WIRE = HALF + 2 * D + 128
+BIAS = 10 * D + FF
+VMEM = pl.BlockSpec(memory_space=pltpu.VMEM)
+SMEM = pl.BlockSpec(memory_space=pltpu.SMEM)
+
+
+def params_of(grid_rank=0):
+    semantics = ("arbitrary",) * grid_rank if grid_rank else None
+    return pltpu.CompilerParams(vmem_limit_bytes=50 * 2**20, dimension_semantics=semantics)
+
+
+def dot_nn(left, right):
+    return lax.dot_general(
+        left, right, (((1,), (0,)), ((), ())), preferred_element_type=jnp.float32
+    )
+
+
+def pack_kernel(rows, ada, qkv, proj, fc1, fc2, bias, cond, out, wide):
+    wide[:, :, WIRE - 128 :] = jnp.zeros((2, 2 * rows, 128), F32)
+
+    def put(source, start, width, row, column):
+        values = source[:, start : start + width].astype(F32)
+        for layer in range(2):
+            wide[layer, row : row + 1, column : column + width] = values[layer : layer + 1]
+
+    for row in range(rows):
+        put(ada, row * 6 * D, 6 * D, row, 0)
+        put(qkv, row * 3 * D, D, row, 6 * D)
+        put(qkv, row * 3 * D + D, 2 * D, rows + row, 0)
+        put(proj, row * D, D, rows + row, 2 * D)
+        put(fc1, row * FF, FF, rows + row, 3 * D)
+    for row in range(4 * rows):
+        put(fc2, row * D, D, row % (2 * rows), HALF + D * (row // (2 * rows)))
+    put(bias, 0, 128, 0, WIRE - 128)
+    put(bias, 128, 128, 1, WIRE - 128)
+    wide_cond = cond[...].astype(F32)
+    act = (wide_cond / (1.0 + jnp.exp(-wide_cond))).astype(BF16).astype(F32)
+    for part in range(3):
+        wide[0, 8 + 4 * part : 12 + 4 * part, WIRE - 128 :] = act[:, part * 128 : part * 128 + 128]
+    out[...] = wide[...].astype(BF16)
+
+
+def pack(ada, qkv, proj, fc1, fc2, bias, cond, rows):
+    return pl.pallas_call(
+        functools.partial(pack_kernel, rows),
+        out_shape=jax.ShapeDtypeStruct((2, 2 * rows, WIRE), BF16),
+        in_specs=[VMEM] * 7,
+        out_specs=VMEM,
+        scratch_shapes=[pltpu.VMEM((2, 2 * rows, WIRE), F32)],
+        compiler_params=params_of(),
+        name="pack",
+    )(ada, qkv, proj, fc1, fc2, bias, cond)
+
+
+def unpack_kernel(rows, devices, wire, left, right, down, bias, cond):
+    for group in range(devices // 4):
+        for half, target in ((0, left), (1, right)):
+            target[4 * rows * group : 4 * rows * (group + 1), :] = jnp.concatenate(
+                [
+                    wire[4 * group + member, half * rows : (half + 1) * rows, :HALF]
+                    for member in range(4)
+                ],
+                axis=0,
+            )
+    for device in range(devices):
+        for part in range(2):
+            start = 4 * rows * device + 2 * rows * part
+            column = HALF + D * part
+            down[start : start + 2 * rows, :] = wire[device, :, column : column + D]
+        tail = wire[device, :, WIRE - 128 :].astype(F32)
+        for part in range(2):
+            chunk = 2 * device + part
+            if chunk < BIAS // 128:
+                bias[0:1, chunk * 128 : chunk * 128 + 128] = tail[part : part + 1]
+        for part in range(3):
+            cond[device % 2, 4 * (device // 2) : 4 * (device // 2) + 4, part * 128 : part * 128 + 128] = tail[
+                8 + 4 * part : 12 + 4 * part
+            ]
+
+
+def unpack_wire(wire):
+    devices, rows = wire.shape[0], wire.shape[1] // 2
+    return pl.pallas_call(
+        functools.partial(unpack_kernel, rows, devices),
+        out_shape=(
+            jax.ShapeDtypeStruct((D, HALF), BF16),
+            jax.ShapeDtypeStruct((D, HALF), BF16),
+            jax.ShapeDtypeStruct((FF, D), BF16),
+            jax.ShapeDtypeStruct((1, BIAS), F32),
+            jax.ShapeDtypeStruct((2, SLOT * devices // 2, D), F32),
+        ),
+        in_specs=[VMEM],
+        out_specs=(VMEM,) * 5,
+        compiler_params=params_of(),
+        name="unpack",
+    )(wire)
+
+
+def norm_stats(values):
+    centred = values - jnp.mean(values, axis=-1, keepdims=True)
+    rstd = lax.rsqrt(jnp.mean(centred * centred, axis=-1, keepdims=True) + EPSILON)
+    return centred * rstd, rstd
+
+
+def mod_part(mod, slot, part):
+    return mod[pl.ds(slot, 1), part * D : (part + 1) * D]
+
+
+def gelu_parts(pre):
+    inner = 0.7978845608028654 * (pre + 0.044715 * (pre * pre * pre))
+    return jnp.tanh(inner)
+
+
+def forward_kernel(counts, hidden, cond, left, right, down, bias, out, mod, qkv, attended, projected, middle, pre_act, branch, *, last):
+    slot = pl.program_id(0)
+
+    @pl.when(slot == 0)
+    def _():
+        wide_cond = cond[...].astype(F32)
+        act = (wide_cond / (1.0 + jnp.exp(-wide_cond))).astype(BF16)
+        mod[...] = dot_nn(act, left[:, : 6 * D]) + bias[:, : 6 * D]
+
+    values = hidden[0].astype(F32)
+    normed, _ = norm_stats(values)
+    normed = (normed * (1.0 + mod_part(mod, slot, 1)) + mod_part(mod, slot, 0)).astype(BF16)
+    queries = (dot_nn(normed, left[:, 6 * D :]) + bias[:, 6 * D : 7 * D]).astype(BF16)
+    keys = dot_nn(normed, right[:, :D]).astype(BF16)
+    heads_in = (dot_nn(normed, right[:, D : 2 * D]) + bias[:, 7 * D : 8 * D]).astype(BF16)
+    qkv[0, :, :D] = queries
+    qkv[0, :, D : 2 * D] = keys
+    qkv[0, :, 2 * D :] = heads_in
+    scaled = queries * jnp.asarray(1.0 / math.sqrt(HEAD), BF16)
+    joined = []
+    for head in range(HEADS):
+        span = slice(head * HEAD, (head + 1) * HEAD)
+        scores = right_product(scaled[:, span], keys[:, span])
+        raised = jnp.exp(scores - jnp.max(scores, axis=-1, keepdims=True))
+        probs = (raised * (1.0 / jnp.sum(raised, axis=-1, keepdims=True))).astype(BF16)
+        joined.append(dot_nn(probs, heads_in[:, span]).astype(BF16))
+    joined = jnp.concatenate(joined, axis=1)
+    attended[0] = joined
+    proj = dot_nn(joined, right[:, 2 * D : 3 * D]) + bias[:, 8 * D : 9 * D]
+    projected[0] = proj
+    mid = values + mod_part(mod, slot, 2) * proj
+    middle[0] = mid
+    normed, _ = norm_stats(mid)
+    normed = (normed * (1.0 + mod_part(mod, slot, 4)) + mod_part(mod, slot, 3)).astype(BF16)
+    pre = dot_nn(normed, right[:, 3 * D :]) + bias[:, 9 * D : 9 * D + FF]
+    pre_act[0] = pre
+    act = (0.5 * pre * (1.0 + gelu_parts(pre))).astype(BF16)
+    ffn = dot_nn(act, down[...]) + bias[:, 9 * D + FF :]
+    branch[0] = ffn
+    result = mid + mod_part(mod, slot, 5) * ffn
+    if last:
+        result = result * jnp.where(slot < counts[0], 1.0, 0.0)
+    out[0] = result
+
+
+def per_slot(width):
+    return pl.BlockSpec((1, SEQ, width), lambda slot: (slot, 0, 0))
+
+
+def whole(*shape):
+    return pl.BlockSpec(shape, lambda slot: (0,) * len(shape))
+
+
+def tokens(width, dtype):
+    return jax.ShapeDtypeStruct((SLOT, SEQ, width), dtype)
+
+
+def cost(flops, moved):
+    return pl.CostEstimate(flops=flops, bytes_accessed=moved, transcendentals=0)
+
+
+def forward_block(counts, hidden, cond, weights, last):
+    left, right, down, bias = weights
+    return pl.pallas_call(
+        functools.partial(forward_kernel, last=last),
+        grid=(SLOT,),
+        out_shape=(
+            tokens(D, F32),
+            jax.ShapeDtypeStruct((SLOT, 6 * D), F32),
+            tokens(3 * D, BF16),
+            tokens(D, BF16),
+            tokens(D, F32),
+            tokens(D, F32),
+            tokens(FF, F32),
+            tokens(D, F32),
+        ),
+        in_specs=[
+            SMEM,
+            per_slot(D),
+            whole(SLOT, D),
+            whole(D, HALF),
+            whole(D, HALF),
+            whole(FF, D),
+            whole(1, BIAS),
+        ],
+        out_specs=(
+            per_slot(D),
+            whole(SLOT, 6 * D),
+            per_slot(3 * D),
+            per_slot(D),
+            per_slot(D),
+            per_slot(D),
+            per_slot(FF),
+            per_slot(D),
+        ),
+        compiler_params=params_of(1),
+        cost_estimate=cost(5 * 10**9, 20 * 2**20),
+        name="forward_block",
+    )(counts, hidden, cond, left, right, down, bias)
+
+
+def norm_backward(d_normed, normed, rstd, scale):
+    inner = d_normed * (1.0 + scale)
+    along = jnp.mean(inner * normed, axis=-1, keepdims=True)
+    return rstd * (inner - jnp.mean(inner, axis=-1, keepdims=True) - normed * along)
+
+
+def row_sum(values):
+    return jnp.sum(values, axis=0, keepdims=True)
+
+
+def ffn_kernel(chips, counts, upstream, branch, pre_act, middle, mod, right, down, d_middle, d_mod, bias, wire, acc_up, acc_down, *, last):
+    slot = pl.program_id(0)
+
+    @pl.when(slot == 0)
+    def _():
+        acc_up[...] = jnp.zeros_like(acc_up)
+        acc_down[...] = jnp.zeros_like(acc_down)
+        bias[...] = jnp.zeros_like(bias)
+        d_mod[...] = jnp.zeros_like(d_mod)
+
+    up = upstream[0].astype(F32)
+    if last:
+        up = up * jnp.where(slot < counts[0], 1.0, 0.0)
+    d_branch = up * mod_part(mod, slot, 5)
+    d_mod[pl.ds(20 + slot, 1), :] = row_sum(up * branch[0])
+    bias[:, FF:] += row_sum(d_branch)
+    low = d_branch.astype(BF16)
+    pre = pre_act[0]
+    curve = gelu_parts(pre)
+    act = (0.5 * pre * (1.0 + curve)).astype(BF16)
+    acc_down[...] += left_product(act, low)
+    slope = 0.5 * (1.0 + curve) + (0.5 * 0.7978845608028654) * pre * (1.0 - curve * curve) * (
+        1.0 + (3 * 0.044715) * (pre * pre)
+    )
+    d_pre = right_product(low, down[...]) * slope
+    bias[:, :FF] += row_sum(d_pre)
+    low = d_pre.astype(BF16)
+    normed, rstd = norm_stats(middle[0])
+    scale = mod_part(mod, slot, 4)
+    shifted = (normed * (1.0 + scale) + mod_part(mod, slot, 3)).astype(BF16)
+    acc_up[...] += left_product(shifted, low)
+    d_normed = right_product(low, right[:, 3 * D :])
+    d_mod[pl.ds(12 + slot, 1), :] = row_sum(d_normed)
+    d_mod[pl.ds(16 + slot, 1), :] = row_sum(d_normed * normed)
+    d_middle[0] = up + norm_backward(d_normed, normed, rstd, scale)
+
+    @pl.when(slot == SLOT - 1)
+    def _():
+        rows = D // chips
+        for chip in range(chips):
+            for half in range(2):
+                wire[half, chip, :, : 2 * D] = acc_up[rows * chip : rows * (chip + 1), 2 * D * half : 2 * D * (half + 1)].astype(BF16)
+                for part in range(2):
+                    start = rows * (4 * chip + 2 * half + part)
+                    wire[half, chip, :, (2 + part) * D : (3 + part) * D] = acc_down[start : start + rows, :].astype(BF16)
+
+
+def ffn_backward(counts, upstream, record, weights, chips, last):
+    _, mod, _, _, _, middle, pre_act, branch = record
+    _, right, down, _ = weights
+    rows = D // chips
+    return pl.pallas_call(
+        functools.partial(ffn_kernel, chips, last=last),
+        grid=(SLOT,),
+        out_shape=(
+            tokens(D, F32),
+            jax.ShapeDtypeStruct((24, D), F32),
+            jax.ShapeDtypeStruct((1, FF + D), F32),
+            jax.ShapeDtypeStruct((2, chips, rows, 4 * D), BF16),
+        ),
+        in_specs=[
+            SMEM,
+            per_slot(D),
+            per_slot(D),
+            per_slot(FF),
+            per_slot(D),
+            whole(SLOT, 6 * D),
+            whole(D, HALF),
+            whole(FF, D),
+        ],
+        out_specs=(
+            per_slot(D),
+            whole(24, D),
+            whole(1, FF + D),
+            whole(2, chips, rows, 4 * D),
+        ),
+        scratch_shapes=[pltpu.VMEM((D, FF), F32), pltpu.VMEM((FF, D), F32)],
+        compiler_params=params_of(1),
+        cost_estimate=cost(8 * 10**9, 20 * 2**20),
+        name="ffn_backward",
+    )(counts, upstream, branch, pre_act, middle, mod, right, down)
+
+
+def attention_kernel(chips, d_middle, hidden, qkv, attended, projected, mod, left, right, d_mod_in, bias_in, cond, d_cond_in, d_hidden, d_cond, wire, acc, acc_proj, d_mod, bias, *, first):
+    slot = pl.program_id(0)
+
+    @pl.when(slot == 0)
+    def _():
+        acc[...] = jnp.zeros_like(acc)
+        acc_proj[...] = jnp.zeros_like(acc_proj)
+        bias[...] = jnp.zeros_like(bias)
+        d_mod[...] = d_mod_in[...]
+
+    d_mid = d_middle[0]
+    d_proj = d_mid * mod_part(mod, slot, 2)
+    d_mod[pl.ds(8 + slot, 1), :] = row_sum(d_mid * projected[0])
+    bias[:, 8 * D : 9 * D] += row_sum(d_proj)
+    low = d_proj.astype(BF16)
+    acc_proj[...] += left_product(attended[0], low)
+    d_heads = right_product(low, right[:, 2 * D : 3 * D]).astype(BF16)
+    factor = 1.0 / math.sqrt(HEAD)
+    scaled = qkv[0, :, :D] * jnp.asarray(factor, BF16)
+    keys = qkv[0, :, D : 2 * D]
+    heads_in = qkv[0, :, 2 * D :]
+    d_query, d_keys, d_values = [], [], []
+    for head in range(HEADS):
+        span = slice(head * HEAD, (head + 1) * HEAD)
+        scores = right_product(keys[:, span], scaled[:, span])
+        raised = jnp.exp(scores - jnp.max(scores, axis=0, keepdims=True))
+        probs = raised * (1.0 / jnp.sum(raised, axis=0, keepdims=True))
+        d_probs = right_product(heads_in[:, span], d_heads[:, span])
+        d_values.append(dot_nn(probs.astype(BF16), d_heads[:, span]))
+        weighted = probs * d_probs
+        d_scores = (weighted - probs * jnp.sum(weighted, axis=0, keepdims=True)).astype(BF16)
+        d_keys.append(dot_nn(d_scores, scaled[:, span]))
+        d_query.append(left_product(d_scores, keys[:, span]) * factor)
+    d_query = jnp.concatenate(d_query, axis=1)
+    d_values = jnp.concatenate(d_values, axis=1)
+    bias[:, 6 * D : 7 * D] += row_sum(d_query)
+    bias[:, 7 * D : 8 * D] += row_sum(d_values)
+    mixed = jnp.concatenate(
+        [d_query.astype(BF16), jnp.concatenate(d_keys, axis=1).astype(BF16), d_values.astype(BF16)], axis=1
+    )
+    normed, rstd = norm_stats(hidden[0].astype(F32))
+    scale = mod_part(mod, slot, 1)
+    shifted = (normed * (1.0 + scale) + mod_part(mod, slot, 0)).astype(BF16)
+    acc[...] += left_product(shifted, mixed)
+    d_normed = right_product(mixed[:, :D], left[:, 6 * D :]) + right_product(mixed[:, D:], right[:, : 2 * D])
+    d_mod[pl.ds(slot, 1), :] = row_sum(d_normed)
+    d_mod[pl.ds(4 + slot, 1), :] = row_sum(d_normed * normed)
+    d_hidden[0] = d_mid + norm_backward(d_normed, normed, rstd, scale)
+
+    @pl.when(slot == SLOT - 1)
+    def _():
+        rows = D // chips
+        bias[:, 9 * D :] = bias_in[...]
+        total = d_cond_in[...]
+        for part in range(6):
+            grads = d_mod[SLOT * part : SLOT * (part + 1), :]
+            bias[:, part * D : (part + 1) * D] = row_sum(grads)
+            total = total + right_product(grads.astype(BF16), left[:, part * D : (part + 1) * D])
+        if first:
+            wide_cond = cond[...].astype(F32)
+            gate = 1.0 / (1.0 + jnp.exp(-wide_cond))
+            total = total * (gate * (1.0 + wide_cond * (1.0 - gate)))
+        d_cond[...] = total
+        low_mod = d_mod[...].astype(BF16)
+        for chip in range(chips):
+            span = slice(rows * chip, rows * (chip + 1))
+            wire[0, chip, :, : 2 * D] = acc[span, : 2 * D].astype(BF16)
+            wire[1, chip, :, :D] = acc[span, 2 * D :].astype(BF16)
+            wire[1, chip, :, D : 2 * D] = acc_proj[span, :].astype(BF16)
+            for half in range(2):
+                pieces = []
+                for part in range(2):
+                    chunk = 4 * chip + 2 * half + part
+                    if chunk < BIAS // 128:
+                        pieces.append(bias[:, chunk * 128 : (chunk + 1) * 128])
+                    else:
+                        pieces.append(jnp.zeros((1, 128), F32))
+                pieces.append(jnp.zeros((rows - 2, 128), F32))
+                wire[half, chip, :, 2 * D : 2 * D + 128] = jnp.concatenate(pieces, axis=0).astype(BF16)
+                wire[half, chip, :, 2 * D + 128 :] = low_mod
+
+
+def attention_backward(d_middle, hidden, record, weights, d_mod, bias, cond, d_cond, chips, first):
+    _, mod, qkv, attended, projected, _, _, _ = record
+    left, right, _, _ = weights
+    rows = D // chips
+    return pl.pallas_call(
+        functools.partial(attention_kernel, chips, first=first),
+        grid=(SLOT,),
+        out_shape=(
+            tokens(D, F32),
+            jax.ShapeDtypeStruct((SLOT, D), F32),
+            jax.ShapeDtypeStruct((2, chips, rows, 3 * D + 128), BF16),
+        ),
+        in_specs=[
+            per_slot(D),
+            per_slot(D),
+            per_slot(3 * D),
+            per_slot(D),
+            per_slot(D),
+            whole(SLOT, 6 * D),
+            whole(D, HALF),
+            whole(D, HALF),
+            whole(24, D),
+            whole(1, FF + D),
+            whole(SLOT, D),
+            whole(SLOT, D),
+        ],
+        out_specs=(
+            per_slot(D),
+            whole(SLOT, D),
+            whole(2, chips, rows, 3 * D + 128),
+        ),
+        scratch_shapes=[
+            pltpu.VMEM((D, 3 * D), F32),
+            pltpu.VMEM((D, D), F32),
+            pltpu.VMEM((24, D), F32),
+            pltpu.VMEM((1, BIAS), F32),
+        ],
+        compiler_params=params_of(1),
+        cost_estimate=cost(6 * 10**9, 20 * 2**20),
+        name="attention_backward",
+    )(d_middle, hidden, qkv, attended, projected, mod, left, right, d_mod, bias, cond, d_cond)
+
+
+def finish_kernel(chips, core, own_ffn, own_attn, got_ffn, got_attn, own_mod, got_mod, cond, chip, ada_out, qkv_out, proj_out, fc1_out, fc2_out, bias_out):
+    rows = D // (2 * chips)
+    is_odd = core[0] == 1
+    mine = 2 * chip[0] + core[0]
+    take = lax.broadcasted_iota(jnp.int32, (16, D), 0)
+    column = lax.broadcasted_iota(jnp.int32, (16, D), 1)
+    pick = ((column == rows * mine + take) & (take < rows)).astype(F32).astype(BF16)
+    chosen = [right_product(pick, cond[side].astype(BF16)).astype(BF16) for side in range(2)]
+    slots = SLOT * chips
+    source = lax.broadcasted_iota(jnp.int32, (slots, 24 * chips), 0)
+    target = lax.broadcasted_iota(jnp.int32, (slots, 24 * chips), 1)
+    places = []
+    for part in range(6):
+        place = (target == 24 * (source // SLOT) + SLOT * part + source % SLOT).astype(F32).astype(BF16)
+        places.append([dot_nn(chosen[side], place).astype(BF16) for side in range(2)])
+    for layer in range(2):
+        even = jnp.where(is_odd, got_mod[layer], own_mod[layer])
+        odd = jnp.where(is_odd, own_mod[layer], got_mod[layer])
+        for part in range(6):
+            block = dot_nn(places[part][0], even) + dot_nn(places[part][1], odd)
+            for row in range(rows):
+                start = row * 6 * D + part * D
+                ada_out[layer : layer + 1, start : start + D] = block[row : row + 1]
+        own = jnp.where(is_odd, own_ffn[layer, rows:, :], own_ffn[layer, :rows, :])
+        got = got_ffn[layer]
+        first = jnp.where(is_odd, got, own[:, : 2 * D])
+        second = jnp.where(is_odd, own[:, : 2 * D], got)
+        for row in range(rows):
+            fc1_out[layer : layer + 1, row * FF : row * FF + 2 * D] = first[row : row + 1]
+            fc1_out[layer : layer + 1, row * FF + 2 * D : (row + 1) * FF] = second[row : row + 1]
+        for row in range(4 * rows):
+            column_start = (2 + row // (2 * rows)) * D
+            fc2_out[layer : layer + 1, row * D : (row + 1) * D] = own_ffn[
+                layer, row % (2 * rows) : row % (2 * rows) + 1, column_start : column_start + D
+            ]
+        own = jnp.where(is_odd, own_attn[layer, rows:, :], own_attn[layer, :rows, :])
+        got = got_attn[layer]
+        first = jnp.where(is_odd, got, own[:, : 2 * D])
+        second = jnp.where(is_odd, own[:, : 2 * D], got)
+        for row in range(rows):
+            qkv_out[layer : layer + 1, row * 3 * D : row * 3 * D + 2 * D] = first[row : row + 1]
+            qkv_out[layer : layer + 1, row * 3 * D + 2 * D : (row + 1) * 3 * D] = second[row : row + 1, :D]
+            proj_out[layer : layer + 1, row * D : (row + 1) * D] = second[row : row + 1, D:]
+        for part in range(2):
+            bias_out[layer : layer + 1, part * 128 : (part + 1) * 128] = own_attn[
+                layer, part : part + 1, 2 * D : 2 * D + 128
+            ]
+
+
+def finish(core, chip, own_ffn, own_attn, got_ffn, got_attn, own_mod, got_mod, cond, shapes, chips):
+    return pl.pallas_call(
+        functools.partial(finish_kernel, chips),
+        out_shape=tuple(jax.ShapeDtypeStruct(shape, F32) for shape in shapes),
+        in_specs=[SMEM] + [VMEM] * 7 + [SMEM],
+        out_specs=(VMEM,) * 6,
+        compiler_params=params_of(),
+        name="finish",
+    )(core, own_ffn, own_attn, got_ffn, got_attn, own_mod, got_mod, cond, chip)
+
+
+def fast_body(
+    latents_in, condition, counts, ada_weight, qkv_weight, proj_weight, fc1_weight, fc2_weight, biases, cotangent
+):
+    devices = lax.axis_size("fsdp")
+    chips = devices // 2
+    rows = D // devices
+    index = lax.axis_index("fsdp")
+    core, chip = (index % 2).reshape(1), (index // 2).reshape(1)
+    pairs = [[2 * one, 2 * one + 1] for one in range(chips)]
+    across = [[2 * one + side for one in range(chips)] for side in range(2)]
+    swap = [(one, one ^ 1) for one in range(devices)]
+
+    packed = pack(ada_weight, qkv_weight, proj_weight, fc1_weight, fc2_weight, biases, condition, rows)
+    gathered = lax.all_gather(packed, "fsdp", axis=0, tiled=False)
+    weights, conds = [], []
+    for layer in range(2):
+        *layer_weights, cond_all = unpack_wire(gathered[:, layer])
+        weights.append(layer_weights)
+        conds.append(cond_all)
+    hidden = [latents_in]
+    records = []
+    for layer in range(2):
+        record = forward_block(counts, hidden[-1], condition, weights[layer], layer == 1)
+        records.append(record)
+        hidden.append(record[0])
+    upstream = cotangent
+    d_cond = jnp.zeros((SLOT, D), F32)
+    reduced = [None, None]
+
+    def summed(wire, width):
+        pair = lax.all_to_all(wire, "fsdp", 0, 0, axis_index_groups=pairs, tiled=True)
+        both = (pair[0].astype(F32) + pair[1].astype(F32))[:, :, :width].astype(BF16)
+        if width < wire.shape[-1]:
+            both = jnp.concatenate([both, wire[0, :, :, width:]], axis=2)
+        spread = lax.all_to_all(both, "fsdp", 0, 0, axis_index_groups=across, tiled=True)
+        return jnp.sum(spread[:, :, :width].astype(F32), axis=0), spread[:, :, width:]
+
+    for layer in (1, 0):
+        d_middle, d_mod, bias, ffn_wire = ffn_backward(
+            counts, upstream, records[layer], weights[layer], chips, layer == 1
+        )
+        ffn_sum, _ = summed(ffn_wire, 4 * D)
+        upstream, d_cond, attn_wire = attention_backward(
+            d_middle, hidden[layer], records[layer], weights[layer], d_mod, bias, condition, d_cond, chips, layer == 0
+        )
+        attn_sum, mods = summed(attn_wire, 2 * D + 128)
+        reduced[layer] = (ffn_sum, attn_sum, mods.reshape(24 * chips, D))
+    own_ffn = jnp.stack([reduced[layer][0] for layer in range(2)])
+    own_attn = jnp.stack([reduced[layer][1] for layer in range(2)])
+    own_mod = jnp.stack([reduced[layer][2] for layer in range(2)])
+    start = (1 - index % 2) * rows
+    to_send = jnp.concatenate([own_ffn[:, :, : 2 * D], own_attn[:, :, : 2 * D]], axis=2)
+    got = lax.ppermute(lax.dynamic_slice_in_dim(to_send, start, rows, axis=1), "fsdp", swap)
+    got_mod = lax.ppermute(own_mod, "fsdp", swap)
+    shapes = [array.shape for array in (ada_weight, qkv_weight, proj_weight, fc1_weight, fc2_weight, biases)]
+    grads = finish(
+        core, chip, own_ffn, own_attn, got[:, :, : 2 * D], got[:, :, 2 * D :], own_mod, got_mod, conds[0], shapes, chips
+    )
+    return (hidden[2], upstream, d_cond, *grads)
+
+
+def choose_body(
+    latents_in, condition, counts, ada_weight, qkv_weight, proj_weight, fc1_weight, fc2_weight, biases, cotangent
+):
+    devices = lax.axis_size("fsdp")
+    rows = D // devices
+    fits = (
+        D % devices == 0
+        and devices == 32
+        and latents_in.shape == (SLOT, SEQ, D)
+        and ada_weight.shape == (2, rows * 6 * D)
+        and qkv_weight.shape == (2, rows * 3 * D)
+        and proj_weight.shape == (2, rows * D)
+        and fc1_weight.shape == (2, rows * FF)
+        and fc2_weight.shape == (2, rows * FF)
+        and biases.shape == (2, 256)
+    )
+    chosen = fast_body if fits else body
+    return chosen(
+        latents_in, condition, counts, ada_weight, qkv_weight, proj_weight, fc1_weight, fc2_weight, biases, cotangent
+    )
+
+
 def solution(mesh):
     return jax.shard_map(
-        body,
+        choose_body,
         mesh=mesh,
         in_specs=(
             P("fsdp", None, None),

time: 1180 us -> 399 us (0.34)
  blocking collectives: 289 us -> 14.9 us
  other arithmetic: 264 us -> 12.5 us
  matrix products: 147 us -> 0 us
  waiting for transfers between devices: 312 us -> 180 us
  local copies, waits for them, and re-layouts: 147 us -> 23.6 us
  Pallas kernels: 0 us -> 120 us
  starting transfers between devices: 0.53 us -> 30.6 us
    all_gather x7 -> x0, blocking collectives: 289 us -> none  [the longest x2 94.6 us: body(): lax.all_gather(qkv_weight[layer_index], 'fsdp', axis=0, tiled=True)]
    unnamed x11 -> x1, waiting for transfers between devices: 255 us -> 0.02 us
    all_gather x10 -> x0, other arithmetic: 230 us -> none  [the longest x2 78.5 us: body(): lax.all_gather(ada_weight[layer_index], 'fsdp', axis=0, tiled=True)]
    dot_general x41 -> x0, matrix products: 147 us -> none  [the longest x10 29.1 us: right_product(): lax.dot_general(left, right, (((1,), (1,)), ((), ())), preferred_element_...]
    pallas_call x0 -> x10, Pallas kernels: none -> 120 us  [the longest x2 40.7 us: attention_backward(): pl.pallas_call(functools.partial(attention_kernel, chips, first=first), g...]
    all_to_all x0 -> x6, waiting for transfers between devices: none -> 87.1 us  [the longest x4 83.7 us: summed(): lax.all_to_all(both, 'fsdp', 0, 0, axis_index_groups=across, tiled=True)]
    reshape x32 -> x0, local copies, waits for them, and re-layouts: 73.4 us -> none  [the longest x10 29.2 us: pad_flat(): flat = values_in.reshape(-1)]
    all_gather x7 -> x1, waiting for transfers between devices: 56.7 us -> 91.1 us  [fast_body(): gathered = lax.all_gather(packed, 'fsdp', axis=0, tiled=False)]
  transfers between devices with their start and end apart: 9 -> 9, of which waited for: 3 -> 8; matrix products, arithmetic and copies ran while one was open for 26% -> 4% of each run, Pallas kernels for 0% -> 0%
where the time goes in v1:
time: 399 us; the launch traced here: 397 us
  waiting for transfers between devices  180 us (45%)
  Pallas kernels  120 us (30%)
  starting transfers between devices  30.6 us (8%)
  local copies, waits for them, and re-layouts  23.6 us (6%)
  blocking collectives  14.9 us (4%)
  between operations  14.9 us (4%)
  other arithmetic  12.5 us (3%)
    all_gather x1, waiting for transfers between devices, fast_body(): gathered = lax.all_gather(packed, 'fsdp', axis=0, tiled=False)  91.1 us
    all_to_all x4, waiting for transfers between devices, summed(): lax.all_to_all(both, 'fsdp', 0, 0, axis_index_groups=across, tiled=True)  83.7 us
    pallas_call x2, Pallas kernels, attention_backward(): pl.pallas_call(functools.partial(attention_kernel, chips, first=first), g...  40.7 us
    pallas_call x2, Pallas kernels, forward_block(): pl.pallas_call(functools.partial(forward_kernel, last=last), grid=(SLOT,)...  37.4 us
    pallas_call x2, Pallas kernels, ffn_backward(): pl.pallas_call(functools.partial(ffn_kernel, chips, last=last), grid=(SLO...  30.7 us
    all_to_all x4, starting transfers between devices, summed(): lax.all_to_all(both, 'fsdp', 0, 0, axis_index_groups=across, tiled=True)  22.9 us
    all_to_all x2, blocking collectives, summed(): lax.all_to_all(wire, 'fsdp', 0, 0, axis_index_groups=pairs, tiled=True)  14.9 us
    unnamed x32, local copies, waits for them, and re-layouts  10.5 us
  transfers between devices with their start and end apart: 9, of which 8 were waited for; matrix products, arithmetic and copies ran while one was open for 4% of the time, Pallas kernels for 0%

profile of v1, /device:TPU:0, one launch (start us, length us, event | category | flops | bytes accessed | tf_op | source)
XLA Modules:
  0.0 396.7 jit_solution(5286871438747453063)
XLA Ops:
  14.4 91.1 %all-gather.3.cloned.1.call-done = bf16[64,24,3584]{2,1,0:T(8,128)(2,1)} async-done(((bf16[2,24,3584]{2,1,0:T(8,128)(2,1)}), bf16[64,24,3584]{2,1,0:T(8,128)(2,1)}) %all-gather.3.cloned.1.call-update) | async-done | bytes 11010064 | tf_op jit(solution)/shard_map/all_gather | solution.py:824
  105.5 9.0 %slice_bitcast_fusion = (bf16[32,24,3584]{2,1,0:T(8,128)(2,1)}, bf16[32,24,3584]{2,1,0:T(8,128)(2,1)}) fusion(bf16[32,2,24,3584]{3,2,1,0:T(8,128)(2,1)} %bitcast.29), kind=kLoop, calls=%fused_computation | loop fusion | bytes 22020096 | tf_op jit(solution)/shard_map/squeeze | solution.py:827
  114.6 4.1 %unpack.2 = (bf16[384,2688]{1,0:T(8,128)(2,1)S(1)}, bf16[384,2688]{1,0:T(8,128)(2,1)}, bf16[1536,384]{1,0:T(8,128)(2,1)S(1)}, f32[1,5376]{1,0:T(1,128)S(1)}, f32[2,64,384]{2,1,0:T(8,128)S(1)}) custom-call(bf16[32,24,3584]{2,1,0:T(8,128)(2,1)} %get-tuple-element.100.wire), custom_call_target="tpu_custom_call" | custom-call | tf_op jit(solution)/shard_map/unpack/pallas_call | solution.py:401
  120.0 4.3 %unpack.3 = (bf16[384,2688]{1,0:T(8,128)(2,1)S(1)}, bf16[384,2688]{1,0:T(8,128)(2,1)}, bf16[1536,384]{1,0:T(8,128)(2,1)S(1)}, f32[1,5376]{1,0:T(1,128)S(1)}, f32[2,64,384]{2,1,0:T(8,128)}) custom-call(bf16[32,24,3584]{2,1,0:T(8,128)(2,1)} %get-tuple-element.99.wire), custom_call_target="tpu_custom_call" | custom-call | tf_op jit(solution)/shard_map/unpack/pallas_call | solution.py:401
  125.7 18.7 %forward_block.2 = (f32[4,256,384]{2,1,0:T(8,128)}, f32[4,2304]{1,0:T(4,128)S(1)}, bf16[4,256,1152]{2,1,0:T(8,128)(2,1)}, bf16[4,256,384]{2,1,0:T(8,128)(2,1)S(1...) custom-call(s32[1]{0:T(128)S(6)} %copy.25.counts, ...), custom_call_target="tpu_custom_call" | custom-call | flops 5000000000 | bytes 20971520 | tf_op jit(solution)/shard_map/forward_block/pallas_call | solution.py:495
  144.4 18.7 %forward_block.3 = (f32[4,256,384]{2,1,0:T(8,128)}, f32[4,2304]{1,0:T(4,128)S(1)}, bf16[4,256,1152]{2,1,0:T(8,128)(2,1)}, bf16[4,256,384]{2,1,0:T(8,128)(2,1)S(1...) custom-call(s32[1]{0:T(128)S(6)} %copy.25.counts, ...), custom_call_target="tpu_custom_call" | custom-call | flops 5000000000 | bytes 20971520 | tf_op jit(solution)/shard_map/forward_block/pallas_call | solution.py:495
  164.2 15.4 %ffn_backward.2 = (f32[4,256,384]{2,1,0:T(8,128)S(1)}, f32[24,384]{1,0:T(8,128)S(1)}, f32[1,1920]{1,0:T(1,128)S(1)}, bf16[2,16,24,1536]{3,2,1,0:T(8,128)(2,1)}) custom-call(s32[1]{0:T(128)S(6)} %copy.25.counts, bf16[4,256,384]{2,1,0:T(8,128)(2,1)S(1)} %copy-done.10, f32[4,256,384]{2,1,0:T(8,128)} %get-tuple-element.64.branch, ...), custom_call_target="tpu_custom_call" | custom-call | flops 8000000000 | bytes 20971520 | tf_op jit(solution)/shard_map/ffn_backward/pallas_call | solution.py:594
  179.6 20.6 %attention_backward.2 = (f32[4,256,384]{2,1,0:T(8,128)S(1)}, f32[4,384]{1,0:T(4,128)S(1)}, bf16[2,16,24,1280]{3,2,1,0:T(8,128)(2,1)}) custom-call(f32[4,256,384]{2,1,0:T(8,128)S(1)} %get-tuple-element.68.d_middle, f32[4,256,384]{2,1,0:T(8,128)} %get-tuple-element.58.hidden, bf16[4,256,1152]{2,1,0:T(8,128)(2,1)} %get-tuple-element.69.qkv, ...), custom_call_target="tpu_custom_call" | custom-call | flops 6000000000 | bytes 20971520 | tf_op jit(solution)/shard_map/attention_backward/pallas_call | solution.py:712
  201.4 15.3 %ffn_backward.3 = (f32[4,256,384]{2,1,0:T(8,128)S(1)}, f32[24,384]{1,0:T(8,128)S(1)}, f32[1,1920]{1,0:T(1,128)S(1)}, bf16[2,16,24,1536]{3,2,1,0:T(8,128)(2,1)}) custom-call(s32[1]{0:T(128)S(6)} %copy.25.counts, f32[4,256,384]{2,1,0:T(8,128)} %copy-done.13, f32[4,256,384]{2,1,0:T(8,128)} %get-tuple-element.75.branch, ...), custom_call_target="tpu_custom_call" | custom-call | flops 8000000000 | bytes 20971520 | tf_op jit(solution)/shard_map/ffn_backward/pallas_call | solution.py:594
  216.7 20.1 %attention_backward.3 = (f32[4,256,384]{2,1,0:T(8,128)}, f32[4,384]{1,0:T(4,128)}, bf16[2,16,24,1280]{3,2,1,0:T(8,128)(2,1)}) custom-call(f32[4,256,384]{2,1,0:T(8,128)S(1)} %get-tuple-element.79.d_middle, bf16[4,256,384]{2,1,0:T(8,128)(2,1)S(1)} %copy-done.11, bf16[4,256,1152]{2,1,0:T(8,128)(2,1)} %get-tuple-element.80.qkv, ...), custom_call_target="tpu_custom_call" | custom-call | flops 6000000000 | bytes 20971520 | tf_op jit(solution)/shard_map/attention_backward/pallas_call | solution.py:712
  236.8 3.7 all-to-all-start.4
  243.6 3.8 all-to-all-start.6
  250.1 9.3 %all_to_all.40 = bf16[2,16,24,1536]{3,2,1,0:T(8,128)(2,1)} all-to-all(bf16[2,16,24,1536]{3,2,1,0:T(8,128)(2,1)} %get-tuple-element.88), channel_id=1, replica_groups={{0,1},{2,3},{4,5},{6,7},{8,9},{10,11},{12,13},{14,15},{16,17},{18,19},{..., dimensions={0} | all-to-all | bytes 4718592 | tf_op jit(solution)/shard_map/all_to_all | solution.py:841
  259.5 5.6 %all_to_all.41 = bf16[2,16,24,1536]{3,2,1,0:T(8,128)(2,1)S(1)} all-to-all(bf16[2,16,24,1536]{3,2,1,0:T(8,128)(2,1)S(1)} %copy-done.15), channel_id=1, replica_groups={{0,1},{2,3},{4,5},{6,7},{8,9},{10,11},{12,13},{14,15},{16,17},{18,19},{..., dimensions={0} | all-to-all | bytes 4718592 | tf_op jit(solution)/shard_map/all_to_all | solution.py:841
  265.1 4.3 %all-to-all-start.5 = ((bf16[16,24,1280]{2,1,0:T(8,128)(2,1)}), bf16[16,24,1280]{2,1,0:T(8,128)(2,1)}, u32[]{:S(2)}, u32[]{:S(2)}) async-start(bf16[16,24,1280]{2,1,0:T(8,128)(2,1)} %pad_maximum_fusion), calls=%async_computation.5 | async-start | bytes 1966080 | tf_op jit(solution)/shard_map/all_to_all | solution.py:845
  273.2 19.7 %all-to-all-done.5 = bf16[16,24,1280]{2,1,0:T(8,128)(2,1)} async-done(((bf16[16,24,1280]{2,1,0:T(8,128)(2,1)}), bf16[16,24,1280]{2,1,0:T(8,128)(2,1)}, u32[]{:S(2)}, u32[]{:S(2)}) %all-to-all-start.5) | async-done | bytes 983072 | tf_op jit(solution)/shard_map/all_to_all | solution.py:845
  292.9 6.8 %all-to-all-start.7 = ((bf16[16,24,1280]{2,1,0:T(8,128)(2,1)}), bf16[16,24,1280]{2,1,0:T(8,128)(2,1)}, u32[]{:S(2)}, u32[]{:S(2)}) async-start(bf16[16,24,1280]{2,1,0:T(8,128)(2,1)} %pad_maximum_fusion.1), calls=%async_computation.7 | async-start | bytes 1966080 | tf_op jit(solution)/shard_map/all_to_all | solution.py:845
  299.7 2.9 fusion
  302.6 19.9 %all-to-all-done.7 = bf16[16,24,1280]{2,1,0:T(8,128)(2,1)} async-done(((bf16[16,24,1280]{2,1,0:T(8,128)(2,1)}), bf16[16,24,1280]{2,1,0:T(8,128)(2,1)}, u32[]{:S(2)}, u32[]{:S(2)}) %all-to-all-start.7) | async-done | bytes 983072 | tf_op jit(solution)/shard_map/all_to_all | solution.py:845
  322.6 5.7 %all-to-all-start.1 = ((bf16[16,24,1536]{2,1,0:T(8,128)(2,1)}), bf16[16,24,1536]{2,1,0:T(8,128)(2,1)}, u32[]{:S(2)}, u32[]{:S(2)}) async-start(bf16[16,24,1536]{2,1,0:T(8,128)(2,1)} %fusion), calls=%async_computation.1 | async-start | bytes 2359296 | tf_op jit(solution)/shard_map/all_to_all | solution.py:845
  329.6 24.4 %all-to-all-done.1 = bf16[16,24,1536]{2,1,0:T(8,128)(2,1)} async-done(((bf16[16,24,1536]{2,1,0:T(8,128)(2,1)}), bf16[16,24,1536]{2,1,0:T(8,128)(2,1)}, u32[]{:S(2)}, u32[]{:S(2)}) %all-to-all-start.1) | async-done | bytes 1179680 | tf_op jit(solution)/shard_map/all_to_all | solution.py:845
  354.0 6.1 %all-to-all-start.3 = ((bf16[16,24,1536]{2,1,0:T(8,128)(2,1)}), bf16[16,24,1536]{2,1,0:T(8,128)(2,1)S(1)}, u32[]{:S(2)}, u32[]{:S(2)}) async-start(bf16[16,24,1536]{2,1,0:T(8,128)(2,1)} %fusion.1), calls=%async_computation.3 | async-start | bytes 2359296 | tf_op jit(solution)/shard_map/all_to_all | solution.py:845
  366.2 19.6 %all-to-all-done.3 = bf16[16,24,1536]{2,1,0:T(8,128)(2,1)S(1)} async-done(((bf16[16,24,1536]{2,1,0:T(8,128)(2,1)}), bf16[16,24,1536]{2,1,0:T(8,128)(2,1)S(1)}, u32[]{:S(2)}, u32[]{:S(2)}) %all-to-all-start.3) | async-done | bytes 1179680 | tf_op jit(solution)/shard_map/all_to_all | solution.py:845
  387.6 2.3 finish.1
  (63 shorter events, 30.2 us)
Async XLA Ops:
  7.2 98.4 %all-gather.3.cloned.1.call-start = ((), (), s32[]{:S(2)}) async-start(), calls=%async_computation.8 | async-start | bytes 11354112 | tf_op jit(solution)/shard_map/all_gather | solution.py:824
  7.2 0.9 copy-start
  8.1 0.9 copy-start.1
  9.0 0.9 copy-start.2
  9.9 0.8 copy-start.3
  10.7 0.7 copy-start.4
  11.4 0.7 copy-start.5
  118.7 1.4 copy-start.8
  120.0 5.6 %copy-start.6 = (bf16[4,384]{1,0:T(4,128)(2,1)S(1)}, bf16[4,384]{1,0:T(4,128)(2,1)}, u32[]{:S(2)}) copy-start(bf16[4,384]{1,0:T(4,128)(2,1)} %cond.9) | copy-start | bytes 9220
  120.0 5.6 %copy-start.11 = (bf16[4,256,384]{2,1,0:T(8,128)(2,1)S(1)}, bf16[4,256,384]{2,1,0:T(8,128)(2,1)}, u32[]{:S(2)}) copy-start(bf16[4,256,384]{2,1,0:T(8,128)(2,1)} %hidden.3) | copy-start | bytes 2359300
  124.4 1.3 copy-start.9
  144.4 19.9 %copy-start.10 = (bf16[4,256,384]{2,1,0:T(8,128)(2,1)S(1)}, bf16[4,256,384]{2,1,0:T(8,128)(2,1)}, u32[]{:S(2)}) copy-start(bf16[4,256,384]{2,1,0:T(8,128)(2,1)} %upstream.1) | copy-start | bytes 2359300
  163.1 1.2 copy-start.12
  200.2 1.1 copy-start.13
  236.8 6.5 %all-to-all-start.4 = ((bf16[2,16,24,1280]{3,2,1,0:T(8,128)(2,1)}), bf16[2,16,24,1280]{3,2,1,0:T(8,128)(2,1)S(1)}, u32[]{:S(2)}, u32[]{:S(2)}) async-start(bf16[2,16,24,1280]{3,2,1,0:T(8,128)(2,1)} %get-tuple-element.90), calls=%async_computation.4 | async-start | bytes 3932160 | tf_op jit(solution)/shard_map/all_to_all | solution.py:841
  243.6 6.5 %all-to-all-start.6 = ((bf16[2,16,24,1280]{3,2,1,0:T(8,128)(2,1)}), bf16[2,16,24,1280]{3,2,1,0:T(8,128)(2,1)S(1)}, u32[]{:S(2)}, u32[]{:S(2)}) async-start(bf16[2,16,24,1280]{3,2,1,0:T(8,128)(2,1)} %get-tuple-element.91), calls=%async_computation.6 | async-start | bytes 3932160 | tf_op jit(solution)/shard_map/all_to_all | solution.py:841
  250.1 9.3 %copy-start.14 = (bf16[2,16,24,1280]{3,2,1,0:T(8,128)(2,1)}, bf16[2,16,24,1280]{3,2,1,0:T(8,128)(2,1)S(1)}, u32[]{:S(2)}) copy-start(bf16[2,16,24,1280]{3,2,1,0:T(8,128)(2,1)S(1)} %all-to-all-done.6) | copy-start | bytes 5898244
  250.1 9.3 %copy-start.15 = (bf16[2,16,24,1536]{3,2,1,0:T(8,128)(2,1)S(1)}, bf16[2,16,24,1536]{3,2,1,0:T(8,128)(2,1)}, u32[]{:S(2)}) copy-start(bf16[2,16,24,1536]{3,2,1,0:T(8,128)(2,1)} %get-tuple-element.89) | copy-start | bytes 7077892
  265.1 27.8 %all-to-all-start.5 = ((bf16[16,24,1280]{2,1,0:T(8,128)(2,1)}), bf16[16,24,1280]{2,1,0:T(8,128)(2,1)}, u32[]{:S(2)}, u32[]{:S(2)}) async-start(bf16[16,24,1280]{2,1,0:T(8,128)(2,1)} %pad_maximum_fusion), calls=%async_computation.5 | async-start | bytes 1966080 | tf_op jit(solution)/shard_map/all_to_all | solution.py:845
  292.9 29.6 %all-to-all-start.7 = ((bf16[16,24,1280]{2,1,0:T(8,128)(2,1)}), bf16[16,24,1280]{2,1,0:T(8,128)(2,1)}, u32[]{:S(2)}, u32[]{:S(2)}) async-start(bf16[16,24,1280]{2,1,0:T(8,128)(2,1)} %pad_maximum_fusion.1), calls=%async_computation.7 | async-start | bytes 1966080 | tf_op jit(solution)/shard_map/all_to_all | solution.py:845
  322.6 31.4 %all-to-all-start.1 = ((bf16[16,24,1536]{2,1,0:T(8,128)(2,1)}), bf16[16,24,1536]{2,1,0:T(8,128)(2,1)}, u32[]{:S(2)}, u32[]{:S(2)}) async-start(bf16[16,24,1536]{2,1,0:T(8,128)(2,1)} %fusion), calls=%async_computation.1 | async-start | bytes 2359296 | tf_op jit(solution)/shard_map/all_to_all | solution.py:845
  354.0 31.8 %all-to-all-start.3 = ((bf16[16,24,1536]{2,1,0:T(8,128)(2,1)}), bf16[16,24,1536]{2,1,0:T(8,128)(2,1)S(1)}, u32[]{:S(2)}, u32[]{:S(2)}) async-start(bf16[16,24,1536]{2,1,0:T(8,128)(2,1)} %fusion.1), calls=%async_computation.3 | async-start | bytes 2359296 | tf_op jit(solution)/shard_map/all_to_all | solution.py:845
  362.2 25.4 %collective-permute-start.1 = (bf16[2,384,384]{2,1,0:T(8,128)(2,1)S(1)}, bf16[2,384,384]{2,1,0:T(8,128)(2,1)S(1)}, u32[]{:S(2)}, u32[]{:S(2)}) collective-permute-start(bf16[2,384,384]{2,1,0:T(8,128)(2,1)S(1)} %pad_maximum_fusion.2.own_mod), channel_id=1, source_target_pairs={{0,1},{1,0},{2,3},{3,2},{4,5},{5,4},{6,7},{7,6},{8,9},{9,8},{10,11... | collective-permute-start | bytes 1769480 | tf_op jit(solution)/shard_map/ppermute | solution.py:864
  386.1 1.5 collective-permute-start
  (1 other events, 0.7 us)
Sparse Core Ops, SparseCore 0:
  13.9 91.6 all-gather.2

commit v2 on v1

--- a/solution.py
+++ b/solution.py
@@ -333,8 +333,22 @@
     )
 
 
-def pack_kernel(rows, ada, qkv, proj, fc1, fc2, bias, cond, out, wide):
+def pack_kernel(rows, ada_in, qkv_in, proj_in, fc1_in, fc2_in, bias_in, cond, out_first, out_last, ada, qkv, proj, fc1, fc2, bias, sems, wide):
+    copies = [
+        pltpu.make_async_copy(source, target, sems.at[place])
+        for place, (source, target) in enumerate(
+            ((ada_in, ada), (qkv_in, qkv), (proj_in, proj), (fc1_in, fc1), (fc2_in, fc2), (bias_in, bias))
+        )
+    ]
+    for copy in copies:
+        copy.start()
     wide[:, :, WIRE - 128 :] = jnp.zeros((2, 2 * rows, 128), F32)
+    wide_cond = cond[...].astype(F32)
+    act = (wide_cond / (1.0 + jnp.exp(-wide_cond))).astype(BF16).astype(F32)
+    for part in range(3):
+        wide[0, 8 + 4 * part : 12 + 4 * part, WIRE - 128 :] = act[:, part * 128 : part * 128 + 128]
+    for copy in copies:
+        copy.wait()
 
     def put(source, start, width, row, column):
         values = source[:, start : start + width].astype(F32)
@@ -351,41 +365,54 @@
         put(fc2, row * D, D, row % (2 * rows), HALF + D * (row // (2 * rows)))
     put(bias, 0, 128, 0, WIRE - 128)
     put(bias, 128, 128, 1, WIRE - 128)
-    wide_cond = cond[...].astype(F32)
-    act = (wide_cond / (1.0 + jnp.exp(-wide_cond))).astype(BF16).astype(F32)
-    for part in range(3):
-        wide[0, 8 + 4 * part : 12 + 4 * part, WIRE - 128 :] = act[:, part * 128 : part * 128 + 128]
-    out[...] = wide[...].astype(BF16)
-
-
-def pack(ada, qkv, proj, fc1, fc2, bias, cond, rows):
+    for layer, out in enumerate((out_first, out_last)):
+        low = wide[layer].astype(BF16)
+        for copy_index in range(out.shape[0]):
+            out[copy_index] = low
+
+
+def pack(ada, qkv, proj, fc1, fc2, bias, cond, rows, copies):
+    flat = (ada, qkv, proj, fc1, fc2, bias)
     return pl.pallas_call(
         functools.partial(pack_kernel, rows),
-        out_shape=jax.ShapeDtypeStruct((2, 2 * rows, WIRE), BF16),
-        in_specs=[VMEM] * 7,
-        out_specs=VMEM,
-        scratch_shapes=[pltpu.VMEM((2, 2 * rows, WIRE), F32)],
+        out_shape=(jax.ShapeDtypeStruct((copies, 2 * rows, WIRE), BF16),) * 2,
+        in_specs=[pl.BlockSpec(memory_space=pl.ANY)] * 6 + [VMEM],
+        out_specs=(VMEM, VMEM),
+        scratch_shapes=[pltpu.VMEM(array.shape, BF16) for array in flat]
+        + [pltpu.SemaphoreType.DMA((6,)), pltpu.VMEM((2, 2 * rows, WIRE), F32)],
         compiler_params=params_of(),
         name="pack",
-    )(ada, qkv, proj, fc1, fc2, bias, cond)
-
-
-def unpack_kernel(rows, devices, wire, left, right, down, bias, cond):
-    for group in range(devices // 4):
+    )(*flat, cond)
+
+
+def unpack_kernel(rows, place, *refs):
+    blocks, (left, right, down, bias, cond, wire, sems) = refs[:16], refs[16:]
+    copies = []
+    for side in range(2):
+        for step in range(4):
+            for half in range(2):
+                number = 8 * side + 2 * step + half
+                target = wire.at[(place[0] + side) % 2, place[1] ^ step, pl.ds(2 * half, 2)]
+                copies.append(pltpu.make_async_copy(blocks[number], target, sems.at[number]))
+    for copy in copies:
+        copy.start()
+    for copy in copies:
+        copy.wait()
+
+    def of(device):
+        return wire.at[device % 2, (device // 2) % 4, device // 8]
+
+    for group in range(8):
         for half, target in ((0, left), (1, right)):
             target[4 * rows * group : 4 * rows * (group + 1), :] = jnp.concatenate(
-                [
-                    wire[4 * group + member, half * rows : (half + 1) * rows, :HALF]
-                    for member in range(4)
-                ],
-                axis=0,
+                [of(4 * group + member)[half * rows : (half + 1) * rows, :HALF] for member in range(4)], axis=0
             )
-    for device in range(devices):
+    for device in range(32):
         for part in range(2):
             start = 4 * rows * device + 2 * rows * part
             column = HALF + D * part
-            down[start : start + 2 * rows, :] = wire[device, :, column : column + D]
-        tail = wire[device, :, WIRE - 128 :].astype(F32)
+            down[start : start + 2 * rows, :] = of(device)[:, column : column + D]
+        tail = of(device)[:, WIRE - 128 :].astype(F32)
         for part in range(2):
             chunk = 2 * device + part
             if chunk < BIAS // 128:
@@ -396,22 +423,23 @@
             ]
 
 
-def unpack_wire(wire):
-    devices, rows = wire.shape[0], wire.shape[1] // 2
+def unpack_wire(place, blocks):
+    rows = blocks[0].shape[1] // 2
     return pl.pallas_call(
-        functools.partial(unpack_kernel, rows, devices),
+        functools.partial(unpack_kernel, rows),
         out_shape=(
             jax.ShapeDtypeStruct((D, HALF), BF16),
             jax.ShapeDtypeStruct((D, HALF), BF16),
             jax.ShapeDtypeStruct((FF, D), BF16),
             jax.ShapeDtypeStruct((1, BIAS), F32),
-            jax.ShapeDtypeStruct((2, SLOT * devices // 2, D), F32),
+            jax.ShapeDtypeStruct((2, SLOT * 16, D), F32),
         ),
-        in_specs=[VMEM],
+        in_specs=[SMEM] + [pl.BlockSpec(memory_space=pl.ANY)] * 16,
         out_specs=(VMEM,) * 5,
+        scratch_shapes=[pltpu.VMEM((2, 4, 4, 2 * rows, WIRE), BF16), pltpu.SemaphoreType.DMA((16,))],
         compiler_params=params_of(),
         name="unpack",
-    )(wire)
+    )(place, *blocks)
 
 
 def norm_stats(values):
@@ -540,7 +568,7 @@
     return jnp.sum(values, axis=0, keepdims=True)
 
 
-def ffn_kernel(chips, counts, upstream, branch, pre_act, middle, mod, right, down, d_middle, d_mod, bias, wire, acc_up, acc_down, *, last):
+def ffn_kernel(chips, core, counts, upstream, branch, pre_act, middle, mod, right, down, d_middle, d_mod, bias, wire, acc_up, acc_down, *, last):
     slot = pl.program_id(0)
 
     @pl.when(slot == 0)
@@ -581,13 +609,14 @@
         rows = D // chips
         for chip in range(chips):
             for half in range(2):
-                wire[half, chip, :, : 2 * D] = acc_up[rows * chip : rows * (chip + 1), 2 * D * half : 2 * D * (half + 1)].astype(BF16)
+                side = (half + core[0]) % 2
+                wire[side, chip, :, : 2 * D] = acc_up[rows * chip : rows * (chip + 1), 2 * D * half : 2 * D * (half + 1)].astype(BF16)
                 for part in range(2):
                     start = rows * (4 * chip + 2 * half + part)
-                    wire[half, chip, :, (2 + part) * D : (3 + part) * D] = acc_down[start : start + rows, :].astype(BF16)
-
-
-def ffn_backward(counts, upstream, record, weights, chips, last):
+                    wire[side, chip, :, (2 + part) * D : (3 + part) * D] = acc_down[start : start + rows, :].astype(BF16)
+
+
+def ffn_backward(core, counts, upstream, record, weights, chips, last):
     _, mod, _, _, _, middle, pre_act, branch = record
     _, right, down, _ = weights
     rows = D // chips
@@ -602,6 +631,7 @@
         ),
         in_specs=[
             SMEM,
+            SMEM,
             per_slot(D),
             per_slot(D),
             per_slot(FF),
@@ -620,10 +650,10 @@
         compiler_params=params_of(1),
         cost_estimate=cost(8 * 10**9, 20 * 2**20),
         name="ffn_backward",
-    )(counts, upstream, branch, pre_act, middle, mod, right, down)
-
-
-def attention_kernel(chips, d_middle, hidden, qkv, attended, projected, mod, left, right, d_mod_in, bias_in, cond, d_cond_in, d_hidden, d_cond, wire, acc, acc_proj, d_mod, bias, *, first):
+    )(core, counts, upstream, branch, pre_act, middle, mod, right, down)
+
+
+def attention_kernel(chips, core, d_middle, hidden, qkv, attended, projected, mod, left, right, d_mod_in, bias_in, cond, d_cond_in, d_hidden, d_cond, wire, acc, acc_proj, d_mod, bias, *, first):
     slot = pl.program_id(0)
 
     @pl.when(slot == 0)
@@ -689,9 +719,9 @@
         low_mod = d_mod[...].astype(BF16)
         for chip in range(chips):
             span = slice(rows * chip, rows * (chip + 1))
-            wire[0, chip, :, : 2 * D] = acc[span, : 2 * D].astype(BF16)
-            wire[1, chip, :, :D] = acc[span, 2 * D :].astype(BF16)
-            wire[1, chip, :, D : 2 * D] = acc_proj[span, :].astype(BF16)
+            wire[core[0], chip, :, : 2 * D] = acc[span, : 2 * D].astype(BF16)
+            wire[1 - core[0], chip, :, :D] = acc[span, 2 * D :].astype(BF16)
+            wire[1 - core[0], chip, :, D : 2 * D] = acc_proj[span, :].astype(BF16)
             for half in range(2):
                 pieces = []
                 for part in range(2):
@@ -701,11 +731,12 @@
                     else:
                         pieces.append(jnp.zeros((1, 128), F32))
                 pieces.append(jnp.zeros((rows - 2, 128), F32))
-                wire[half, chip, :, 2 * D : 2 * D + 128] = jnp.concatenate(pieces, axis=0).astype(BF16)
-                wire[half, chip, :, 2 * D + 128 :] = low_mod
-
-
-def attention_backward(d_middle, hidden, record, weights, d_mod, bias, cond, d_cond, chips, first):
+                side = (half + core[0]) % 2
+                wire[side, chip, :, 2 * D : 2 * D + 128] = jnp.concatenate(pieces, axis=0).astype(BF16)
+                wire[side, chip, :, 2 * D + 128 :] = low_mod
+
+
+def attention_backward(core, d_middle, hidden, record, weights, d_mod, bias, cond, d_cond, chips, first):
     _, mod, qkv, attended, projected, _, _, _ = record
     left, right, _, _ = weights
     rows = D // chips
@@ -718,6 +749,7 @@
             jax.ShapeDtypeStruct((2, chips, rows, 3 * D + 128), BF16),
         ),
         in_specs=[
+            SMEM,
             per_slot(D),
             per_slot(D),
             per_slot(3 * D),
@@ -745,7 +777,7 @@
         compiler_params=params_of(1),
         cost_estimate=cost(6 * 10**9, 20 * 2**20),
         name="attention_backward",
-    )(d_middle, hidden, qkv, attended, projected, mod, left, right, d_mod, bias, cond, d_cond)
+    )(core, d_middle, hidden, qkv, attended, projected, mod, left, right, d_mod, bias, cond, d_cond)
 
 
 def finish_kernel(chips, core, own_ffn, own_attn, got_ffn, got_attn, own_mod, got_mod, cond, chip, ada_out, qkv_out, proj_out, fc1_out, fc2_out, bias_out):
@@ -820,41 +852,75 @@
     across = [[2 * one + side for one in range(chips)] for side in range(2)]
     swap = [(one, one ^ 1) for one in range(devices)]
 
-    packed = pack(ada_weight, qkv_weight, proj_weight, fc1_weight, fc2_weight, biases, condition, rows)
-    gathered = lax.all_gather(packed, "fsdp", axis=0, tiled=False)
-    weights, conds = [], []
-    for layer in range(2):
-        *layer_weights, cond_all = unpack_wire(gathered[:, layer])
-        weights.append(layer_weights)
-        conds.append(cond_all)
-    hidden = [latents_in]
-    records = []
-    for layer in range(2):
-        record = forward_block(counts, hidden[-1], condition, weights[layer], layer == 1)
-        records.append(record)
-        hidden.append(record[0])
+    lines = [[8 * level + one for level in range(4)] for one in range(8)]
+    place = jnp.stack([index % 2, (index // 2) % 4])
+    tie = lax.optimization_barrier
+
+    def along(value, bit):
+        return lax.ppermute(value, "fsdp", [(one, one ^ bit) for one in range(devices)])
+
+    def stacked(copies):
+        return lax.all_to_all(copies, "fsdp", 0, 0, axis_index_groups=lines, tiled=True)
+
+    def spread_out(stack):
+        low, high = stack[:2], stack[2:]
+        low_x, high_y = along(low, 2), along(high, 4)
+        low_y, high_x = along(low, 4), along(high, 2)
+        return low, high, low_x, high_x, low_y, high_y
+
+    def spread_more(held):
+        low_x, high_y = held[2], held[5]
+        held = (*held, along(low_x, 4), along(high_y, 2))
+        return (*held, *[along(value, 1) for value in held])
+
+    copies_first, copies_last = pack(
+        ada_weight, qkv_weight, proj_weight, fc1_weight, fc2_weight, biases, condition, rows, 4
+    )
+    stack_first = stacked(copies_first)
+    stack_first, copies_last = tie((stack_first, copies_last))
+    stack_last = stacked(copies_last)
+    *first_weights, cond_all = unpack_wire(place, spread_more(spread_out(stack_first)))
+    held_last = spread_out(stack_last)
+    first = forward_block(counts, latents_in, condition, first_weights, False)
+    held_last, first = tie((held_last, first))
+    *last_weights, _ = unpack_wire(place, spread_more(held_last))
+    last = forward_block(counts, first[0], condition, last_weights, True)
+    weights, records, hidden = [first_weights, last_weights], [first, last], [latents_in, first[0], last[0]]
     upstream = cotangent
     d_cond = jnp.zeros((SLOT, D), F32)
     reduced = [None, None]
 
-    def summed(wire, width):
-        pair = lax.all_to_all(wire, "fsdp", 0, 0, axis_index_groups=pairs, tiled=True)
-        both = (pair[0].astype(F32) + pair[1].astype(F32))[:, :, :width].astype(BF16)
+    def paired(wire, width):
+        got = lax.ppermute(wire[1], "fsdp", swap)
+        both = (wire[0].astype(F32) + got.astype(F32))[:, :, :width].astype(BF16)
         if width < wire.shape[-1]:
             both = jnp.concatenate([both, wire[0, :, :, width:]], axis=2)
+        return both
+
+    def summed(both, width):
         spread = lax.all_to_all(both, "fsdp", 0, 0, axis_index_groups=across, tiled=True)
         return jnp.sum(spread[:, :, :width].astype(F32), axis=0), spread[:, :, width:]
 
-    for layer in (1, 0):
-        d_middle, d_mod, bias, ffn_wire = ffn_backward(
-            counts, upstream, records[layer], weights[layer], chips, layer == 1
-        )
-        ffn_sum, _ = summed(ffn_wire, 4 * D)
-        upstream, d_cond, attn_wire = attention_backward(
-            d_middle, hidden[layer], records[layer], weights[layer], d_mod, bias, condition, d_cond, chips, layer == 0
-        )
-        attn_sum, mods = summed(attn_wire, 2 * D + 128)
-        reduced[layer] = (ffn_sum, attn_sum, mods.reshape(24 * chips, D))
+    d_middle, d_mod, bias, wire = ffn_backward(core, counts, upstream, records[1], weights[1], chips, True)
+    d_middle, both = tie((d_middle, paired(wire, 4 * D)))
+    ffn_last, _ = summed(both, 4 * D)
+    upstream, d_cond, wire = attention_backward(
+        core, d_middle, hidden[1], records[1], weights[1], d_mod, bias, condition, d_cond, chips, False
+    )
+    wire, ffn_last = tie((wire, ffn_last))
+    upstream, both = tie((upstream, paired(wire, 2 * D + 128)))
+    attn_last, mods_last = summed(both, 2 * D + 128)
+    d_middle, d_mod, bias, wire = ffn_backward(core, counts, upstream, records[0], weights[0], chips, False)
+    wire, attn_last, mods_last = tie((wire, attn_last, mods_last))
+    d_middle, both = tie((d_middle, paired(wire, 4 * D)))
+    ffn_first, _ = summed(both, 4 * D)
+    upstream, d_cond, wire = attention_backward(
+        core, d_middle, hidden[0], records[0], weights[0], d_mod, bias, condition, d_cond, chips, True
+    )
+    wire, ffn_first = tie((wire, ffn_first))
+    attn_first, mods_first = summed(paired(wire, 2 * D + 128), 2 * D + 128)
+    reduced[0] = (ffn_first, attn_first, mods_first.reshape(24 * chips, D))
+    reduced[1] = (ffn_last, attn_last, mods_last.reshape(24 * chips, D))
     own_ffn = jnp.stack([reduced[layer][0] for layer in range(2)])
     own_attn = jnp.stack([reduced[layer][1] for layer in range(2)])
     own_mod = jnp.stack([reduced[layer][2] for layer in range(2)])
@@ -864,7 +930,7 @@
     got_mod = lax.ppermute(own_mod, "fsdp", swap)
     shapes = [array.shape for array in (ada_weight, qkv_weight, proj_weight, fc1_weight, fc2_weight, biases)]
     grads = finish(
-        core, chip, own_ffn, own_attn, got[:, :, : 2 * D], got[:, :, 2 * D :], own_mod, got_mod, conds[0], shapes, chips
+        core, chip, own_ffn, own_attn, got[:, :, : 2 * D], got[:, :, 2 * D :], own_mod, got_mod, cond_all, shapes, chips
     )
     return (hidden[2], upstream, d_cond, *grads)
 

time: 399 us -> 310 us (0.78)
  waiting for transfers between devices: 180 us -> 79.5 us
  starting transfers between devices: 30.6 us -> 46.4 us
  between operations: 14.9 us -> 1.75 us
  blocking collectives: 14.9 us -> 24.1 us
  Pallas kernels: 120 us -> 124 us
    all_gather x1 -> x0, waiting for transfers between devices: 91.1 us -> none  [fast_body(): gathered = lax.all_gather(packed, 'fsdp', axis=0, tiled=False)]
    all_to_all x4, waiting for transfers between devices: 83.7 us -> 43.1 us  [summed(): lax.all_to_all(both, 'fsdp', 0, 0, axis_index_groups=across, tiled=True)]
    ppermute x0 -> x32, waiting for transfers between devices: none -> 34.9 us  [the longest x28 26.2 us: along(): lax.ppermute(value, 'fsdp', [(one, one ^ bit) for one in range(devices)])]
    ppermute x0 -> x32, starting transfers between devices: none -> 16.8 us  [the longest x28 16.4 us: along(): lax.ppermute(value, 'fsdp', [(one, one ^ bit) for one in range(devices)])]
    all_to_all x2 -> x1, blocking collectives: 14.9 us -> 24.1 us  [stacked(): lax.all_to_all(copies, 'fsdp', 0, 0, axis_index_groups=lines, tiled=True)]
    pallas_call x3, Pallas kernels: 9.39 us -> 13.9 us  [the longest x2 12.4 us: unpack_wire(): pl.pallas_call(functools.partial(unpack_kernel, rows), out_shape=(jax.Sha...]
    squeeze x3 -> x6, local copies, waits for them, and re-layouts: 11 us -> 8.08 us  [the longest x4 6.1 us: paired(): got = lax.ppermute(wire[1], 'fsdp', swap)]
    unnamed x32 -> x54, local copies, waits for them, and re-layouts: 10.5 us -> 12.5 us
  transfers between devices with their start and end apart: 9 -> 39, of which waited for: 8 -> 20; matrix products, arithmetic and copies ran while one was open for 4% -> 1% of each run, Pallas kernels for 0% -> 26%
where the time goes in v2:
time: 310 us; the launch traced here: 309 us
  Pallas kernels  124 us (40%)
  waiting for transfers between devices  79.5 us (26%)
  starting transfers between devices  46.4 us (15%)
  blocking collectives  24.1 us (8%)
  local copies, waits for them, and re-layouts  22.8 us (7%)
  other arithmetic  9.74 us (3%)
    all_to_all x4, waiting for transfers between devices, summed(): lax.all_to_all(both, 'fsdp', 0, 0, axis_index_groups=across, tiled=True)  43.1 us
    pallas_call x2, Pallas kernels, attention_backward(): pl.pallas_call(functools.partial(attention_kernel, chips, first=first), g...  40.5 us
    pallas_call x2, Pallas kernels, forward_block(): pl.pallas_call(functools.partial(forward_kernel, last=last), grid=(SLOT,)...  37.2 us
    pallas_call x2, Pallas kernels, ffn_backward(): pl.pallas_call(functools.partial(ffn_kernel, chips, last=last), grid=(SLO...  30.6 us
    ppermute x28, waiting for transfers between devices, along(): lax.ppermute(value, 'fsdp', [(one, one ^ bit) for one in range(devices)])  26.2 us
    all_to_all x4, starting transfers between devices, summed(): lax.all_to_all(both, 'fsdp', 0, 0, axis_index_groups=across, tiled=True)  24.7 us
    all_to_all x1, blocking collectives, stacked(): lax.all_to_all(copies, 'fsdp', 0, 0, axis_index_groups=lines, tiled=True)  24.1 us
    ppermute x28, starting transfers between devices, along(): lax.ppermute(value, 'fsdp', [(one, one ^ bit) for one in range(devices)])  16.4 us
  transfers between devices with their start and end apart: 39, of which 20 were waited for; matrix products, arithmetic and copies ran while one was open for 1% of the time, Pallas kernels for 26%

profile of v2, /device:TPU:0, one launch (start us, length us, event | category | flops | bytes accessed | tf_op | source)
XLA Modules:
  0.0 308.8 jit_solution(17468462649796794848)
XLA Ops:
  7.8 24.1 %all_to_all.30 = bf16[4,24,3584]{2,1,0:T(8,128)(2,1)S(1)} all-to-all(bf16[4,24,3584]{2,1,0:T(8,128)(2,1)S(1)} %get-tuple-element.85), channel_id=1, replica_groups={{0,8,16,24},{1,9,17,25},{2,10,18,26},{3,11,19,27},{4,12,20,28},{5,13,21..., dimensions={0} | all-to-all | bytes 1376256 | tf_op jit(solution)/shard_map/all_to_all | solution.py:863
  31.9 4.2 %all-to-all-start.1 = ((bf16[4,24,3584]{2,1,0:T(8,128)(2,1)}), bf16[4,24,3584]{2,1,0:T(8,128)(2,1)}, u32[]{:S(2)}, u32[]{:S(2)}) async-start(bf16[4,24,3584]{2,1,0:T(8,128)(2,1)} %get-tuple-element.87), calls=%async_computation.1 | async-start | bytes 1376256 | tf_op jit(solution)/shard_map/all_to_all | solution.py:863
  40.3 6.9 %collective-permute-done.4.refs_2_ = bf16[2,24,3584]{2,1,0:T(8,128)(2,1)S(1)} collective-permute-done((bf16[2,24,3584]{2,1,0:T(8,128)(2,1)S(1)}, bf16[2,24,3584]{2,1,0:T(8,128)(2,1)S(1)}, u32[]{:S(2)}, u32[]{:S(2)}) %collective-permute-start.4) | collective-permute-done | bytes 344096 | tf_op jit(solution)/shard_map/ppermute | solution.py:860
  50.2 2.3 collective-permute-done.5.refs_3_
  57.4 3.7 %collective-permute-done.8.refs_6_ = bf16[2,24,3584]{2,1,0:T(8,128)(2,1)S(1)} collective-permute-done((bf16[2,24,3584]{2,1,0:T(8,128)(2,1)S(1)}, bf16[2,24,3584]{2,1,0:T(8,128)(2,1)S(1)}, u32[]{:S(2)}, u32[]{:S(2)}) %collective-permute-start.8) | collective-permute-done | bytes 344096 | tf_op jit(solution)/shard_map/ppermute | solution.py:860
  67.0 6.1 %unpack.2 = (bf16[384,2688]{1,0:T(8,128)(2,1)}, bf16[384,2688]{1,0:T(8,128)(2,1)}, bf16[1536,384]{1,0:T(8,128)(2,1)}, f32[1,5376]{1,0:T(1,128)S(1)}, f32[2,64,384]{2,1,0:T(8,128)S(1)}) custom-call(s32[2]{0:T(128)S(1)} %pad_add_fusion.place, bf16[2,24,3584]{2,1,0:T(8,128)(2,1)S(1)} %get-tuple-element.166.refs_0_, ...), custom_call_target="tpu_custom_call" | custom-call | tf_op jit(solution)/shard_map/unpack/pallas_call | solution.py:428
  74.5 18.5 %forward_block.2 = (f32[4,256,384]{2,1,0:T(8,128)}, f32[4,2304]{1,0:T(4,128)S(1)}, bf16[4,256,1152]{2,1,0:T(8,128)(2,1)}, bf16[4,256,384]{2,1,0:T(8,128)(2,1)S(1...) custom-call(s32[1]{0:T(128)S(6)} %copy.19.counts, ...), custom_call_target="tpu_custom_call" | custom-call | flops 5000000000 | bytes 20971520 | tf_op jit(solution)/shard_map/forward_block/pallas_call | solution.py:523
  96.0 6.4 %collective-permute-done.18.refs_6_ = bf16[2,24,3584]{2,1,0:T(8,128)(2,1)S(1)} collective-permute-done((bf16[2,24,3584]{2,1,0:T(8,128)(2,1)S(1)}, bf16[2,24,3584]{2,1,0:T(8,128)(2,1)S(1)}, u32[]{:S(2)}, u32[]{:S(2)}) %collective-permute-start.18) | collective-permute-done | bytes 344096 | tf_op jit(solution)/shard_map/ppermute | solution.py:860
  107.8 6.2 %unpack.3 = (bf16[384,2688]{1,0:T(8,128)(2,1)}, bf16[384,2688]{1,0:T(8,128)(2,1)}, bf16[1536,384]{1,0:T(8,128)(2,1)}, f32[1,5376]{1,0:T(1,128)S(1)}, f32[2,64,384]{2,1,0:T(8,128)}) custom-call(s32[2]{0:T(128)S(1)} %pad_add_fusion.place, bf16[2,24,3584]{2,1,0:T(8,128)(2,1)S(1)} %get-tuple-element.102.refs_0_, ...), custom_call_target="tpu_custom_call" | custom-call | tf_op jit(solution)/shard_map/unpack/pallas_call | solution.py:428
  115.3 18.6 %forward_block.3 = (f32[4,256,384]{2,1,0:T(8,128)}, f32[4,2304]{1,0:T(4,128)S(1)}, bf16[4,256,1152]{2,1,0:T(8,128)(2,1)}, bf16[4,256,384]{2,1,0:T(8,128)(2,1)S(1...) custom-call(s32[1]{0:T(128)S(6)} %copy.19.counts, ...), custom_call_target="tpu_custom_call" | custom-call | flops 5000000000 | bytes 20971520 | tf_op jit(solution)/shard_map/forward_block/pallas_call | solution.py:523
  135.1 15.3 %ffn_backward.2 = (f32[4,256,384]{2,1,0:T(8,128)S(1)}, f32[24,384]{1,0:T(8,128)S(1)}, f32[1,1920]{1,0:T(1,128)S(1)}, bf16[2,16,24,1536]{3,2,1,0:T(8,128)(2,1)}) custom-call(s32[1]{0:T(128)} %bitcast.core, s32[1]{0:T(128)S(6)} %copy.19.counts, bf16[4,256,384]{2,1,0:T(8,128)(2,1)S(1)} %copy-done.13, f32[4,256,384]{2,1,0:T(8,128)} %get-tuple-element.113.branch, ...), custom_call_target="tpu_custom_call" | custom-call | flops 8000000000 | bytes 20971520 | tf_op jit(solution)/shard_map/ffn_backward/pallas_call | solution.py:623
  152.1 2.7 collective-permute-done.28
  156.1 5.1 %all-to-all-start.2 = ((bf16[16,24,1536]{2,1,0:T(8,128)(2,1)}), bf16[16,24,1536]{2,1,0:T(8,128)(2,1)}, u32[]{:S(2)}, u32[]{:S(2)}) async-start(bf16[16,24,1536]{2,1,0:T(8,128)(2,1)} %fusion.1), calls=%async_computation.2 | async-start | bytes 2359296 | tf_op jit(solution)/shard_map/all_to_all | solution.py:901
  161.3 20.4 %attention_backward.2 = (f32[4,256,384]{2,1,0:T(8,128)S(1)}, f32[4,384]{1,0:T(4,128)S(1)}, bf16[2,16,24,1280]{3,2,1,0:T(8,128)(2,1)}) custom-call(s32[1]{0:T(128)} %bitcast.core, f32[4,256,384]{2,1,0:T(8,128)S(1)} %get-tuple-element.119.d_middle, f32[4,256,384]{2,1,0:T(8,128)} %get-tuple-element.101.hidden, bf16[4,256,1152]{2,1,0:T(8,128)(2,1)} %get-tuple-element.120.qkv, ...), custom_call_target="tpu_custom_call" | custom-call | flops 6000000000 | bytes 20971520 | tf_op jit(solution)/shard_map/attention_backward/pallas_call | solution.py:743
  182.9 5.6 %all-to-all-done.2 = bf16[16,24,1536]{2,1,0:T(8,128)(2,1)} async-done(((bf16[16,24,1536]{2,1,0:T(8,128)(2,1)}), bf16[16,24,1536]{2,1,0:T(8,128)(2,1)}, u32[]{:S(2)}, u32[]{:S(2)}) %all-to-all-start.2) | async-done | bytes 1179680 | tf_op jit(solution)/shard_map/all_to_all | solution.py:901
  195.4 6.9 %all-to-all-start.3 = ((bf16[16,24,1280]{2,1,0:T(8,128)(2,1)}), bf16[16,24,1280]{2,1,0:T(8,128)(2,1)}, u32[]{:S(2)}, u32[]{:S(2)}) async-start(bf16[16,24,1280]{2,1,0:T(8,128)(2,1)} %pad_maximum_fusion), calls=%async_computation.3 | async-start | bytes 1966080 | tf_op jit(solution)/shard_map/all_to_all | solution.py:901
  202.3 15.3 %ffn_backward.3 = (f32[4,256,384]{2,1,0:T(8,128)S(1)}, f32[24,384]{1,0:T(8,128)S(1)}, f32[1,1920]{1,0:T(1,128)S(1)}, bf16[2,16,24,1536]{3,2,1,0:T(8,128)(2,1)}) custom-call(s32[1]{0:T(128)} %bitcast.core, s32[1]{0:T(128)S(6)} %copy.19.counts, f32[4,256,384]{2,1,0:T(8,128)} %copy-done.16, f32[4,256,384]{2,1,0:T(8,128)} %get-tuple-element.130.branch, ...), custom_call_target="tpu_custom_call" | custom-call | flops 8000000000 | bytes 20971520 | tf_op jit(solution)/shard_map/ffn_backward/pallas_call | solution.py:623
  217.6 8.1 %all-to-all-done.3 = bf16[16,24,1280]{2,1,0:T(8,128)(2,1)} async-done(((bf16[16,24,1280]{2,1,0:T(8,128)(2,1)}), bf16[16,24,1280]{2,1,0:T(8,128)(2,1)}, u32[]{:S(2)}, u32[]{:S(2)}) %all-to-all-start.3) | async-done | bytes 983072 | tf_op jit(solution)/shard_map/all_to_all | solution.py:901
  229.5 2.8 collective-permute-done.30
  233.7 5.9 %all-to-all-start.4 = ((bf16[16,24,1536]{2,1,0:T(8,128)(2,1)}), bf16[16,24,1536]{2,1,0:T(8,128)(2,1)}, u32[]{:S(2)}, u32[]{:S(2)}) async-start(bf16[16,24,1536]{2,1,0:T(8,128)(2,1)} %fusion), calls=%async_computation.4 | async-start | bytes 2359296 | tf_op jit(solution)/shard_map/all_to_all | solution.py:901
  240.8 20.1 %attention_backward.3 = (f32[4,256,384]{2,1,0:T(8,128)}, f32[4,384]{1,0:T(4,128)}, bf16[2,16,24,1280]{3,2,1,0:T(8,128)(2,1)}) custom-call(s32[1]{0:T(128)} %bitcast.core, f32[4,256,384]{2,1,0:T(8,128)S(1)} %get-tuple-element.138.d_middle, bf16[4,256,384]{2,1,0:T(8,128)(2,1)S(1)} %copy-done.15, bf16[4,256,1152]{2,1,0:T(8,128)(2,1)} %get-tuple-element.139.qkv, ...), custom_call_target="tpu_custom_call" | custom-call | flops 6000000000 | bytes 20971520 | tf_op jit(solution)/shard_map/attention_backward/pallas_call | solution.py:743
  260.9 5.9 %all-to-all-done.4 = bf16[16,24,1536]{2,1,0:T(8,128)(2,1)} async-done(((bf16[16,24,1536]{2,1,0:T(8,128)(2,1)}), bf16[16,24,1536]{2,1,0:T(8,128)(2,1)}, u32[]{:S(2)}, u32[]{:S(2)}) %all-to-all-start.4) | async-done | bytes 1179680 | tf_op jit(solution)/shard_map/all_to_all | solution.py:901
  273.8 6.8 %all-to-all-start.5 = ((bf16[16,24,1280]{2,1,0:T(8,128)(2,1)}), bf16[16,24,1280]{2,1,0:T(8,128)(2,1)S(1)}, u32[]{:S(2)}, u32[]{:S(2)}) async-start(bf16[16,24,1280]{2,1,0:T(8,128)(2,1)} %pad_maximum_fusion.1), calls=%async_computation.5 | async-start | bytes 1966080 | tf_op jit(solution)/shard_map/all_to_all | solution.py:901
  280.6 23.4 %all-to-all-done.5 = bf16[16,24,1280]{2,1,0:T(8,128)(2,1)S(1)} async-done(((bf16[16,24,1280]{2,1,0:T(8,128)(2,1)}), bf16[16,24,1280]{2,1,0:T(8,128)(2,1)S(1)}, u32[]{:S(2)}, u32[]{:S(2)}) %all-to-all-start.5) | async-done | bytes 983072 | tf_op jit(solution)/shard_map/all_to_all | solution.py:901
  (147 shorter events, 65.4 us)
Async XLA Ops:
  31.9 29.8 %all-to-all-start.1 = ((bf16[4,24,3584]{2,1,0:T(8,128)(2,1)}), bf16[4,24,3584]{2,1,0:T(8,128)(2,1)}, u32[]{:S(2)}, u32[]{:S(2)}) async-start(bf16[4,24,3584]{2,1,0:T(8,128)(2,1)} %get-tuple-element.87), calls=%async_computation.1 | async-start | bytes 1376256 | tf_op jit(solution)/shard_map/all_to_all | solution.py:863
  36.2 11.1 %collective-permute-start.4 = (bf16[2,24,3584]{2,1,0:T(8,128)(2,1)S(1)}, bf16[2,24,3584]{2,1,0:T(8,128)(2,1)S(1)}, u32[]{:S(2)}, u32[]{:S(2)}) collective-permute-start(bf16[2,24,3584]{2,1,0:T(8,128)(2,1)S(1)} %get-tuple-element.166.refs_0_), channel_id=1, source_target_pairs={{0,2},{1,3},{2,0},{3,1},{4,6},{5,7},{6,4},{7,5},{8,10},{9,11},{10,... | collective-permute-start | bytes 1032200 | tf_op jit(solution)/shard_map/ppermute | solution.py:860
  37.7 11.0 %collective-permute-start.7 = (bf16[2,24,3584]{2,1,0:T(8,128)(2,1)S(1)}, bf16[2,24,3584]{2,1,0:T(8,128)(2,1)S(1)}, u32[]{:S(2)}, u32[]{:S(2)}) collective-permute-start(bf16[2,24,3584]{2,1,0:T(8,128)(2,1)S(1)} %get-tuple-element.165.refs_1_), channel_id=1, source_target_pairs={{0,4},{1,5},{2,6},{3,7},{4,0},{5,1},{6,2},{7,3},{8,12},{9,13},{10,... | collective-permute-start | bytes 1032200 | tf_op jit(solution)/shard_map/ppermute | solution.py:860
  39.2 13.3 %collective-permute-start.5 = (bf16[2,24,3584]{2,1,0:T(8,128)(2,1)S(1)}, bf16[2,24,3584]{2,1,0:T(8,128)(2,1)S(1)}, u32[]{:S(2)}, u32[]{:S(2)}) collective-permute-start(bf16[2,24,3584]{2,1,0:T(8,128)(2,1)S(1)} %get-tuple-element.165.refs_1_), channel_id=1, source_target_pairs={{0,2},{1,3},{2,0},{3,1},{4,6},{5,7},{6,4},{7,5},{8,10},{9,11},{10,... | collective-permute-start | bytes 1032200 | tf_op jit(solution)/shard_map/ppermute | solution.py:860
  39.8 16.3 %collective-permute-start.6 = (bf16[2,24,3584]{2,1,0:T(8,128)(2,1)S(1)}, bf16[2,24,3584]{2,1,0:T(8,128)(2,1)S(1)}, u32[]{:S(2)}, u32[]{:S(2)}) collective-permute-start(bf16[2,24,3584]{2,1,0:T(8,128)(2,1)S(1)} %get-tuple-element.166.refs_0_), channel_id=1, source_target_pairs={{0,4},{1,5},{2,6},{3,7},{4,0},{5,1},{6,2},{7,3},{8,12},{9,13},{10,... | collective-permute-start | bytes 1032200 | tf_op jit(solution)/shard_map/ppermute | solution.py:860
  40.3 16.6 %collective-permute-start.10 = (bf16[2,24,3584]{2,1,0:T(8,128)(2,1)S(1)}, bf16[2,24,3584]{2,1,0:T(8,128)(2,1)S(1)}, u32[]{:S(2)}, u32[]{:S(2)}) collective-permute-start(bf16[2,24,3584]{2,1,0:T(8,128)(2,1)S(1)} %get-tuple-element.166.refs_0_), channel_id=1, source_target_pairs={{0,1},{1,0},{2,3},{3,2},{4,5},{5,4},{6,7},{7,6},{8,9},{9,8},{10,11... | collective-permute-start | bytes 1032200 | tf_op jit(solution)/shard_map/ppermute | solution.py:860
  47.2 10.1 %collective-permute-start.11 = (bf16[2,24,3584]{2,1,0:T(8,128)(2,1)S(1)}, bf16[2,24,3584]{2,1,0:T(8,128)(2,1)S(1)}, u32[]{:S(2)}, u32[]{:S(2)}) collective-permute-start(bf16[2,24,3584]{2,1,0:T(8,128)(2,1)S(1)} %get-tuple-element.165.refs_1_), channel_id=1, source_target_pairs={{0,1},{1,0},{2,3},{3,2},{4,5},{5,4},{6,7},{7,6},{8,9},{9,8},{10,11... | collective-permute-start | bytes 1032200 | tf_op jit(solution)/shard_map/ppermute | solution.py:860
  48.7 12.4 %collective-permute-start.8 = (bf16[2,24,3584]{2,1,0:T(8,128)(2,1)S(1)}, bf16[2,24,3584]{2,1,0:T(8,128)(2,1)S(1)}, u32[]{:S(2)}, u32[]{:S(2)}) collective-permute-start(bf16[2,24,3584]{2,1,0:T(8,128)(2,1)S(1)} %collective-permute-done.4.refs_2_), channel_id=1, source_target_pairs={{0,4},{1,5},{2,6},{3,7},{4,0},{5,1},{6,2},{7,3},{8,12},{9,13},{10,... | collective-permute-start | bytes 1032200 | tf_op jit(solution)/shard_map/ppermute | solution.py:860
  52.6 8.6 %collective-permute-start.9 = (bf16[2,24,3584]{2,1,0:T(8,128)(2,1)S(1)}, bf16[2,24,3584]{2,1,0:T(8,128)(2,1)S(1)}, u32[]{:S(2)}, u32[]{:S(2)}) collective-permute-start(bf16[2,24,3584]{2,1,0:T(8,128)(2,1)S(1)} %collective-permute-done.7.refs_5_), channel_id=1, source_target_pairs={{0,2},{1,3},{2,0},{3,1},{4,6},{5,7},{6,4},{7,5},{8,10},{9,11},{10,... | collective-permute-start | bytes 1032200 | tf_op jit(solution)/shard_map/ppermute | solution.py:860
  56.8 6.0 %collective-permute-start.15 = (bf16[2,24,3584]{2,1,0:T(8,128)(2,1)S(1)}, bf16[2,24,3584]{2,1,0:T(8,128)(2,1)}, u32[]{:S(2)}, u32[]{:S(2)}) collective-permute-start(bf16[2,24,3584]{2,1,0:T(8,128)(2,1)S(1)} %collective-permute-done.7.refs_5_), channel_id=1, source_target_pairs={{0,1},{1,0},{2,3},{3,2},{4,5},{5,4},{6,7},{7,6},{8,9},{9,8},{10,11... | collective-permute-start | bytes 1032200 | tf_op jit(solution)/shard_map/ppermute | solution.py:860
  57.3 6.5 %collective-permute-start.13 = (bf16[2,24,3584]{2,1,0:T(8,128)(2,1)S(1)}, bf16[2,24,3584]{2,1,0:T(8,128)(2,1)}, u32[]{:S(2)}, u32[]{:S(2)}) collective-permute-start(bf16[2,24,3584]{2,1,0:T(8,128)(2,1)S(1)} %collective-permute-done.5.refs_3_), channel_id=1, source_target_pairs={{0,1},{1,0},{2,3},{3,2},{4,5},{5,4},{6,7},{7,6},{8,9},{9,8},{10,11... | collective-permute-start | bytes 1032200 | tf_op jit(solution)/shard_map/ppermute | solution.py:860
  62.9 30.2 %collective-permute-start = (bf16[2,24,3584]{2,1,0:T(8,128)(2,1)S(1)}, bf16[2,24,3584]{2,1,0:T(8,128)(2,1)S(1)}, u32[]{:S(2)}, u32[]{:S(2)}) collective-permute-start(bf16[2,24,3584]{2,1,0:T(8,128)(2,1)S(1)} %get-tuple-element.102.refs_0_), channel_id=1, source_target_pairs={{0,2},{1,3},{2,0},{3,1},{4,6},{5,7},{6,4},{7,5},{8,10},{9,11},{10,... | collective-permute-start | bytes 1032200 | tf_op jit(solution)/shard_map/ppermute | solution.py:860
  63.8 29.2 %collective-permute-start.2 = (bf16[2,24,3584]{2,1,0:T(8,128)(2,1)S(1)}, bf16[2,24,3584]{2,1,0:T(8,128)(2,1)S(1)}, u32[]{:S(2)}, u32[]{:S(2)}) collective-permute-start(bf16[2,24,3584]{2,1,0:T(8,128)(2,1)S(1)} %get-tuple-element.102.refs_0_), channel_id=1, source_target_pairs={{0,4},{1,5},{2,6},{3,7},{4,0},{5,1},{6,2},{7,3},{8,12},{9,13},{10,... | collective-permute-start | bytes 1032200 | tf_op jit(solution)/shard_map/ppermute | solution.py:860
  65.3 27.7 %collective-permute-start.1 = (bf16[2,24,3584]{2,1,0:T(8,128)(2,1)S(1)}, bf16[2,24,3584]{2,1,0:T(8,128)(2,1)S(1)}, u32[]{:S(2)}, u32[]{:S(2)}) collective-permute-start(bf16[2,24,3584]{2,1,0:T(8,128)(2,1)S(1)} %get-tuple-element.103.refs_1_), channel_id=1, source_target_pairs={{0,2},{1,3},{2,0},{3,1},{4,6},{5,7},{6,4},{7,5},{8,10},{9,11},{10,... | collective-permute-start | bytes 1032200 | tf_op jit(solution)/shard_map/ppermute | solution.py:860
  66.5 26.6 %collective-permute-start.3 = (bf16[2,24,3584]{2,1,0:T(8,128)(2,1)S(1)}, bf16[2,24,3584]{2,1,0:T(8,128)(2,1)S(1)}, u32[]{:S(2)}, u32[]{:S(2)}) collective-permute-start(bf16[2,24,3584]{2,1,0:T(8,128)(2,1)S(1)} %get-tuple-element.103.refs_1_), channel_id=1, source_target_pairs={{0,4},{1,5},{2,6},{3,7},{4,0},{5,1},{6,2},{7,3},{8,12},{9,13},{10,... | collective-permute-start | bytes 1032200 | tf_op jit(solution)/shard_map/ppermute | solution.py:860
  93.1 9.4 %collective-permute-start.18 = (bf16[2,24,3584]{2,1,0:T(8,128)(2,1)S(1)}, bf16[2,24,3584]{2,1,0:T(8,128)(2,1)S(1)}, u32[]{:S(2)}, u32[]{:S(2)}) collective-permute-start(bf16[2,24,3584]{2,1,0:T(8,128)(2,1)S(1)} %collective-permute-done.refs_2_), channel_id=1, source_target_pairs={{0,4},{1,5},{2,6},{3,7},{4,0},{5,1},{6,2},{7,3},{8,12},{9,13},{10,... | collective-permute-start | bytes 1032200 | tf_op jit(solution)/shard_map/ppermute | solution.py:860
  94.7 9.0 %collective-permute-start.19 = (bf16[2,24,3584]{2,1,0:T(8,128)(2,1)S(1)}, bf16[2,24,3584]{2,1,0:T(8,128)(2,1)S(1)}, u32[]{:S(2)}, u32[]{:S(2)}) collective-permute-start(bf16[2,24,3584]{2,1,0:T(8,128)(2,1)S(1)} %collective-permute-done.3.refs_5_), channel_id=1, source_target_pairs={{0,2},{1,3},{2,0},{3,1},{4,6},{5,7},{6,4},{7,5},{8,10},{9,11},{10,... | collective-permute-start | bytes 1032200 | tf_op jit(solution)/shard_map/ppermute | solution.py:860
  95.5 8.1 %collective-permute-start.20 = (bf16[2,24,3584]{2,1,0:T(8,128)(2,1)S(1)}, bf16[2,24,3584]{2,1,0:T(8,128)(2,1)S(1)}, u32[]{:S(2)}, u32[]{:S(2)}) collective-permute-start(bf16[2,24,3584]{2,1,0:T(8,128)(2,1)S(1)} %get-tuple-element.102.refs_0_), channel_id=1, source_target_pairs={{0,1},{1,0},{2,3},{3,2},{4,5},{5,4},{6,7},{7,6},{8,9},{9,8},{10,11... | collective-permute-start | bytes 1032200 | tf_op jit(solution)/shard_map/ppermute | solution.py:860
  95.5 8.6 %collective-permute-start.21 = (bf16[2,24,3584]{2,1,0:T(8,128)(2,1)S(1)}, bf16[2,24,3584]{2,1,0:T(8,128)(2,1)S(1)}, u32[]{:S(2)}, u32[]{:S(2)}) collective-permute-start(bf16[2,24,3584]{2,1,0:T(8,128)(2,1)S(1)} %get-tuple-element.103.refs_1_), channel_id=1, source_target_pairs={{0,1},{1,0},{2,3},{3,2},{4,5},{5,4},{6,7},{7,6},{8,9},{9,8},{10,11... | collective-permute-start | bytes 1032200 | tf_op jit(solution)/shard_map/ppermute | solution.py:860
  96.0 8.2 %collective-permute-start.22 = (bf16[2,24,3584]{2,1,0:T(8,128)(2,1)S(1)}, bf16[2,24,3584]{2,1,0:T(8,128)(2,1)S(1)}, u32[]{:S(2)}, u32[]{:S(2)}) collective-permute-start(bf16[2,24,3584]{2,1,0:T(8,128)(2,1)S(1)} %collective-permute-done.refs_2_), channel_id=1, source_target_pairs={{0,1},{1,0},{2,3},{3,2},{4,5},{5,4},{6,7},{7,6},{8,9},{9,8},{10,11... | collective-permute-start | bytes 1032200 | tf_op jit(solution)/shard_map/ppermute | solution.py:860
  156.1 32.3 %all-to-all-start.2 = ((bf16[16,24,1536]{2,1,0:T(8,128)(2,1)}), bf16[16,24,1536]{2,1,0:T(8,128)(2,1)}, u32[]{:S(2)}, u32[]{:S(2)}) async-start(bf16[16,24,1536]{2,1,0:T(8,128)(2,1)} %fusion.1), calls=%async_computation.2 | async-start | bytes 2359296 | tf_op jit(solution)/shard_map/all_to_all | solution.py:901
  195.4 30.4 %all-to-all-start.3 = ((bf16[16,24,1280]{2,1,0:T(8,128)(2,1)}), bf16[16,24,1280]{2,1,0:T(8,128)(2,1)}, u32[]{:S(2)}, u32[]{:S(2)}) async-start(bf16[16,24,1280]{2,1,0:T(8,128)(2,1)} %pad_maximum_fusion), calls=%async_computation.3 | async-start | bytes 1966080 | tf_op jit(solution)/shard_map/all_to_all | solution.py:901
  233.7 33.1 %all-to-all-start.4 = ((bf16[16,24,1536]{2,1,0:T(8,128)(2,1)}), bf16[16,24,1536]{2,1,0:T(8,128)(2,1)}, u32[]{:S(2)}, u32[]{:S(2)}) async-start(bf16[16,24,1536]{2,1,0:T(8,128)(2,1)} %fusion), calls=%async_computation.4 | async-start | bytes 2359296 | tf_op jit(solution)/shard_map/all_to_all | solution.py:901
  273.8 30.2 %all-to-all-start.5 = ((bf16[16,24,1280]{2,1,0:T(8,128)(2,1)}), bf16[16,24,1280]{2,1,0:T(8,128)(2,1)S(1)}, u32[]{:S(2)}, u32[]{:S(2)}) async-start(bf16[16,24,1280]{2,1,0:T(8,128)(2,1)} %pad_maximum_fusion.1), calls=%async_computation.5 | async-start | bytes 1966080 | tf_op jit(solution)/shard_map/all_to_all | solution.py:901
  (42 other events, 167.0 us)

commit v3 on v2

--- a/solution.py
+++ b/solution.py
@@ -314,6 +314,8 @@
 BF16 = jnp.bfloat16
 F32 = jnp.float32
 SLOT = 4
+STEP = 1
+CHUNK = 512
 SEQ = 256
 HALF = 7 * D
 WIRE = HALF + 2 * D + 128
@@ -322,9 +324,9 @@
 SMEM = pl.BlockSpec(memory_space=pltpu.SMEM)
 
 
-def params_of(grid_rank=0):
+def params_of(grid_rank=0, megabytes=36):
     semantics = ("arbitrary",) * grid_rank if grid_rank else None
-    return pltpu.CompilerParams(vmem_limit_bytes=50 * 2**20, dimension_semantics=semantics)
+    return pltpu.CompilerParams(vmem_limit_bytes=megabytes * 2**20, dimension_semantics=semantics)
 
 
 def dot_nn(left, right):
@@ -333,7 +335,7 @@
     )
 
 
-def pack_kernel(rows, ada_in, qkv_in, proj_in, fc1_in, fc2_in, bias_in, cond, out_first, out_last, ada, qkv, proj, fc1, fc2, bias, sems, wide):
+def pack_kernel(rows, ada_in, qkv_in, proj_in, fc1_in, fc2_in, bias_in, cond, out_left, out_right, out_last, ada, qkv, proj, fc1, fc2, bias, sems, wide):
     copies = [
         pltpu.make_async_copy(source, target, sems.at[place])
         for place, (source, target) in enumerate(
@@ -365,35 +367,42 @@
         put(fc2, row * D, D, row % (2 * rows), HALF + D * (row // (2 * rows)))
     put(bias, 0, 128, 0, WIRE - 128)
     put(bias, 128, 128, 1, WIRE - 128)
-    for layer, out in enumerate((out_first, out_last)):
-        low = wide[layer].astype(BF16)
-        for copy_index in range(out.shape[0]):
-            out[copy_index] = low
+    low = wide[0].astype(BF16)
+    low_last = wide[1].astype(BF16)
+    for copy_index in range(out_last.shape[0]):
+        out_left[copy_index] = low[:, : WIRE // 2]
+        out_right[copy_index] = low[:, WIRE // 2 :]
+        out_last[copy_index] = low_last
 
 
 def pack(ada, qkv, proj, fc1, fc2, bias, cond, rows, copies):
     flat = (ada, qkv, proj, fc1, fc2, bias)
     return pl.pallas_call(
         functools.partial(pack_kernel, rows),
-        out_shape=(jax.ShapeDtypeStruct((copies, 2 * rows, WIRE), BF16),) * 2,
-        in_specs=[pl.BlockSpec(memory_space=pl.ANY)] * 6 + [VMEM],
-        out_specs=(VMEM, VMEM),
+        out_shape=tuple(
+            jax.ShapeDtypeStruct((copies, 2 * rows, width), BF16) for width in (WIRE // 2, WIRE // 2, WIRE)
+        ),
+        in_specs=[pl.BlockSpec(memory_space=pltpu.HBM)] * 6 + [VMEM],
+        out_specs=(VMEM,) * 3,
         scratch_shapes=[pltpu.VMEM(array.shape, BF16) for array in flat]
         + [pltpu.SemaphoreType.DMA((6,)), pltpu.VMEM((2, 2 * rows, WIRE), F32)],
-        compiler_params=params_of(),
+        compiler_params=params_of(0, 62),
         name="pack",
     )(*flat, cond)
 
 
-def unpack_kernel(rows, place, *refs):
-    blocks, (left, right, down, bias, cond, wire, sems) = refs[:16], refs[16:]
+def unpack_kernel(rows, spots, place, *refs):
+    blocks, (left, right, down, bias, cond, wire, sems) = refs[:-7], refs[-7:]
     copies = []
-    for side in range(2):
-        for step in range(4):
-            for half in range(2):
-                number = 8 * side + 2 * step + half
-                target = wire.at[(place[0] + side) % 2, place[1] ^ step, pl.ds(2 * half, 2)]
-                copies.append(pltpu.make_async_copy(blocks[number], target, sems.at[number]))
+    for number, (block, (side, step, level, column)) in enumerate(zip(blocks, spots, strict=True)):
+        target = wire.at[
+            (place[0] + side) % 2,
+            place[1] ^ step,
+            pl.ds(level, block.shape[0]),
+            :,
+            pl.ds(column, block.shape[2]),
+        ]
+        copies.append(pltpu.make_async_copy(block, target, sems.at[number]))
     for copy in copies:
         copy.start()
     for copy in copies:
@@ -423,10 +432,11 @@
             ]
 
 
-def unpack_wire(place, blocks):
+def unpack_wire(place, held):
+    blocks, spots = [block for block, _ in held], [spot for _, spot in held]
     rows = blocks[0].shape[1] // 2
     return pl.pallas_call(
-        functools.partial(unpack_kernel, rows),
+        functools.partial(unpack_kernel, rows, spots),
         out_shape=(
             jax.ShapeDtypeStruct((D, HALF), BF16),
             jax.ShapeDtypeStruct((D, HALF), BF16),
@@ -434,10 +444,10 @@
             jax.ShapeDtypeStruct((1, BIAS), F32),
             jax.ShapeDtypeStruct((2, SLOT * 16, D), F32),
         ),
-        in_specs=[SMEM] + [pl.BlockSpec(memory_space=pl.ANY)] * 16,
+        in_specs=[SMEM] + [pl.BlockSpec(memory_space=pl.ANY)] * len(blocks),
         out_specs=(VMEM,) * 5,
-        scratch_shapes=[pltpu.VMEM((2, 4, 4, 2 * rows, WIRE), BF16), pltpu.SemaphoreType.DMA((16,))],
-        compiler_params=params_of(),
+        scratch_shapes=[pltpu.VMEM((2, 4, 4, 2 * rows, WIRE), BF16), pltpu.SemaphoreType.DMA((len(blocks),))],
+        compiler_params=params_of(0, 24),
         name="unpack",
     )(place, *blocks)
 
@@ -448,66 +458,122 @@
     return centred * rstd, rstd
 
 
-def mod_part(mod, slot, part):
-    return mod[pl.ds(slot, 1), part * D : (part + 1) * D]
-
-
-def gelu_parts(pre):
-    inner = 0.7978845608028654 * (pre + 0.044715 * (pre * pre * pre))
-    return jnp.tanh(inner)
-
-
-def forward_kernel(counts, hidden, cond, left, right, down, bias, out, mod, qkv, attended, projected, middle, pre_act, branch, *, last):
-    slot = pl.program_id(0)
-
-    @pl.when(slot == 0)
+def mod_part(mod, step, part):
+    rows = [
+        jnp.broadcast_to(mod[pl.ds(STEP * step + slot, 1), part * D : (part + 1) * D], (SEQ, D))
+        for slot in range(STEP)
+    ]
+    return rows[0] if STEP == 1 else jnp.concatenate(rows, axis=0)
+
+
+def put_sums(d_mod, step, part, values):
+    for slot in range(STEP):
+        d_mod[pl.ds(SLOT * part + STEP * step + slot, 1), :] = row_sum(values[slot * SEQ : (slot + 1) * SEQ])
+
+
+def occupied(counts, step):
+    rows = [
+        jnp.full((SEQ, 1), jnp.where(STEP * step + slot < counts[0], 1.0, 0.0), F32) for slot in range(STEP)
+    ]
+    return rows[0] if STEP == 1 else jnp.concatenate(rows, axis=0)
+
+
+def flat(ref):
+    return ref[...].reshape(STEP * SEQ, ref.shape[2])
+
+
+def gelu_and_slope(pre):
+    factor, cubic = 0.7978845608028654, 0.044715
+    square = pre * pre
+    half = 0.5 + 0.5 * jnp.tanh(pre * (factor + (factor * cubic) * square))
+    act = pre * half
+    return act, half + act * (1.0 - half) * (2.0 * factor + (6.0 * factor * cubic) * square)
+
+
+def row_sum(values):
+    return jnp.sum(values, axis=0, keepdims=True)
+
+
+def head_masks(factor):
+    lane = lax.broadcasted_iota(jnp.int32, (1, 2 * HEAD), 1)
+    first = jnp.where(lane < HEAD, factor, 0.0).astype(BF16)
+    second = jnp.where(lane < HEAD, 0.0, factor).astype(BF16)
+    return first, second
+
+
+def both_heads(pair, masks):
+    return jnp.concatenate([pair * masks[0], pair * masks[1]], axis=0)
+
+
+def merge_heads(stack):
+    lane = lax.broadcasted_iota(jnp.int32, (SEQ, 2 * HEAD), 1)
+    return jnp.where(lane < HEAD, stack[:SEQ], stack[SEQ:])
+
+
+def softmax_keys(scores):
+    raised = jnp.exp(scores - jnp.max(scores, axis=0, keepdims=True))
+    return raised * (1.0 / jnp.sum(raised, axis=0, keepdims=True))
+
+
+def forward_kernel(counts, hidden, cond, left, right, down, bias, out, mod, qkv, attended, projected, middle, active, slope, branch, *, last):
+    step = pl.program_id(0)
+
+    @pl.when(step == 0)
     def _():
         wide_cond = cond[...].astype(F32)
         act = (wide_cond / (1.0 + jnp.exp(-wide_cond))).astype(BF16)
         mod[...] = dot_nn(act, left[:, : 6 * D]) + bias[:, : 6 * D]
 
-    values = hidden[0].astype(F32)
+    values = flat(hidden).astype(F32)
     normed, _ = norm_stats(values)
-    normed = (normed * (1.0 + mod_part(mod, slot, 1)) + mod_part(mod, slot, 0)).astype(BF16)
+    normed = (normed * (1.0 + mod_part(mod, step, 1)) + mod_part(mod, step, 0)).astype(BF16)
     queries = (dot_nn(normed, left[:, 6 * D :]) + bias[:, 6 * D : 7 * D]).astype(BF16)
-    keys = dot_nn(normed, right[:, :D]).astype(BF16)
-    heads_in = (dot_nn(normed, right[:, D : 2 * D]) + bias[:, 7 * D : 8 * D]).astype(BF16)
-    qkv[0, :, :D] = queries
-    qkv[0, :, D : 2 * D] = keys
-    qkv[0, :, 2 * D :] = heads_in
-    scaled = queries * jnp.asarray(1.0 / math.sqrt(HEAD), BF16)
+    mixed = dot_nn(normed, right[:, : 2 * D])
+    keys = mixed[:, :D].astype(BF16)
+    heads_in = (mixed[:, D:] + bias[:, 7 * D : 8 * D]).astype(BF16)
+    qkv[:, :, :D] = queries.reshape(STEP, SEQ, D)
+    qkv[:, :, D : 2 * D] = keys.reshape(STEP, SEQ, D)
+    qkv[:, :, 2 * D :] = heads_in.reshape(STEP, SEQ, D)
+    masks = head_masks(1.0 / math.sqrt(HEAD))
     joined = []
-    for head in range(HEADS):
-        span = slice(head * HEAD, (head + 1) * HEAD)
-        scores = right_product(scaled[:, span], keys[:, span])
-        raised = jnp.exp(scores - jnp.max(scores, axis=-1, keepdims=True))
-        probs = (raised * (1.0 / jnp.sum(raised, axis=-1, keepdims=True))).astype(BF16)
-        joined.append(dot_nn(probs, heads_in[:, span]).astype(BF16))
-    joined = jnp.concatenate(joined, axis=1)
-    attended[0] = joined
+    for slot in range(STEP):
+        rows = slice(slot * SEQ, (slot + 1) * SEQ)
+        pairs = []
+        for pair in range(HEADS // 2):
+            span = slice(pair * 2 * HEAD, (pair + 1) * 2 * HEAD)
+            probs = softmax_keys(right_product(keys[rows, span], both_heads(queries[rows, span], masks)))
+            pairs.append(merge_heads(left_product(probs.astype(BF16), heads_in[rows, span])).astype(BF16))
+        joined.append(jnp.concatenate(pairs, axis=1))
+    joined = joined[0] if STEP == 1 else jnp.concatenate(joined, axis=0)
+    attended[...] = joined.reshape(STEP, SEQ, D)
     proj = dot_nn(joined, right[:, 2 * D : 3 * D]) + bias[:, 8 * D : 9 * D]
-    projected[0] = proj
-    mid = values + mod_part(mod, slot, 2) * proj
-    middle[0] = mid
+    projected[...] = proj.reshape(STEP, SEQ, D)
+    mid = values + mod_part(mod, step, 2) * proj
+    middle[...] = mid.reshape(STEP, SEQ, D)
     normed, _ = norm_stats(mid)
-    normed = (normed * (1.0 + mod_part(mod, slot, 4)) + mod_part(mod, slot, 3)).astype(BF16)
-    pre = dot_nn(normed, right[:, 3 * D :]) + bias[:, 9 * D : 9 * D + FF]
-    pre_act[0] = pre
-    act = (0.5 * pre * (1.0 + gelu_parts(pre))).astype(BF16)
-    ffn = dot_nn(act, down[...]) + bias[:, 9 * D + FF :]
-    branch[0] = ffn
-    result = mid + mod_part(mod, slot, 5) * ffn
+    normed = (normed * (1.0 + mod_part(mod, step, 4)) + mod_part(mod, step, 3)).astype(BF16)
+    ffn = bias[:, 9 * D + FF :]
+    for start in range(0, FF, CHUNK):
+        stop = start + CHUNK
+        pre = dot_nn(normed, right[:, 3 * D + start : 3 * D + stop]) + bias[:, 9 * D + start : 9 * D + stop]
+        act, rate = gelu_and_slope(pre)
+        act = act.astype(BF16)
+        active[:, :, start:stop] = act.reshape(STEP, SEQ, CHUNK)
+        slope[:, :, start:stop] = rate.reshape(STEP, SEQ, CHUNK)
+        ffn = ffn + dot_nn(act, down[start:stop, :])
+    branch[...] = ffn.reshape(STEP, SEQ, D)
+    result = mid + mod_part(mod, step, 5) * ffn
     if last:
-        result = result * jnp.where(slot < counts[0], 1.0, 0.0)
-    out[0] = result
+        result = result * occupied(counts, step)
+    out[...] = result.reshape(STEP, SEQ, D)
 
 
 def per_slot(width):
-    return pl.BlockSpec((1, SEQ, width), lambda slot: (slot, 0, 0))
+    return pl.BlockSpec((STEP, SEQ, width), lambda step: (step, 0, 0))
 
 
 def whole(*shape):
-    return pl.BlockSpec(shape, lambda slot: (0,) * len(shape))
+    return pl.BlockSpec(shape, lambda step: (0,) * len(shape))
 
 
 def tokens(width, dtype):
@@ -522,7 +588,7 @@
     left, right, down, bias = weights
     return pl.pallas_call(
         functools.partial(forward_kernel, last=last),
-        grid=(SLOT,),
+        grid=(SLOT // STEP,),
         out_shape=(
             tokens(D, F32),
             jax.ShapeDtypeStruct((SLOT, 6 * D), F32),
@@ -530,6 +596,7 @@
             tokens(D, BF16),
             tokens(D, F32),
             tokens(D, F32),
+            tokens(FF, BF16),
             tokens(FF, F32),
             tokens(D, F32),
         ),
@@ -550,6 +617,7 @@
             per_slot(D),
             per_slot(D),
             per_slot(FF),
+            per_slot(FF),
             per_slot(D),
         ),
         compiler_params=params_of(1),
@@ -564,76 +632,76 @@
     return rstd * (inner - jnp.mean(inner, axis=-1, keepdims=True) - normed * along)
 
 
-def row_sum(values):
-    return jnp.sum(values, axis=0, keepdims=True)
-
-
-def ffn_kernel(chips, core, counts, upstream, branch, pre_act, middle, mod, right, down, d_middle, d_mod, bias, wire, acc_up, acc_down, *, last):
-    slot = pl.program_id(0)
-
-    @pl.when(slot == 0)
+def ffn_kernel(chips, core, counts, upstream, branch, active, slope, middle, mod, right, down, d_middle, d_mod, bias, keep, send, acc_up, acc_down, *, last):
+    step = pl.program_id(0)
+
+    @pl.when(step == 0)
     def _():
         acc_up[...] = jnp.zeros_like(acc_up)
         acc_down[...] = jnp.zeros_like(acc_down)
         bias[...] = jnp.zeros_like(bias)
         d_mod[...] = jnp.zeros_like(d_mod)
 
-    up = upstream[0].astype(F32)
+    up = flat(upstream).astype(F32)
     if last:
-        up = up * jnp.where(slot < counts[0], 1.0, 0.0)
-    d_branch = up * mod_part(mod, slot, 5)
-    d_mod[pl.ds(20 + slot, 1), :] = row_sum(up * branch[0])
+        up = up * occupied(counts, step)
+    d_branch = up * mod_part(mod, step, 5)
+    put_sums(d_mod, step, 5, up * flat(branch))
     bias[:, FF:] += row_sum(d_branch)
     low = d_branch.astype(BF16)
-    pre = pre_act[0]
-    curve = gelu_parts(pre)
-    act = (0.5 * pre * (1.0 + curve)).astype(BF16)
-    acc_down[...] += left_product(act, low)
-    slope = 0.5 * (1.0 + curve) + (0.5 * 0.7978845608028654) * pre * (1.0 - curve * curve) * (
-        1.0 + (3 * 0.044715) * (pre * pre)
-    )
-    d_pre = right_product(low, down[...]) * slope
-    bias[:, :FF] += row_sum(d_pre)
-    low = d_pre.astype(BF16)
-    normed, rstd = norm_stats(middle[0])
-    scale = mod_part(mod, slot, 4)
-    shifted = (normed * (1.0 + scale) + mod_part(mod, slot, 3)).astype(BF16)
-    acc_up[...] += left_product(shifted, low)
-    d_normed = right_product(low, right[:, 3 * D :])
-    d_mod[pl.ds(12 + slot, 1), :] = row_sum(d_normed)
-    d_mod[pl.ds(16 + slot, 1), :] = row_sum(d_normed * normed)
-    d_middle[0] = up + norm_backward(d_normed, normed, rstd, scale)
-
-    @pl.when(slot == SLOT - 1)
+    normed, rstd = norm_stats(flat(middle))
+    scale = mod_part(mod, step, 4)
+    shifted = (normed * (1.0 + scale) + mod_part(mod, step, 3)).astype(BF16)
+    d_normed = 0.0
+    for start in range(0, FF, CHUNK):
+        stop = start + CHUNK
+        d_pre = right_product(low, down[start:stop, :]) * slope[:, :, start:stop].reshape(STEP * SEQ, CHUNK)
+        acc_down[start:stop, :] += left_product(active[:, :, start:stop].reshape(STEP * SEQ, CHUNK), low)
+        bias[:, start:stop] += row_sum(d_pre)
+        low_pre = d_pre.astype(BF16)
+        acc_up[:, start:stop] += left_product(shifted, low_pre)
+        d_normed = d_normed + right_product(low_pre, right[:, 3 * D + start : 3 * D + stop])
+    put_sums(d_mod, step, 3, d_normed)
+    put_sums(d_mod, step, 4, d_normed * normed)
+    d_middle[...] = (up + norm_backward(d_normed, normed, rstd, scale)).reshape(STEP, SEQ, D)
+
+    @pl.when(step == SLOT // STEP - 1)
     def _():
         rows = D // chips
+        is_odd = core[0] == 1
         for chip in range(chips):
-            for half in range(2):
-                side = (half + core[0]) % 2
-                wire[side, chip, :, : 2 * D] = acc_up[rows * chip : rows * (chip + 1), 2 * D * half : 2 * D * (half + 1)].astype(BF16)
-                for part in range(2):
-                    start = rows * (4 * chip + 2 * half + part)
-                    wire[side, chip, :, (2 + part) * D : (3 + part) * D] = acc_down[start : start + rows, :].astype(BF16)
+            span = slice(rows * chip, rows * (chip + 1))
+            even, odd = acc_up[span, : 2 * D], acc_up[span, 2 * D :]
+            keep[chip, :, : 2 * D] = jnp.where(is_odd, odd, even).astype(BF16)
+            send[chip, :, : 2 * D] = jnp.where(is_odd, even, odd).astype(BF16)
+            for part in range(2):
+                start = rows * (4 * chip + part)
+                even = acc_down[start : start + rows, :]
+                odd = acc_down[start + 2 * rows : start + 3 * rows, :]
+                keep[chip, :, (2 + part) * D : (3 + part) * D] = jnp.where(is_odd, odd, even).astype(BF16)
+                send[chip, :, (2 + part) * D : (3 + part) * D] = jnp.where(is_odd, even, odd).astype(BF16)
 
 
 def ffn_backward(core, counts, upstream, record, weights, chips, last):
-    _, mod, _, _, _, middle, pre_act, branch = record
+    _, mod, _, _, _, middle, active, slope, branch = record
     _, right, down, _ = weights
     rows = D // chips
     return pl.pallas_call(
         functools.partial(ffn_kernel, chips, last=last),
-        grid=(SLOT,),
+        grid=(SLOT // STEP,),
         out_shape=(
             tokens(D, F32),
             jax.ShapeDtypeStruct((24, D), F32),
             jax.ShapeDtypeStruct((1, FF + D), F32),
-            jax.ShapeDtypeStruct((2, chips, rows, 4 * D), BF16),
+            jax.ShapeDtypeStruct((chips, rows, 4 * D), BF16),
+            jax.ShapeDtypeStruct((chips, rows, 4 * D), BF16),
         ),
         in_specs=[
             SMEM,
             SMEM,
             per_slot(D),
             per_slot(D),
+            per_slot(FF),
             per_slot(FF),
             per_slot(D),
             whole(SLOT, 6 * D),
@@ -644,65 +712,72 @@
             per_slot(D),
             whole(24, D),
             whole(1, FF + D),
-            whole(2, chips, rows, 4 * D),
+            whole(chips, rows, 4 * D),
+            whole(chips, rows, 4 * D),
         ),
         scratch_shapes=[pltpu.VMEM((D, FF), F32), pltpu.VMEM((FF, D), F32)],
         compiler_params=params_of(1),
         cost_estimate=cost(8 * 10**9, 20 * 2**20),
         name="ffn_backward",
-    )(core, counts, upstream, branch, pre_act, middle, mod, right, down)
-
-
-def attention_kernel(chips, core, d_middle, hidden, qkv, attended, projected, mod, left, right, d_mod_in, bias_in, cond, d_cond_in, d_hidden, d_cond, wire, acc, acc_proj, d_mod, bias, *, first):
-    slot = pl.program_id(0)
-
-    @pl.when(slot == 0)
+    )(core, counts, upstream, branch, active, slope, middle, mod, right, down)
+
+
+def attention_kernel(chips, core, d_middle, hidden, qkv, attended, projected, mod, left, right, d_mod_in, bias_in, cond, d_cond_in, d_hidden, d_cond, keep, send, acc, acc_proj, d_mod, bias, *, first):
+    step = pl.program_id(0)
+
+    @pl.when(step == 0)
     def _():
         acc[...] = jnp.zeros_like(acc)
         acc_proj[...] = jnp.zeros_like(acc_proj)
         bias[...] = jnp.zeros_like(bias)
         d_mod[...] = d_mod_in[...]
 
-    d_mid = d_middle[0]
-    d_proj = d_mid * mod_part(mod, slot, 2)
-    d_mod[pl.ds(8 + slot, 1), :] = row_sum(d_mid * projected[0])
+    d_mid = flat(d_middle)
+    d_proj = d_mid * mod_part(mod, step, 2)
+    put_sums(d_mod, step, 2, d_mid * flat(projected))
     bias[:, 8 * D : 9 * D] += row_sum(d_proj)
     low = d_proj.astype(BF16)
-    acc_proj[...] += left_product(attended[0], low)
+    acc_proj[...] += left_product(flat(attended), low)
     d_heads = right_product(low, right[:, 2 * D : 3 * D]).astype(BF16)
     factor = 1.0 / math.sqrt(HEAD)
-    scaled = qkv[0, :, :D] * jnp.asarray(factor, BF16)
-    keys = qkv[0, :, D : 2 * D]
-    heads_in = qkv[0, :, 2 * D :]
-    d_query, d_keys, d_values = [], [], []
-    for head in range(HEADS):
-        span = slice(head * HEAD, (head + 1) * HEAD)
-        scores = right_product(keys[:, span], scaled[:, span])
-        raised = jnp.exp(scores - jnp.max(scores, axis=0, keepdims=True))
-        probs = raised * (1.0 / jnp.sum(raised, axis=0, keepdims=True))
-        d_probs = right_product(heads_in[:, span], d_heads[:, span])
-        d_values.append(dot_nn(probs.astype(BF16), d_heads[:, span]))
-        weighted = probs * d_probs
-        d_scores = (weighted - probs * jnp.sum(weighted, axis=0, keepdims=True)).astype(BF16)
-        d_keys.append(dot_nn(d_scores, scaled[:, span]))
-        d_query.append(left_product(d_scores, keys[:, span]) * factor)
-    d_query = jnp.concatenate(d_query, axis=1)
-    d_values = jnp.concatenate(d_values, axis=1)
-    bias[:, 6 * D : 7 * D] += row_sum(d_query)
-    bias[:, 7 * D : 8 * D] += row_sum(d_values)
-    mixed = jnp.concatenate(
-        [d_query.astype(BF16), jnp.concatenate(d_keys, axis=1).astype(BF16), d_values.astype(BF16)], axis=1
-    )
-    normed, rstd = norm_stats(hidden[0].astype(F32))
-    scale = mod_part(mod, slot, 1)
-    shifted = (normed * (1.0 + scale) + mod_part(mod, slot, 0)).astype(BF16)
+    masks, plain = head_masks(factor), head_masks(1.0)
+    mixed = []
+    for slot in range(STEP):
+        rows = slice(slot * SEQ, (slot + 1) * SEQ)
+        d_query, d_keys, d_values = [], [], []
+        for pair in range(HEADS // 2):
+            span = slice(pair * 2 * HEAD, (pair + 1) * 2 * HEAD)
+            queries = both_heads(qkv[slot, :, span], masks)
+            keys = qkv[slot, :, D + pair * 2 * HEAD : D + (pair + 1) * 2 * HEAD]
+            heads_in = qkv[slot, :, 2 * D + pair * 2 * HEAD : 2 * D + (pair + 1) * 2 * HEAD]
+            d_pair = both_heads(d_heads[rows, span], plain)
+            probs = softmax_keys(right_product(keys, queries))
+            d_probs = right_product(heads_in, d_pair)
+            d_values.append(dot_nn(probs.astype(BF16), d_pair))
+            weighted = probs * d_probs
+            d_scores = (weighted - probs * jnp.sum(weighted, axis=0, keepdims=True)).astype(BF16)
+            d_keys.append(dot_nn(d_scores, queries))
+            d_query.append(merge_heads(left_product(d_scores, keys)) * factor)
+        d_query = jnp.concatenate(d_query, axis=1)
+        d_values = jnp.concatenate(d_values, axis=1)
+        bias[:, 6 * D : 7 * D] += row_sum(d_query)
+        bias[:, 7 * D : 8 * D] += row_sum(d_values)
+        mixed.append(
+            jnp.concatenate(
+                [d_query.astype(BF16), jnp.concatenate(d_keys, axis=1).astype(BF16), d_values.astype(BF16)], axis=1
+            )
+        )
+    mixed = mixed[0] if STEP == 1 else jnp.concatenate(mixed, axis=0)
+    normed, rstd = norm_stats(flat(hidden).astype(F32))
+    scale = mod_part(mod, step, 1)
+    shifted = (normed * (1.0 + scale) + mod_part(mod, step, 0)).astype(BF16)
     acc[...] += left_product(shifted, mixed)
     d_normed = right_product(mixed[:, :D], left[:, 6 * D :]) + right_product(mixed[:, D:], right[:, : 2 * D])
-    d_mod[pl.ds(slot, 1), :] = row_sum(d_normed)
-    d_mod[pl.ds(4 + slot, 1), :] = row_sum(d_normed * normed)
-    d_hidden[0] = d_mid + norm_backward(d_normed, normed, rstd, scale)
-
-    @pl.when(slot == SLOT - 1)
+    put_sums(d_mod, step, 0, d_normed)
+    put_sums(d_mod, step, 1, d_normed * normed)
+    d_hidden[...] = (d_mid + norm_backward(d_normed, normed, rstd, scale)).reshape(STEP, SEQ, D)
+
+    @pl.when(step == SLOT // STEP - 1)
     def _():
         rows = D // chips
         bias[:, 9 * D :] = bias_in[...]
@@ -717,11 +792,12 @@
             total = total * (gate * (1.0 + wide_cond * (1.0 - gate)))
         d_cond[...] = total
         low_mod = d_mod[...].astype(BF16)
+        is_odd = core[0] == 1
         for chip in range(chips):
             span = slice(rows * chip, rows * (chip + 1))
-            wire[core[0], chip, :, : 2 * D] = acc[span, : 2 * D].astype(BF16)
-            wire[1 - core[0], chip, :, :D] = acc[span, 2 * D :].astype(BF16)
-            wire[1 - core[0], chip, :, D : 2 * D] = acc_proj[span, :].astype(BF16)
+            even = acc[span, : 2 * D]
+            odd = jnp.concatenate([acc[span, 2 * D :], acc_proj[span, :]], axis=1)
+            tails = []
             for half in range(2):
                 pieces = []
                 for part in range(2):
@@ -731,22 +807,27 @@
                     else:
                         pieces.append(jnp.zeros((1, 128), F32))
                 pieces.append(jnp.zeros((rows - 2, 128), F32))
-                side = (half + core[0]) % 2
-                wire[side, chip, :, 2 * D : 2 * D + 128] = jnp.concatenate(pieces, axis=0).astype(BF16)
-                wire[side, chip, :, 2 * D + 128 :] = low_mod
+                tails.append(jnp.concatenate(pieces, axis=0))
+            keep[chip, :, : 2 * D] = jnp.where(is_odd, odd, even).astype(BF16)
+            send[chip, :, : 2 * D] = jnp.where(is_odd, even, odd).astype(BF16)
+            keep[chip, :, 2 * D : 2 * D + 128] = jnp.where(is_odd, tails[1], tails[0]).astype(BF16)
+            send[chip, :, 2 * D : 2 * D + 128] = jnp.where(is_odd, tails[0], tails[1]).astype(BF16)
+            keep[chip, :, 2 * D + 128 :] = low_mod
+            send[chip, :, 2 * D + 128 :] = jnp.zeros_like(low_mod)
 
 
 def attention_backward(core, d_middle, hidden, record, weights, d_mod, bias, cond, d_cond, chips, first):
-    _, mod, qkv, attended, projected, _, _, _ = record
+    _, mod, qkv, attended, projected, *_ = record
     left, right, _, _ = weights
     rows = D // chips
     return pl.pallas_call(
         functools.partial(attention_kernel, chips, first=first),
-        grid=(SLOT,),
+        grid=(SLOT // STEP,),
         out_shape=(
             tokens(D, F32),
             jax.ShapeDtypeStruct((SLOT, D), F32),
-            jax.ShapeDtypeStruct((2, chips, rows, 3 * D + 128), BF16),
+            jax.ShapeDtypeStruct((chips, rows, 3 * D + 128), BF16),
+            jax.ShapeDtypeStruct((chips, rows, 3 * D + 128), BF16),
         ),
         in_specs=[
             SMEM,
@@ -766,7 +847,8 @@
         out_specs=(
             per_slot(D),
             whole(SLOT, D),
-            whole(2, chips, rows, 3 * D + 128),
+            whole(chips, rows, 3 * D + 128),
+            whole(chips, rows, 3 * D + 128),
         ),
         scratch_shapes=[
             pltpu.VMEM((D, 3 * D), F32),
@@ -862,65 +944,65 @@
     def stacked(copies):
         return lax.all_to_all(copies, "fsdp", 0, 0, axis_index_groups=lines, tiled=True)
 
-    def spread_out(stack):
-        low, high = stack[:2], stack[2:]
-        low_x, high_y = along(low, 2), along(high, 4)
-        low_y, high_x = along(low, 4), along(high, 2)
-        return low, high, low_x, high_x, low_y, high_y
-
-    def spread_more(held):
-        low_x, high_y = held[2], held[5]
-        held = (*held, along(low_x, 4), along(high_y, 2))
-        return (*held, *[along(value, 1) for value in held])
-
-    copies_first, copies_last = pack(
+    def with_other_core(held):
+        return [*held, *[(along(block, 1), (1, *spot[1:])) for block, spot in held]]
+
+    def planes_of(stack, column):
+        return [(stack if step == 0 else along(stack, 2 * step), (0, step, 0, column)) for step in range(4)]
+
+    copies_left, copies_right, copies_last = pack(
         ada_weight, qkv_weight, proj_weight, fc1_weight, fc2_weight, biases, condition, rows, 4
     )
-    stack_first = stacked(copies_first)
-    stack_first, copies_last = tie((stack_first, copies_last))
+    stack_left, copies_right = tie((stacked(copies_left), copies_right))
+    blocks, stack_right, copies_last = tie(
+        ([block for block, _ in planes_of(stack_left, 0)], stacked(copies_right), copies_last)
+    )
+    planes_left = [(block, (0, step, 0, 0)) for step, block in enumerate(blocks)]
+    planes_right = planes_of(stack_right, WIRE // 2)
     stack_last = stacked(copies_last)
-    *first_weights, cond_all = unpack_wire(place, spread_more(spread_out(stack_first)))
-    held_last = spread_out(stack_last)
+    held_first = [*with_other_core(planes_left), *with_other_core(planes_right)]
+    stack_last, place = tie((stack_last, place))
+    *first_weights, cond_all = unpack_wire(place, held_first)
+    planes_last = planes_of(stack_last, 0)
     first = forward_block(counts, latents_in, condition, first_weights, False)
-    held_last, first = tie((held_last, first))
-    *last_weights, _ = unpack_wire(place, spread_more(held_last))
+    blocks, first = tie(([block for block, _ in planes_last], first))
+    held_last = with_other_core([(block, spot) for block, (_, spot) in zip(blocks, planes_last, strict=True)])
+    *last_weights, _ = unpack_wire(place, held_last)
     last = forward_block(counts, first[0], condition, last_weights, True)
     weights, records, hidden = [first_weights, last_weights], [first, last], [latents_in, first[0], last[0]]
     upstream = cotangent
     d_cond = jnp.zeros((SLOT, D), F32)
     reduced = [None, None]
 
-    def paired(wire, width):
-        got = lax.ppermute(wire[1], "fsdp", swap)
-        both = (wire[0].astype(F32) + got.astype(F32))[:, :, :width].astype(BF16)
-        if width < wire.shape[-1]:
-            both = jnp.concatenate([both, wire[0, :, :, width:]], axis=2)
-        return both
-
-    def summed(both, width):
-        spread = lax.all_to_all(both, "fsdp", 0, 0, axis_index_groups=across, tiled=True)
-        return jnp.sum(spread[:, :, :width].astype(F32), axis=0), spread[:, :, width:]
-
-    d_middle, d_mod, bias, wire = ffn_backward(core, counts, upstream, records[1], weights[1], chips, True)
-    d_middle, both = tie((d_middle, paired(wire, 4 * D)))
-    ffn_last, _ = summed(both, 4 * D)
-    upstream, d_cond, wire = attention_backward(
+    def paired(keep, send):
+        got = lax.ppermute(send, "fsdp", swap)
+        return (keep.astype(F32) + got.astype(F32)).astype(BF16)
+
+    def exchanged(both):
+        return lax.all_to_all(both, "fsdp", 0, 0, axis_index_groups=across, tiled=True)
+
+    def summed(spread):
+        return jnp.sum(spread.astype(F32), axis=0)
+
+    d_middle, d_mod, bias, *wire = ffn_backward(core, counts, upstream, records[1], weights[1], chips, True)
+    d_middle, both = tie((d_middle, paired(*wire)))
+    ffn_last = exchanged(both)
+    upstream, d_cond, *wire = attention_backward(
         core, d_middle, hidden[1], records[1], weights[1], d_mod, bias, condition, d_cond, chips, False
     )
-    wire, ffn_last = tie((wire, ffn_last))
-    upstream, both = tie((upstream, paired(wire, 2 * D + 128)))
-    attn_last, mods_last = summed(both, 2 * D + 128)
-    d_middle, d_mod, bias, wire = ffn_backward(core, counts, upstream, records[0], weights[0], chips, False)
-    wire, attn_last, mods_last = tie((wire, attn_last, mods_last))
-    d_middle, both = tie((d_middle, paired(wire, 4 * D)))
-    ffn_first, _ = summed(both, 4 * D)
-    upstream, d_cond, wire = attention_backward(
+    upstream, both, ffn_last = tie((upstream, paired(*wire), ffn_last))
+    attn_last = exchanged(both)
+    d_middle, d_mod, bias, *wire = ffn_backward(core, counts, upstream, records[0], weights[0], chips, False)
+    d_middle, both, attn_last = tie((d_middle, paired(*wire), attn_last))
+    ffn_first = exchanged(both)
+    upstream, d_cond, *wire = attention_backward(
         core, d_middle, hidden[0], records[0], weights[0], d_mod, bias, condition, d_cond, chips, True
     )
-    wire, ffn_first = tie((wire, ffn_first))
-    attn_first, mods_first = summed(paired(wire, 2 * D + 128), 2 * D + 128)
-    reduced[0] = (ffn_first, attn_first, mods_first.reshape(24 * chips, D))
-    reduced[1] = (ffn_last, attn_last, mods_last.reshape(24 * chips, D))
+    both, ffn_first = tie((paired(*wire), ffn_first))
+    attn_first = exchanged(both)
+    width = 2 * D + 128
+    for layer, (ffn, attn) in enumerate(((ffn_first, attn_first), (ffn_last, attn_last))):
+        reduced[layer] = (summed(ffn), summed(attn[:, :, :width]), attn[:, :, width:].reshape(24 * chips, D))
     own_ffn = jnp.stack([reduced[layer][0] for layer in range(2)])
     own_attn = jnp.stack([reduced[layer][1] for layer in range(2)])
     own_mod = jnp.stack([reduced[layer][2] for layer in range(2)])

time: 310 us -> 271 us (0.87)
  Pallas kernels: 124 us -> 89.2 us
  local copies, waits for them, and re-layouts: 22.8 us -> 41.2 us
  waiting for transfers between devices: 79.5 us -> 63.7 us
  blocking collectives: 24.1 us -> 17 us
    unnamed x54 -> x96, local copies, waits for them, and re-layouts: 12.5 us -> 40.2 us
    all_to_all x4, waiting for transfers between devices: 43.1 us -> 21.4 us  [exchanged(): lax.all_to_all(both, 'fsdp', 0, 0, axis_index_groups=across, tiled=True)]
    pallas_call x2, Pallas kernels: 40.5 us -> 25.8 us  [attention_backward(): pl.pallas_call(functools.partial(attention_kernel, chips, first=first), g...]
    pallas_call x2, Pallas kernels: 30.6 us -> 19.6 us  [ffn_backward(): pl.pallas_call(functools.partial(ffn_kernel, chips, last=last), grid=(SLO...]
    pallas_call x5, Pallas kernels: 51.1 us -> 41.5 us  [the longest x2 31.6 us: forward_block(): pl.pallas_call(functools.partial(forward_kernel, last=last), grid=(SLOT /...]
    squeeze x6 -> x0, local copies, waits for them, and re-layouts: 8.08 us -> none  [the longest x4 6.1 us: paired(): got = lax.ppermute(wire[1], 'fsdp', swap)]
    all_to_all x1, blocking collectives: 24.1 us -> 17 us  [stacked(): lax.all_to_all(copies, 'fsdp', 0, 0, axis_index_groups=lines, tiled=True)]
    all_to_all x1 -> x2, starting transfers between devices: 4.18 us -> 8.17 us  [stacked(): lax.all_to_all(copies, 'fsdp', 0, 0, axis_index_groups=lines, tiled=True)]
  transfers between devices with their start and end apart: 39 -> 33, of which waited for: 20 -> 18; matrix products, arithmetic and copies ran while one was open for 1% -> 3% of each run, Pallas kernels for 26% -> 20%
where the time goes in v3:
time: 271 us; the launch traced here: 269 us
  Pallas kernels  89.2 us (33%)
  waiting for transfers between devices  63.7 us (24%)
  starting transfers between devices  47 us (17%)
  local copies, waits for them, and re-layouts  41.2 us (15%)
  blocking collectives  17 us (6%)
  other arithmetic  9.56 us (4%)
    unnamed x96, local copies, waits for them, and re-layouts  40.2 us
    pallas_call x2, Pallas kernels, forward_block(): pl.pallas_call(functools.partial(forward_kernel, last=last), grid=(SLOT /...  31.6 us
    ppermute x21, waiting for transfers between devices, along(): lax.ppermute(value, 'fsdp', [(one, one ^ bit) for one in range(devices)])  30.1 us
    pallas_call x2, Pallas kernels, attention_backward(): pl.pallas_call(functools.partial(attention_kernel, chips, first=first), g...  25.8 us
    all_to_all x4, starting transfers between devices, exchanged(): lax.all_to_all(both, 'fsdp', 0, 0, axis_index_groups=across, tiled=True)  24.9 us
    all_to_all x4, waiting for transfers between devices, exchanged(): lax.all_to_all(both, 'fsdp', 0, 0, axis_index_groups=across, tiled=True)  21.4 us
    pallas_call x2, Pallas kernels, ffn_backward(): pl.pallas_call(functools.partial(ffn_kernel, chips, last=last), grid=(SLO...  19.6 us
    all_to_all x1, blocking collectives, stacked(): lax.all_to_all(copies, 'fsdp', 0, 0, axis_index_groups=lines, tiled=True)  17 us
  transfers between devices with their start and end apart: 33, of which 18 were waited for; matrix products, arithmetic and copies ran while one was open for 3% of the time, Pallas kernels for 20%

profile of v3, /device:TPU:0, one launch (start us, length us, event | category | flops | bytes accessed | tf_op | source)
XLA Modules:
  0.0 269.4 jit_solution(7811752761398892819)
XLA Ops:
  0.6 2.9 %pack.1 = (bf16[4,24,1792]{2,1,0:T(8,128)(2,1)}, bf16[4,24,1792]{2,1,0:T(8,128)(2,1)}, bf16[4,24,3584]{2,1,0:T(8,128)(2,1)}) custom-call(bf16[2,27648]{1,0:T(2,128)(2,1)} %ada_in.1, bf16[2,13824]{1,0:T(2,128)(2,1)} %qkv_in.1, bf16[2,4608]{1,0:T(2,128)(2,1)} %proj_in.1, bf16[2,18432]{1,0:T(2,128)(2,1)} %fc1_in.1, bf16[2,18432]{1,0:T(2,128)(2,1)} %fc2_in.1, ...), custom_call_target="tpu_custom_call" | custom-call | tf_op jit(solution)/shard_map/pack/pallas_call | solution.py:380
  3.6 17.0 %all_to_all.35.refs_0_ = bf16[4,24,1792]{2,1,0:T(8,128)(2,1)S(1)} all-to-all(bf16[4,24,1792]{2,1,0:T(8,128)(2,1)} %get-tuple-element.96), channel_id=1, replica_groups={{0,8,16,24},{1,9,17,25},{2,10,18,26},{3,11,19,27},{4,12,20,28},{5,13,21..., dimensions={0} | all-to-all | bytes 688128 | tf_op jit(solution)/shard_map/all_to_all | solution.py:945
  20.5 3.5 %all-to-all-start.1 = ((bf16[4,24,1792]{2,1,0:T(8,128)(2,1)}), bf16[4,24,1792]{2,1,0:T(8,128)(2,1)S(1)}, u32[]{:S(2)}, u32[]{:S(2)}) async-start(bf16[4,24,1792]{2,1,0:T(8,128)(2,1)} %get-tuple-element.99), calls=%async_computation.1 | async-start | bytes 688128 | tf_op jit(solution)/shard_map/all_to_all | solution.py:945
  27.6 7.5 %collective-permute-done.refs_1_ = bf16[4,24,1792]{2,1,0:T(8,128)(2,1)S(1)} collective-permute-done((bf16[4,24,1792]{2,1,0:T(8,128)(2,1)S(1)}, bf16[4,24,1792]{2,1,0:T(8,128)(2,1)S(1)}, u32[]{:S(2)}, u32[]{:S(2)}) %collective-permute-start) | collective-permute-done | bytes 344096 | tf_op jit(solution)/shard_map/ppermute | solution.py:942
  35.1 6.3 %collective-permute-done.1.refs_2_ = bf16[4,24,1792]{2,1,0:T(8,128)(2,1)S(1)} collective-permute-done((bf16[4,24,1792]{2,1,0:T(8,128)(2,1)S(1)}, bf16[4,24,1792]{2,1,0:T(8,128)(2,1)S(1)}, u32[]{:S(2)}, u32[]{:S(2)}) %collective-permute-start.1) | collective-permute-done | bytes 344096 | tf_op jit(solution)/shard_map/ppermute | solution.py:942
  41.4 4.7 %all-to-all-start.2 = ((bf16[4,24,3584]{2,1,0:T(8,128)(2,1)}), bf16[4,24,3584]{2,1,0:T(8,128)(2,1)S(1)}, u32[]{:S(2)}, u32[]{:S(2)}) async-start(bf16[4,24,3584]{2,1,0:T(8,128)(2,1)} %get-tuple-element.101), calls=%async_computation.2 | async-start | bytes 1376256 | tf_op jit(solution)/shard_map/all_to_all | solution.py:945
  50.1 6.7 %collective-permute-done.10.refs_9_ = bf16[4,24,1792]{2,1,0:T(8,128)(2,1)S(1)} collective-permute-done((bf16[4,24,1792]{2,1,0:T(8,128)(2,1)S(1)}, bf16[4,24,1792]{2,1,0:T(8,128)(2,1)S(1)}, u32[]{:S(2)}, u32[]{:S(2)}) %collective-permute-start.10) | collective-permute-done | bytes 344096 | tf_op jit(solution)/shard_map/ppermute | solution.py:942
  56.8 4.8 %collective-permute-done.11.refs_10_ = bf16[4,24,1792]{2,1,0:T(8,128)(2,1)S(1)} collective-permute-done((bf16[4,24,1792]{2,1,0:T(8,128)(2,1)S(1)}, bf16[4,24,1792]{2,1,0:T(8,128)(2,1)S(1)}, u32[]{:S(2)}, u32[]{:S(2)}) %collective-permute-start.11) | collective-permute-done | bytes 344096 | tf_op jit(solution)/shard_map/ppermute | solution.py:942
  72.1 3.1 %unpack.2 = (bf16[384,2688]{1,0:T(8,128)(2,1)S(1)}, bf16[384,2688]{1,0:T(8,128)(2,1)S(1)}, bf16[1536,384]{1,0:T(8,128)(2,1)S(1)}, f32[1,5376]{1,0:T(1,128)S(1)}, f32[2,64,384]{2,1,0:T(8,128)S(1)}) custom-call(s32[2]{0:T(128)S(1)} %pad_add_fusion.place, bf16[4,24,1792]{2,1,0:T(8,128)(2,1)S(1)} %all_to_all.35.refs_0_, ...), custom_call_target="tpu_custom_call" | custom-call | tf_op jit(solution)/shard_map/unpack/pallas_call | solution.py:438
  75.8 15.7 %forward_block.2 = (f32[4,256,384]{2,1,0:T(8,128)S(1)}, f32[4,2304]{1,0:T(4,128)S(1)}, bf16[4,256,1152]{2,1,0:T(8,128)(2,1)S(1)}, bf16[4,256,384]{2,1,0:T(8,128)...) custom-call(s32[1]{0:T(128)S(6)} %copy.19.counts, ...), custom_call_target="tpu_custom_call" | custom-call | flops 5000000000 | bytes 20971520 | tf_op jit(solution)/shard_map/forward_block/pallas_call | solution.py:589
  103.0 3.9 %unpack.3 = (bf16[384,2688]{1,0:T(8,128)(2,1)S(1)}, bf16[384,2688]{1,0:T(8,128)(2,1)S(1)}, bf16[1536,384]{1,0:T(8,128)(2,1)S(1)}, f32[1,5376]{1,0:T(1,128)S(1)}, f32[2,64,384]{2,1,0:T(8,128)}) custom-call(s32[2]{0:T(128)S(1)} %pad_add_fusion.place, bf16[4,24,3584]{2,1,0:T(8,128)(2,1)S(1)} %all-to-all-done.2.refs_0_, ...), custom_call_target="tpu_custom_call" | custom-call | tf_op jit(solution)/shard_map/unpack/pallas_call | solution.py:438
  106.9 15.9 %forward_block.3 = (f32[4,256,384]{2,1,0:T(8,128)}, f32[4,2304]{1,0:T(4,128)S(1)}, bf16[4,256,1152]{2,1,0:T(8,128)(2,1)S(1)}, bf16[4,256,384]{2,1,0:T(8,128)(2,1...) custom-call(s32[1]{0:T(128)S(6)} %copy.19.counts, ...), custom_call_target="tpu_custom_call" | custom-call | flops 5000000000 | bytes 20971520 | tf_op jit(solution)/shard_map/forward_block/pallas_call | solution.py:589
  126.3 9.7 %ffn_backward.2 = (f32[4,256,384]{2,1,0:T(8,128)S(1)}, f32[24,384]{1,0:T(8,128)S(1)}, f32[1,1920]{1,0:T(1,128)S(1)}, bf16[16,24,1536]{2,1,0:T(8,128)(2,1)S(1)}, bf16[16,24,1536]{2,1,0:T(8,128)(2,1)S(1)}) custom-call(s32[1]{0:T(128)} %bitcast.core, s32[1]{0:T(128)S(6)} %copy.19.counts, bf16[4,256,384]{2,1,0:T(8,128)(2,1)S(1)} %copy-done.18, ...), custom_call_target="tpu_custom_call" | custom-call | flops 8000000000 | bytes 20971520 | tf_op jit(solution)/shard_map/ffn_backward/pallas_call | solution.py:689
  136.2 2.7 %collective-permute-done.21 = bf16[16,24,1536]{2,1,0:T(8,128)(2,1)S(1)} collective-permute-done((bf16[16,24,1536]{2,1,0:T(8,128)(2,1)S(1)}, bf16[16,24,1536]{2,1,0:T(8,128)(2,1)S(1)}, u32[]{:S(2)}, u32[]{:S(2)}) %collective-permute-start.21) | collective-permute-done | bytes 1179680 | tf_op jit(solution)/shard_map/ppermute | solution.py:978
  140.2 6.0 %all-to-all-start.3 = ((bf16[16,24,1536]{2,1,0:T(8,128)(2,1)}), bf16[16,24,1536]{2,1,0:T(8,128)(2,1)}, u32[]{:S(2)}, u32[]{:S(2)}) async-start(bf16[16,24,1536]{2,1,0:T(8,128)(2,1)} %add_convert_fusion.1), calls=%async_computation.3 | async-start | bytes 2359296 | tf_op jit(solution)/shard_map/all_to_all | solution.py:982
  154.8 12.5 %attention_backward.2 = (f32[4,256,384]{2,1,0:T(8,128)S(1)}, f32[4,384]{1,0:T(4,128)S(1)}, bf16[16,24,1280]{2,1,0:T(8,128)(2,1)S(1)}, bf16[16,24,1280]{2,1,0:T(8,128)(2,1)S(1)}) custom-call(s32[1]{0:T(128)} %bitcast.core, f32[4,256,384]{2,1,0:T(8,128)S(1)} %copy-done.35, f32[4,256,384]{2,1,0:T(8,128)S(1)} %copy-done.29, ...), custom_call_target="tpu_custom_call" | custom-call | flops 6000000000 | bytes 20971520 | tf_op jit(solution)/shard_map/attention_backward/pallas_call | solution.py:823
  168.5 2.6 collective-permute-done.22
  173.3 6.8 %all-to-all-start.4 = ((bf16[16,24,1280]{2,1,0:T(8,128)(2,1)}), bf16[16,24,1280]{2,1,0:T(8,128)(2,1)}, u32[]{:S(2)}, u32[]{:S(2)}) async-start(bf16[16,24,1280]{2,1,0:T(8,128)(2,1)} %add_convert_fusion.3), calls=%async_computation.4 | async-start | bytes 1966080 | tf_op jit(solution)/shard_map/all_to_all | solution.py:982
  186.3 9.9 %ffn_backward.3 = (f32[4,256,384]{2,1,0:T(8,128)S(1)}, f32[24,384]{1,0:T(8,128)S(1)}, f32[1,1920]{1,0:T(1,128)S(1)}, bf16[16,24,1536]{2,1,0:T(8,128)(2,1)S(1)}, bf16[16,24,1536]{2,1,0:T(8,128)(2,1)S(1)}) custom-call(s32[1]{0:T(128)} %bitcast.core, s32[1]{0:T(128)S(6)} %copy.19.counts, f32[4,256,384]{2,1,0:T(8,128)S(1)} %copy-done.31, ...), custom_call_target="tpu_custom_call" | custom-call | flops 8000000000 | bytes 20971520 | tf_op jit(solution)/shard_map/ffn_backward/pallas_call | solution.py:689
  197.4 2.8 %collective-permute-done.23 = bf16[16,24,1536]{2,1,0:T(8,128)(2,1)S(1)} collective-permute-done((bf16[16,24,1536]{2,1,0:T(8,128)(2,1)S(1)}, bf16[16,24,1536]{2,1,0:T(8,128)(2,1)S(1)}, u32[]{:S(2)}, u32[]{:S(2)}) %collective-permute-start.23) | collective-permute-done | bytes 1179680 | tf_op jit(solution)/shard_map/ppermute | solution.py:978
  203.0 5.8 %all-to-all-start.5 = ((bf16[16,24,1536]{2,1,0:T(8,128)(2,1)}), bf16[16,24,1536]{2,1,0:T(8,128)(2,1)}, u32[]{:S(2)}, u32[]{:S(2)}) async-start(bf16[16,24,1536]{2,1,0:T(8,128)(2,1)} %add_convert_fusion), calls=%async_computation.5 | async-start | bytes 2359296 | tf_op jit(solution)/shard_map/all_to_all | solution.py:982
  217.1 13.3 %attention_backward.3 = (f32[4,256,384]{2,1,0:T(8,128)}, f32[4,384]{1,0:T(4,128)}, bf16[16,24,1280]{2,1,0:T(8,128)(2,1)S(1)}, bf16[16,24,1280]{2,1,0:T(8,128)(2,1)S(1)}) custom-call(s32[1]{0:T(128)} %bitcast.core, f32[4,256,384]{2,1,0:T(8,128)S(1)} %copy-done.39, bf16[4,256,384]{2,1,0:T(8,128)(2,1)S(1)} %copy-done.20, bf16[4,256,1152]{2,1,0:T(8,128)(2,1)S(1)} %copy-done.26, ...), custom_call_target="tpu_custom_call" | custom-call | flops 6000000000 | bytes 20971520 | tf_op jit(solution)/shard_map/attention_backward/pallas_call | solution.py:823
  235.9 6.3 %all-to-all-start.6 = ((bf16[16,24,1280]{2,1,0:T(8,128)(2,1)}), bf16[16,24,1280]{2,1,0:T(8,128)(2,1)S(1)}, u32[]{:S(2)}, u32[]{:S(2)}) async-start(bf16[16,24,1280]{2,1,0:T(8,128)(2,1)} %add_convert_fusion.2), calls=%async_computation.6 | async-start | bytes 1966080 | tf_op jit(solution)/shard_map/all_to_all | solution.py:982
  247.3 17.3 %all-to-all-done.6 = bf16[16,24,1280]{2,1,0:T(8,128)(2,1)S(1)} async-done(((bf16[16,24,1280]{2,1,0:T(8,128)(2,1)}), bf16[16,24,1280]{2,1,0:T(8,128)(2,1)S(1)}, u32[]{:S(2)}, u32[]{:S(2)}) %all-to-all-start.6) | async-done | bytes 983072 | tf_op jit(solution)/shard_map/all_to_all | solution.py:982
  (167 shorter events, 80.0 us)
Async XLA Ops:
  20.5 20.8 %all-to-all-start.1 = ((bf16[4,24,1792]{2,1,0:T(8,128)(2,1)}), bf16[4,24,1792]{2,1,0:T(8,128)(2,1)S(1)}, u32[]{:S(2)}, u32[]{:S(2)}) async-start(bf16[4,24,1792]{2,1,0:T(8,128)(2,1)} %get-tuple-element.99), calls=%async_computation.1 | async-start | bytes 688128 | tf_op jit(solution)/shard_map/all_to_all | solution.py:945
  24.0 11.1 %collective-permute-start = (bf16[4,24,1792]{2,1,0:T(8,128)(2,1)S(1)}, bf16[4,24,1792]{2,1,0:T(8,128)(2,1)S(1)}, u32[]{:S(2)}, u32[]{:S(2)}) collective-permute-start(bf16[4,24,1792]{2,1,0:T(8,128)(2,1)S(1)} %all_to_all.35.refs_0_), channel_id=1, source_target_pairs={{0,2},{1,3},{2,0},{3,1},{4,6},{5,7},{6,4},{7,5},{8,10},{9,11},{10,... | collective-permute-start | bytes 1032200 | tf_op jit(solution)/shard_map/ppermute | solution.py:942
  25.6 15.8 %collective-permute-start.1 = (bf16[4,24,1792]{2,1,0:T(8,128)(2,1)S(1)}, bf16[4,24,1792]{2,1,0:T(8,128)(2,1)S(1)}, u32[]{:S(2)}, u32[]{:S(2)}) collective-permute-start(bf16[4,24,1792]{2,1,0:T(8,128)(2,1)S(1)} %all_to_all.35.refs_0_), channel_id=1, source_target_pairs={{0,4},{1,5},{2,6},{3,7},{4,0},{5,1},{6,2},{7,3},{8,12},{9,13},{10,... | collective-permute-start | bytes 1032200 | tf_op jit(solution)/shard_map/ppermute | solution.py:942
  27.1 14.3 %collective-permute-start.2 = (bf16[4,24,1792]{2,1,0:T(8,128)(2,1)S(1)}, bf16[4,24,1792]{2,1,0:T(8,128)(2,1)S(1)}, u32[]{:S(2)}, u32[]{:S(2)}) collective-permute-start(bf16[4,24,1792]{2,1,0:T(8,128)(2,1)S(1)} %all_to_all.35.refs_0_), channel_id=1, source_target_pairs={{0,6},{1,7},{2,4},{3,5},{4,2},{5,3},{6,0},{7,1},{8,14},{9,15},{10,... | collective-permute-start | bytes 1032200 | tf_op jit(solution)/shard_map/ppermute | solution.py:942
  41.4 23.6 %all-to-all-start.2 = ((bf16[4,24,3584]{2,1,0:T(8,128)(2,1)}), bf16[4,24,3584]{2,1,0:T(8,128)(2,1)S(1)}, u32[]{:S(2)}, u32[]{:S(2)}) async-start(bf16[4,24,3584]{2,1,0:T(8,128)(2,1)} %get-tuple-element.101), calls=%async_computation.2 | async-start | bytes 1376256 | tf_op jit(solution)/shard_map/all_to_all | solution.py:945
  46.1 10.7 %collective-permute-start.10 = (bf16[4,24,1792]{2,1,0:T(8,128)(2,1)S(1)}, bf16[4,24,1792]{2,1,0:T(8,128)(2,1)S(1)}, u32[]{:S(2)}, u32[]{:S(2)}) collective-permute-start(bf16[4,24,1792]{2,1,0:T(8,128)(2,1)S(1)} %all-to-all-done.1.refs_8_), channel_id=1, source_target_pairs={{0,2},{1,3},{2,0},{3,1},{4,6},{5,7},{6,4},{7,5},{8,10},{9,11},{10,... | collective-permute-start | bytes 1032200 | tf_op jit(solution)/shard_map/ppermute | solution.py:942
  47.3 14.3 %collective-permute-start.11 = (bf16[4,24,1792]{2,1,0:T(8,128)(2,1)S(1)}, bf16[4,24,1792]{2,1,0:T(8,128)(2,1)S(1)}, u32[]{:S(2)}, u32[]{:S(2)}) collective-permute-start(bf16[4,24,1792]{2,1,0:T(8,128)(2,1)S(1)} %all-to-all-done.1.refs_8_), channel_id=1, source_target_pairs={{0,4},{1,5},{2,6},{3,7},{4,0},{5,1},{6,2},{7,3},{8,12},{9,13},{10,... | collective-permute-start | bytes 1032200 | tf_op jit(solution)/shard_map/ppermute | solution.py:942
  48.1 13.5 %collective-permute-start.12 = (bf16[4,24,1792]{2,1,0:T(8,128)(2,1)S(1)}, bf16[4,24,1792]{2,1,0:T(8,128)(2,1)S(1)}, u32[]{:S(2)}, u32[]{:S(2)}) collective-permute-start(bf16[4,24,1792]{2,1,0:T(8,128)(2,1)S(1)} %all-to-all-done.1.refs_8_), channel_id=1, source_target_pairs={{0,6},{1,7},{2,4},{3,5},{4,2},{5,3},{6,0},{7,1},{8,14},{9,15},{10,... | collective-permute-start | bytes 1032200 | tf_op jit(solution)/shard_map/ppermute | solution.py:942
  49.6 12.6 %collective-permute-start.13 = (bf16[4,24,1792]{2,1,0:T(8,128)(2,1)S(1)}, bf16[4,24,1792]{2,1,0:T(8,128)(2,1)S(1)}, u32[]{:S(2)}, u32[]{:S(2)}) collective-permute-start(bf16[4,24,1792]{2,1,0:T(8,128)(2,1)S(1)} %all-to-all-done.1.refs_8_), channel_id=1, source_target_pairs={{0,1},{1,0},{2,3},{3,2},{4,5},{5,4},{6,7},{7,6},{8,9},{9,8},{10,11... | collective-permute-start | bytes 1032200 | tf_op jit(solution)/shard_map/ppermute | solution.py:942
  49.6 13.3 %collective-permute-start.6 = (bf16[4,24,1792]{2,1,0:T(8,128)(2,1)S(1)}, bf16[4,24,1792]{2,1,0:T(8,128)(2,1)S(1)}, u32[]{:S(2)}, u32[]{:S(2)}) collective-permute-start(bf16[4,24,1792]{2,1,0:T(8,128)(2,1)S(1)} %all_to_all.35.refs_0_), channel_id=1, source_target_pairs={{0,1},{1,0},{2,3},{3,2},{4,5},{5,4},{6,7},{7,6},{8,9},{9,8},{10,11... | collective-permute-start | bytes 1032200 | tf_op jit(solution)/shard_map/ppermute | solution.py:942
  56.8 7.4 %collective-permute-start.7 = (bf16[4,24,1792]{2,1,0:T(8,128)(2,1)S(1)}, bf16[4,24,1792]{2,1,0:T(8,128)(2,1)S(1)}, u32[]{:S(2)}, u32[]{:S(2)}) collective-permute-start(bf16[4,24,1792]{2,1,0:T(8,128)(2,1)S(1)} %collective-permute-done.refs_1_), channel_id=1, source_target_pairs={{0,1},{1,0},{2,3},{3,2},{4,5},{5,4},{6,7},{7,6},{8,9},{9,8},{10,11... | collective-permute-start | bytes 1032200 | tf_op jit(solution)/shard_map/ppermute | solution.py:942
  61.6 3.9 %collective-permute-start.9 = (bf16[4,24,1792]{2,1,0:T(8,128)(2,1)S(1)}, bf16[4,24,1792]{2,1,0:T(8,128)(2,1)}, u32[]{:S(2)}, u32[]{:S(2)}) collective-permute-start(bf16[4,24,1792]{2,1,0:T(8,128)(2,1)S(1)} %collective-permute-done.2.refs_3_), channel_id=1, source_target_pairs={{0,1},{1,0},{2,3},{3,2},{4,5},{5,4},{6,7},{7,6},{8,9},{9,8},{10,11... | collective-permute-start | bytes 1032200 | tf_op jit(solution)/shard_map/ppermute | solution.py:942
  62.9 4.2 %collective-permute-start.14 = (bf16[4,24,1792]{2,1,0:T(8,128)(2,1)S(1)}, bf16[4,24,1792]{2,1,0:T(8,128)(2,1)}, u32[]{:S(2)}, u32[]{:S(2)}) collective-permute-start(bf16[4,24,1792]{2,1,0:T(8,128)(2,1)S(1)} %collective-permute-done.10.refs_9_), channel_id=1, source_target_pairs={{0,1},{1,0},{2,3},{3,2},{4,5},{5,4},{6,7},{7,6},{8,9},{9,8},{10,11... | collective-permute-start | bytes 1032200 | tf_op jit(solution)/shard_map/ppermute | solution.py:942
  63.6 5.5 %collective-permute-start.15 = (bf16[4,24,1792]{2,1,0:T(8,128)(2,1)S(1)}, bf16[4,24,1792]{2,1,0:T(8,128)(2,1)}, u32[]{:S(2)}, u32[]{:S(2)}) collective-permute-start(bf16[4,24,1792]{2,1,0:T(8,128)(2,1)S(1)} %collective-permute-done.11.refs_10_), channel_id=1, source_target_pairs={{0,1},{1,0},{2,3},{3,2},{4,5},{5,4},{6,7},{7,6},{8,9},{9,8},{10,11... | collective-permute-start | bytes 1032200 | tf_op jit(solution)/shard_map/ppermute | solution.py:942
  64.9 4.3 %collective-permute-start.16 = (bf16[4,24,1792]{2,1,0:T(8,128)(2,1)S(1)}, bf16[4,24,1792]{2,1,0:T(8,128)(2,1)}, u32[]{:S(2)}, u32[]{:S(2)}) collective-permute-start(bf16[4,24,1792]{2,1,0:T(8,128)(2,1)S(1)} %collective-permute-done.12.refs_11_), channel_id=1, source_target_pairs={{0,1},{1,0},{2,3},{3,2},{4,5},{5,4},{6,7},{7,6},{8,9},{9,8},{10,11... | collective-permute-start | bytes 1032200 | tf_op jit(solution)/shard_map/ppermute | solution.py:942
  64.9 32.2 %collective-permute-start.3 = (bf16[4,24,3584]{2,1,0:T(8,128)(2,1)S(1)}, bf16[4,24,3584]{2,1,0:T(8,128)(2,1)S(1)}, u32[]{:S(2)}, u32[]{:S(2)}) collective-permute-start(bf16[4,24,3584]{2,1,0:T(8,128)(2,1)S(1)} %all-to-all-done.2.refs_0_), channel_id=1, source_target_pairs={{0,2},{1,3},{2,0},{3,1},{4,6},{5,7},{6,4},{7,5},{8,10},{9,11},{10,... | collective-permute-start | bytes 2064392 | tf_op jit(solution)/shard_map/ppermute | solution.py:942
  65.6 32.3 %collective-permute-start.4 = (bf16[4,24,3584]{2,1,0:T(8,128)(2,1)S(1)}, bf16[4,24,3584]{2,1,0:T(8,128)(2,1)S(1)}, u32[]{:S(2)}, u32[]{:S(2)}) collective-permute-start(bf16[4,24,3584]{2,1,0:T(8,128)(2,1)S(1)} %all-to-all-done.2.refs_0_), channel_id=1, source_target_pairs={{0,4},{1,5},{2,6},{3,7},{4,0},{5,1},{6,2},{7,3},{8,12},{9,13},{10,... | collective-permute-start | bytes 2064392 | tf_op jit(solution)/shard_map/ppermute | solution.py:942
  67.1 30.8 %collective-permute-start.5 = (bf16[4,24,3584]{2,1,0:T(8,128)(2,1)S(1)}, bf16[4,24,3584]{2,1,0:T(8,128)(2,1)S(1)}, u32[]{:S(2)}, u32[]{:S(2)}) collective-permute-start(bf16[4,24,3584]{2,1,0:T(8,128)(2,1)S(1)} %all-to-all-done.2.refs_0_), channel_id=1, source_target_pairs={{0,6},{1,7},{2,4},{3,5},{4,2},{5,3},{6,0},{7,1},{8,14},{9,15},{10,... | collective-permute-start | bytes 2064392 | tf_op jit(solution)/shard_map/ppermute | solution.py:942
  98.4 3.6 %collective-permute-start.19 = (bf16[4,24,3584]{2,1,0:T(8,128)(2,1)S(1)}, bf16[4,24,3584]{2,1,0:T(8,128)(2,1)S(1)}, u32[]{:S(2)}, u32[]{:S(2)}) collective-permute-start(bf16[4,24,3584]{2,1,0:T(8,128)(2,1)S(1)} %collective-permute-done.4.refs_2_), channel_id=1, source_target_pairs={{0,1},{1,0},{2,3},{3,2},{4,5},{5,4},{6,7},{7,6},{8,9},{9,8},{10,11... | collective-permute-start | bytes 2064392 | tf_op jit(solution)/shard_map/ppermute | solution.py:942
  98.4 4.5 %collective-permute-start.20 = (bf16[4,24,3584]{2,1,0:T(8,128)(2,1)S(1)}, bf16[4,24,3584]{2,1,0:T(8,128)(2,1)S(1)}, u32[]{:S(2)}, u32[]{:S(2)}) collective-permute-start(bf16[4,24,3584]{2,1,0:T(8,128)(2,1)S(1)} %collective-permute-done.5.refs_3_), channel_id=1, source_target_pairs={{0,1},{1,0},{2,3},{3,2},{4,5},{5,4},{6,7},{7,6},{8,9},{9,8},{10,11... | collective-permute-start | bytes 2064392 | tf_op jit(solution)/shard_map/ppermute | solution.py:942
  140.2 33.1 %all-to-all-start.3 = ((bf16[16,24,1536]{2,1,0:T(8,128)(2,1)}), bf16[16,24,1536]{2,1,0:T(8,128)(2,1)}, u32[]{:S(2)}, u32[]{:S(2)}) async-start(bf16[16,24,1536]{2,1,0:T(8,128)(2,1)} %add_convert_fusion.1), calls=%async_computation.3 | async-start | bytes 2359296 | tf_op jit(solution)/shard_map/all_to_all | solution.py:982
  173.3 29.6 %all-to-all-start.4 = ((bf16[16,24,1280]{2,1,0:T(8,128)(2,1)}), bf16[16,24,1280]{2,1,0:T(8,128)(2,1)}, u32[]{:S(2)}, u32[]{:S(2)}) async-start(bf16[16,24,1280]{2,1,0:T(8,128)(2,1)} %add_convert_fusion.3), calls=%async_computation.4 | async-start | bytes 1966080 | tf_op jit(solution)/shard_map/all_to_all | solution.py:982
  203.0 32.9 %all-to-all-start.5 = ((bf16[16,24,1536]{2,1,0:T(8,128)(2,1)}), bf16[16,24,1536]{2,1,0:T(8,128)(2,1)}, u32[]{:S(2)}, u32[]{:S(2)}) async-start(bf16[16,24,1536]{2,1,0:T(8,128)(2,1)} %add_convert_fusion), calls=%async_computation.5 | async-start | bytes 2359296 | tf_op jit(solution)/shard_map/all_to_all | solution.py:982
  235.9 28.7 %all-to-all-start.6 = ((bf16[16,24,1280]{2,1,0:T(8,128)(2,1)}), bf16[16,24,1280]{2,1,0:T(8,128)(2,1)S(1)}, u32[]{:S(2)}, u32[]{:S(2)}) async-start(bf16[16,24,1280]{2,1,0:T(8,128)(2,1)} %add_convert_fusion.2), calls=%async_computation.6 | async-start | bytes 1966080 | tf_op jit(solution)/shard_map/all_to_all | solution.py:982
  (57 other events, 217.0 us)

commit v4 on v3

--- a/solution.py
+++ b/solution.py
@@ -632,6 +632,10 @@
     return rstd * (inner - jnp.mean(inner, axis=-1, keepdims=True) - normed * along)
 
 
+def offsets(place, chip):
+    return (chip // 4 + 4 - place[2]) % 4, place[1] ^ (chip % 4)
+
+
 def ffn_kernel(chips, core, counts, upstream, branch, active, slope, middle, mod, right, down, d_middle, d_mod, bias, keep, send, acc_up, acc_down, *, last):
     step = pl.program_id(0)
 
@@ -671,15 +675,17 @@
         is_odd = core[0] == 1
         for chip in range(chips):
             span = slice(rows * chip, rows * (chip + 1))
+            step_z, step_plane = offsets(core, chip)
             even, odd = acc_up[span, : 2 * D], acc_up[span, 2 * D :]
-            keep[chip, :, : 2 * D] = jnp.where(is_odd, odd, even).astype(BF16)
-            send[chip, :, : 2 * D] = jnp.where(is_odd, even, odd).astype(BF16)
+            keep[step_plane, step_z, :, : 2 * D] = jnp.where(is_odd, odd, even).astype(BF16)
+            send[step_plane, step_z, :, : 2 * D] = jnp.where(is_odd, even, odd).astype(BF16)
             for part in range(2):
                 start = rows * (4 * chip + part)
                 even = acc_down[start : start + rows, :]
                 odd = acc_down[start + 2 * rows : start + 3 * rows, :]
-                keep[chip, :, (2 + part) * D : (3 + part) * D] = jnp.where(is_odd, odd, even).astype(BF16)
-                send[chip, :, (2 + part) * D : (3 + part) * D] = jnp.where(is_odd, even, odd).astype(BF16)
+                columns = slice((2 + part) * D, (3 + part) * D)
+                keep[step_plane, step_z, :, columns] = jnp.where(is_odd, odd, even).astype(BF16)
+                send[step_plane, step_z, :, columns] = jnp.where(is_odd, even, odd).astype(BF16)
 
 
 def ffn_backward(core, counts, upstream, record, weights, chips, last):
@@ -693,8 +699,8 @@
             tokens(D, F32),
             jax.ShapeDtypeStruct((24, D), F32),
             jax.ShapeDtypeStruct((1, FF + D), F32),
-            jax.ShapeDtypeStruct((chips, rows, 4 * D), BF16),
-            jax.ShapeDtypeStruct((chips, rows, 4 * D), BF16),
+            jax.ShapeDtypeStruct((4, 4, rows, 4 * D), BF16),
+            jax.ShapeDtypeStruct((4, 4, rows, 4 * D), BF16),
         ),
         in_specs=[
             SMEM,
@@ -712,8 +718,8 @@
             per_slot(D),
             whole(24, D),
             whole(1, FF + D),
-            whole(chips, rows, 4 * D),
-            whole(chips, rows, 4 * D),
+            whole(4, 4, rows, 4 * D),
+            whole(4, 4, rows, 4 * D),
         ),
         scratch_shapes=[pltpu.VMEM((D, FF), F32), pltpu.VMEM((FF, D), F32)],
         compiler_params=params_of(1),
@@ -808,12 +814,15 @@
                         pieces.append(jnp.zeros((1, 128), F32))
                 pieces.append(jnp.zeros((rows - 2, 128), F32))
                 tails.append(jnp.concatenate(pieces, axis=0))
-            keep[chip, :, : 2 * D] = jnp.where(is_odd, odd, even).astype(BF16)
-            send[chip, :, : 2 * D] = jnp.where(is_odd, even, odd).astype(BF16)
-            keep[chip, :, 2 * D : 2 * D + 128] = jnp.where(is_odd, tails[1], tails[0]).astype(BF16)
-            send[chip, :, 2 * D : 2 * D + 128] = jnp.where(is_odd, tails[0], tails[1]).astype(BF16)
-            keep[chip, :, 2 * D + 128 :] = low_mod
-            send[chip, :, 2 * D + 128 :] = jnp.zeros_like(low_mod)
+            step_z, step_plane = offsets(core, chip)
+            keep[step_plane, step_z, :, : 2 * D] = jnp.where(is_odd, odd, even).astype(BF16)
+            send[step_plane, step_z, :, : 2 * D] = jnp.where(is_odd, even, odd).astype(BF16)
+            keep[step_plane, step_z, :, 2 * D :] = jnp.where(is_odd, tails[1], tails[0]).astype(BF16)
+            send[step_plane, step_z, :, 2 * D :] = jnp.where(is_odd, tails[0], tails[1]).astype(BF16)
+        for step_plane in range(4):
+            keep[step_plane, 4, :, :D] = low_mod
+            keep[step_plane, 4, :, D:] = jnp.zeros((24, D + 128), BF16)
+            send[step_plane, 4] = jnp.zeros((24, 2 * D + 128), BF16)
 
 
 def attention_backward(core, d_middle, hidden, record, weights, d_mod, bias, cond, d_cond, chips, first):
@@ -826,8 +835,8 @@
         out_shape=(
             tokens(D, F32),
             jax.ShapeDtypeStruct((SLOT, D), F32),
-            jax.ShapeDtypeStruct((chips, rows, 3 * D + 128), BF16),
-            jax.ShapeDtypeStruct((chips, rows, 3 * D + 128), BF16),
+            jax.ShapeDtypeStruct((4, 5, rows, 2 * D + 128), BF16),
+            jax.ShapeDtypeStruct((4, 5, rows, 2 * D + 128), BF16),
         ),
         in_specs=[
             SMEM,
@@ -847,8 +856,8 @@
         out_specs=(
             per_slot(D),
             whole(SLOT, D),
-            whole(chips, rows, 3 * D + 128),
-            whole(chips, rows, 3 * D + 128),
+            whole(4, 5, rows, 2 * D + 128),
+            whole(4, 5, rows, 2 * D + 128),
         ),
         scratch_shapes=[
             pltpu.VMEM((D, 3 * D), F32),
@@ -856,16 +865,16 @@
             pltpu.VMEM((24, D), F32),
             pltpu.VMEM((1, BIAS), F32),
         ],
-        compiler_params=params_of(1),
+        compiler_params=params_of(1, 52 if first else 36),
         cost_estimate=cost(6 * 10**9, 20 * 2**20),
         name="attention_backward",
     )(core, d_middle, hidden, qkv, attended, projected, mod, left, right, d_mod, bias, cond, d_cond)
 
 
-def finish_kernel(chips, core, own_ffn, own_attn, got_ffn, got_attn, own_mod, got_mod, cond, chip, ada_out, qkv_out, proj_out, fc1_out, fc2_out, bias_out):
+def finish_kernel(chips, place, own_ffn, own_attn, got_ffn, got_attn, own_mod, got_mod, cond, ada_out, qkv_out, proj_out, fc1_out, fc2_out, bias_out):
     rows = D // (2 * chips)
-    is_odd = core[0] == 1
-    mine = 2 * chip[0] + core[0]
+    is_odd = place[0] == 1
+    mine = 8 * place[2] + 2 * place[1] + place[0]
     take = lax.broadcasted_iota(jnp.int32, (16, D), 0)
     column = lax.broadcasted_iota(jnp.int32, (16, D), 1)
     pick = ((column == rows * mine + take) & (take < rows)).astype(F32).astype(BF16)
@@ -873,13 +882,23 @@
     slots = SLOT * chips
     source = lax.broadcasted_iota(jnp.int32, (slots, 24 * chips), 0)
     target = lax.broadcasted_iota(jnp.int32, (slots, 24 * chips), 1)
+    block = target // 24
+    chip = 4 * ((place[2] + 4 - block // 4) % 4) + ((block % 4) ^ place[1])
     places = []
     for part in range(6):
-        place = (target == 24 * (source // SLOT) + SLOT * part + source % SLOT).astype(F32).astype(BF16)
-        places.append([dot_nn(chosen[side], place).astype(BF16) for side in range(2)])
+        spot = (source // SLOT == chip) & (target % 24 == SLOT * part + source % SLOT)
+        spot = spot.astype(F32).astype(BF16)
+        places.append([dot_nn(chosen[side], spot).astype(BF16) for side in range(2)])
+
+    def in_rows(mods):
+        return jnp.concatenate(
+            [mods[level, :, step * D : (step + 1) * D] for level in range(4) for step in range(4)], axis=0
+        )
+
     for layer in range(2):
-        even = jnp.where(is_odd, got_mod[layer], own_mod[layer])
-        odd = jnp.where(is_odd, own_mod[layer], got_mod[layer])
+        own, got = in_rows(own_mod.at[layer]), in_rows(got_mod.at[layer])
+        even = jnp.where(is_odd, got, own)
+        odd = jnp.where(is_odd, own, got)
         for part in range(6):
             block = dot_nn(places[part][0], even) + dot_nn(places[part][1], odd)
             for row in range(rows):
@@ -911,15 +930,15 @@
             ]
 
 
-def finish(core, chip, own_ffn, own_attn, got_ffn, got_attn, own_mod, got_mod, cond, shapes, chips):
+def finish(place, own_ffn, own_attn, got_ffn, got_attn, own_mod, got_mod, cond, shapes, chips):
     return pl.pallas_call(
         functools.partial(finish_kernel, chips),
         out_shape=tuple(jax.ShapeDtypeStruct(shape, F32) for shape in shapes),
-        in_specs=[SMEM] + [VMEM] * 7 + [SMEM],
+        in_specs=[SMEM] + [VMEM] * 7,
         out_specs=(VMEM,) * 6,
         compiler_params=params_of(),
         name="finish",
-    )(core, own_ffn, own_attn, got_ffn, got_attn, own_mod, got_mod, cond, chip)
+    )(place, own_ffn, own_attn, got_ffn, got_attn, own_mod, got_mod, cond)
 
 
 def fast_body(
@@ -929,13 +948,10 @@
     chips = devices // 2
     rows = D // devices
     index = lax.axis_index("fsdp")
-    core, chip = (index % 2).reshape(1), (index // 2).reshape(1)
-    pairs = [[2 * one, 2 * one + 1] for one in range(chips)]
-    across = [[2 * one + side for one in range(chips)] for side in range(2)]
     swap = [(one, one ^ 1) for one in range(devices)]
 
     lines = [[8 * level + one for level in range(4)] for one in range(8)]
-    place = jnp.stack([index % 2, (index // 2) % 4])
+    place = core = jnp.stack([index % 2, index // 2 % 4, index // 8])
     tie = lax.optimization_barrier
 
     def along(value, bit):
@@ -954,9 +970,8 @@
         ada_weight, qkv_weight, proj_weight, fc1_weight, fc2_weight, biases, condition, rows, 4
     )
     stack_left, copies_right = tie((stacked(copies_left), copies_right))
-    blocks, stack_right, copies_last = tie(
-        ([block for block, _ in planes_of(stack_left, 0)], stacked(copies_right), copies_last)
-    )
+    stack_right, copies_last = tie((stacked(copies_right), copies_last))
+    blocks, stack_right = tie(([block for block, _ in planes_of(stack_left, 0)], stack_right))
     planes_left = [(block, (0, step, 0, 0)) for step, block in enumerate(blocks)]
     planes_right = planes_of(stack_right, WIRE // 2)
     stack_last = stacked(copies_last)
@@ -972,47 +987,61 @@
     weights, records, hidden = [first_weights, last_weights], [first, last], [latents_in, first[0], last[0]]
     upstream = cotangent
     d_cond = jnp.zeros((SLOT, D), F32)
-    reduced = [None, None]
 
     def paired(keep, send):
         got = lax.ppermute(send, "fsdp", swap)
-        return (keep.astype(F32) + got.astype(F32)).astype(BF16)
-
-    def exchanged(both):
-        return lax.all_to_all(both, "fsdp", 0, 0, axis_index_groups=across, tiled=True)
-
-    def summed(spread):
-        return jnp.sum(spread.astype(F32), axis=0)
+        return [(keep[step].astype(F32) + got[step].astype(F32)).astype(BF16) for step in range(4)]
+
+    def in_plane(parts):
+        return [parts[step] if step == 0 else along(parts[step], 2 * step) for step in range(4)]
+
+    def in_line(parts):
+        def shifted(value, step):
+            return lax.ppermute(value, "fsdp", [(one, (one + 8 * step) % devices) for one in range(devices)])
+
+        return [parts[step] if step == 0 else shifted(parts[step], step) for step in range(4)]
+
+    def plane_sums(parts):
+        return [sum(part[level].astype(F32) for part in parts).astype(BF16) for level in range(4)]
+
+    def with_mods(parts):
+        mods = [part[4, :, :D] for part in parts]
+        return [jnp.concatenate([level, *mods], axis=1) for level in plane_sums(parts)]
+
+    def total(parts):
+        return sum(part.astype(F32) for part in parts)
 
     d_middle, d_mod, bias, *wire = ffn_backward(core, counts, upstream, records[1], weights[1], chips, True)
     d_middle, both = tie((d_middle, paired(*wire)))
-    ffn_last = exchanged(both)
+    ffn_last = in_plane(both)
     upstream, d_cond, *wire = attention_backward(
         core, d_middle, hidden[1], records[1], weights[1], d_mod, bias, condition, d_cond, chips, False
     )
-    upstream, both, ffn_last = tie((upstream, paired(*wire), ffn_last))
-    attn_last = exchanged(both)
+    upstream, wire, ffn_last = tie((upstream, wire, ffn_last))
+    upstream, both, sums = tie((upstream, paired(*wire), plane_sums(ffn_last)))
+    ffn_last, attn_last = in_line(sums), in_plane(both)
     d_middle, d_mod, bias, *wire = ffn_backward(core, counts, upstream, records[0], weights[0], chips, False)
-    d_middle, both, attn_last = tie((d_middle, paired(*wire), attn_last))
-    ffn_first = exchanged(both)
+    d_middle, wire, ffn_last, attn_last = tie((d_middle, wire, ffn_last, attn_last))
+    d_middle, both, sums = tie((d_middle, paired(*wire), with_mods(attn_last)))
+    attn_last, ffn_first = in_line(sums), in_plane(both)
     upstream, d_cond, *wire = attention_backward(
         core, d_middle, hidden[0], records[0], weights[0], d_mod, bias, condition, d_cond, chips, True
     )
-    both, ffn_first = tie((paired(*wire), ffn_first))
-    attn_first = exchanged(both)
+    wire, attn_last, ffn_first = tie((wire, attn_last, ffn_first))
+    attn_first = in_plane(paired(*wire))
+    ffn_first = in_line(plane_sums(ffn_first))
+    attn_first = in_line(with_mods(attn_first))
     width = 2 * D + 128
-    for layer, (ffn, attn) in enumerate(((ffn_first, attn_first), (ffn_last, attn_last))):
-        reduced[layer] = (summed(ffn), summed(attn[:, :, :width]), attn[:, :, width:].reshape(24 * chips, D))
-    own_ffn = jnp.stack([reduced[layer][0] for layer in range(2)])
-    own_attn = jnp.stack([reduced[layer][1] for layer in range(2)])
-    own_mod = jnp.stack([reduced[layer][2] for layer in range(2)])
+    own_ffn = jnp.stack([total(ffn_first), total(ffn_last)])
+    own_attn = jnp.stack([total([part[:, :width] for part in parts]) for parts in (attn_first, attn_last)])
+    own_mod = jnp.stack([jnp.stack([part[:, width:] for part in parts]) for parts in (attn_first, attn_last)])
     start = (1 - index % 2) * rows
     to_send = jnp.concatenate([own_ffn[:, :, : 2 * D], own_attn[:, :, : 2 * D]], axis=2)
     got = lax.ppermute(lax.dynamic_slice_in_dim(to_send, start, rows, axis=1), "fsdp", swap)
     got_mod = lax.ppermute(own_mod, "fsdp", swap)
     shapes = [array.shape for array in (ada_weight, qkv_weight, proj_weight, fc1_weight, fc2_weight, biases)]
     grads = finish(
-        core, chip, own_ffn, own_attn, got[:, :, : 2 * D], got[:, :, 2 * D :], own_mod, got_mod, cond_all, shapes, chips
+        place, own_ffn, own_attn, got[:, :, : 2 * D], got[:, :, 2 * D :], own_mod, got_mod, cond_all, shapes, chips
     )
     return (hidden[2], upstream, d_cond, *grads)
 

time: 271 us -> 247 us (0.911)
  local copies, waits for them, and re-layouts: 41.2 us -> 14.8 us
  other arithmetic: 9.56 us -> 2.02 us
  Pallas kernels: 89.2 us -> 95.4 us
  starting transfers between devices: 47 us -> 50.6 us
    unnamed x96 -> x74, local copies, waits for them, and re-layouts: 40.2 us -> 14.7 us
    all_to_all x4 -> x0, starting transfers between devices: 24.9 us -> none  [exchanged(): lax.all_to_all(both, 'fsdp', 0, 0, axis_index_groups=across, tiled=True)]
    all_to_all x4 -> x0, waiting for transfers between devices: 21.4 us -> none  [exchanged(): lax.all_to_all(both, 'fsdp', 0, 0, axis_index_groups=across, tiled=True)]
    ppermute x0 -> x12, waiting for transfers between devices: none -> 17.4 us  [shifted(): lax.ppermute(value, 'fsdp', [(one, (one + 8 * step) % devices) for one in...]
    ppermute x0 -> x12, starting transfers between devices: none -> 15.4 us  [shifted(): lax.ppermute(value, 'fsdp', [(one, (one + 8 * step) % devices) for one in...]
    ppermute x21 -> x33, starting transfers between devices: 13.1 us -> 27.3 us  [along(): lax.ppermute(value, 'fsdp', [(one, one ^ bit) for one in range(devices)])]
    all_to_all x2, waiting for transfers between devices: 0.01 us -> 6.22 us  [stacked(): lax.all_to_all(copies, 'fsdp', 0, 0, axis_index_groups=lines, tiled=True)]
    reduce_sum x4 -> x0, other arithmetic: 4.18 us -> none  [summed(): return jnp.sum(spread.astype(F32), axis=0)]
  transfers between devices with their start and end apart: 33 -> 53, of which waited for: 18 -> 21; matrix products, arithmetic and copies ran while one was open for 3% -> 0% of each run, Pallas kernels for 20% -> 24%
where the time goes in v4:
time: 247 us; the launch traced here: 246 us
  Pallas kernels  95.4 us (39%)
  waiting for transfers between devices  64.4 us (26%)
  starting transfers between devices  50.6 us (20%)
  blocking collectives  17 us (7%)
  local copies, waits for them, and re-layouts  14.8 us (6%)
    pallas_call x2, Pallas kernels, forward_block(): pl.pallas_call(functools.partial(forward_kernel, last=last), grid=(SLOT /...  31.8 us
    ppermute x33, waiting for transfers between devices, along(): lax.ppermute(value, 'fsdp', [(one, one ^ bit) for one in range(devices)])  31.5 us
    pallas_call x2, Pallas kernels, attention_backward(): pl.pallas_call(functools.partial(attention_kernel, chips, first=first), g...  29.9 us
    ppermute x33, starting transfers between devices, along(): lax.ppermute(value, 'fsdp', [(one, one ^ bit) for one in range(devices)])  27.3 us
    pallas_call x2, Pallas kernels, ffn_backward(): pl.pallas_call(functools.partial(ffn_kernel, chips, last=last), grid=(SLO...  21.1 us
    ppermute x12, waiting for transfers between devices, shifted(): lax.ppermute(value, 'fsdp', [(one, (one + 8 * step) % devices) for one in...  17.4 us
    all_to_all x1, blocking collectives, stacked(): lax.all_to_all(copies, 'fsdp', 0, 0, axis_index_groups=lines, tiled=True)  17 us
    ppermute x12, starting transfers between devices, shifted(): lax.ppermute(value, 'fsdp', [(one, (one + 8 * step) % devices) for one in...  15.4 us
  transfers between devices with their start and end apart: 53, of which 21 were waited for; matrix products, arithmetic and copies ran while one was open for 0% of the time, Pallas kernels for 24%

profile of v4, /device:TPU:0, one launch (start us, length us, event | category | flops | bytes accessed | tf_op | source)
XLA Modules:
  0.0 246.1 jit_solution(11835744942208278751)
XLA Ops:
  0.6 2.9 %pack.1 = (bf16[4,24,1792]{2,1,0:T(8,128)(2,1)}, bf16[4,24,1792]{2,1,0:T(8,128)(2,1)}, bf16[4,24,3584]{2,1,0:T(8,128)(2,1)}) custom-call(bf16[2,27648]{1,0:T(2,128)(2,1)} %ada_in.1, bf16[2,13824]{1,0:T(2,128)(2,1)} %qkv_in.1, bf16[2,4608]{1,0:T(2,128)(2,1)} %proj_in.1, bf16[2,18432]{1,0:T(2,128)(2,1)} %fc1_in.1, bf16[2,18432]{1,0:T(2,128)(2,1)} %fc2_in.1, ...), custom_call_target="tpu_custom_call" | custom-call | tf_op jit(solution)/shard_map/pack/pallas_call | solution.py:380
  3.6 17.0 %all_to_all.15.refs_0_ = bf16[4,24,1792]{2,1,0:T(8,128)(2,1)S(1)} all-to-all(bf16[4,24,1792]{2,1,0:T(8,128)(2,1)} %get-tuple-element.138), channel_id=1, replica_groups={{0,8,16,24},{1,9,17,25},{2,10,18,26},{3,11,19,27},{4,12,20,28},{5,13,21..., dimensions={0} | all-to-all | bytes 688128 | tf_op jit(solution)/shard_map/all_to_all | solution.py:961
  20.5 3.5 %all-to-all-start.1 = ((bf16[4,24,1792]{2,1,0:T(8,128)(2,1)}), bf16[4,24,1792]{2,1,0:T(8,128)(2,1)S(1)}, u32[]{:S(2)}, u32[]{:S(2)}) async-start(bf16[4,24,1792]{2,1,0:T(8,128)(2,1)} %get-tuple-element.140), calls=%async_computation.1 | async-start | bytes 688128 | tf_op jit(solution)/shard_map/all_to_all | solution.py:961
  27.6 6.2 %all-to-all-done.1.refs_8_ = bf16[4,24,1792]{2,1,0:T(8,128)(2,1)S(1)} async-done(((bf16[4,24,1792]{2,1,0:T(8,128)(2,1)}), bf16[4,24,1792]{2,1,0:T(8,128)(2,1)S(1)}, u32[]{:S(2)}, u32[]{:S(2)}) %all-to-all-start.1) | async-done | bytes 344096 | tf_op jit(solution)/shard_map/all_to_all | solution.py:961
  33.8 3.5 %all-to-all-start.2 = ((bf16[4,24,3584]{2,1,0:T(8,128)(2,1)}), bf16[4,24,3584]{2,1,0:T(8,128)(2,1)S(1)}, u32[]{:S(2)}, u32[]{:S(2)}) async-start(bf16[4,24,3584]{2,1,0:T(8,128)(2,1)} %get-tuple-element.142), calls=%async_computation.2 | async-start | bytes 1376256 | tf_op jit(solution)/shard_map/all_to_all | solution.py:961
  37.3 4.1 %collective-permute-done.4.refs_2_ = bf16[4,24,1792]{2,1,0:T(8,128)(2,1)S(1)} collective-permute-done((bf16[4,24,1792]{2,1,0:T(8,128)(2,1)S(1)}, bf16[4,24,1792]{2,1,0:T(8,128)(2,1)S(1)}, u32[]{:S(2)}, u32[]{:S(2)}) %collective-permute-start.4) | collective-permute-done | bytes 344096 | tf_op jit(solution)/shard_map/ppermute | solution.py:958
  45.4 7.0 %collective-permute-done.10.refs_9_ = bf16[4,24,1792]{2,1,0:T(8,128)(2,1)S(1)} collective-permute-done((bf16[4,24,1792]{2,1,0:T(8,128)(2,1)S(1)}, bf16[4,24,1792]{2,1,0:T(8,128)(2,1)S(1)}, u32[]{:S(2)}, u32[]{:S(2)}) %collective-permute-start.10) | collective-permute-done | bytes 344096 | tf_op jit(solution)/shard_map/ppermute | solution.py:958
  52.4 5.1 %collective-permute-done.11.refs_10_ = bf16[4,24,1792]{2,1,0:T(8,128)(2,1)S(1)} collective-permute-done((bf16[4,24,1792]{2,1,0:T(8,128)(2,1)S(1)}, bf16[4,24,1792]{2,1,0:T(8,128)(2,1)S(1)}, u32[]{:S(2)}, u32[]{:S(2)}) %collective-permute-start.11) | collective-permute-done | bytes 344096 | tf_op jit(solution)/shard_map/ppermute | solution.py:958
  67.9 3.1 %unpack.2 = (bf16[384,2688]{1,0:T(8,128)(2,1)S(1)}, bf16[384,2688]{1,0:T(8,128)(2,1)S(1)}, bf16[1536,384]{1,0:T(8,128)(2,1)S(1)}, f32[1,5376]{1,0:T(1,128)S(1)}, f32[2,64,384]{2,1,0:T(8,128)S(1)}) custom-call(s32[3]{0:T(128)S(1)} %pad_add_fusion.place.core, bf16[4,24,1792]{2,1,0:T(8,128)(2,1)S(1)} %all_to_all.15.refs_0_, ...), custom_call_target="tpu_custom_call" | custom-call | tf_op jit(solution)/shard_map/unpack/pallas_call | solution.py:438
  71.7 15.8 %forward_block.2 = (f32[4,256,384]{2,1,0:T(8,128)S(1)}, f32[4,2304]{1,0:T(4,128)S(1)}, bf16[4,256,1152]{2,1,0:T(8,128)(2,1)S(1)}, bf16[4,256,384]{2,1,0:T(8,128)...) custom-call(s32[1]{0:T(128)S(6)} %copy.47.counts, ...), custom_call_target="tpu_custom_call" | custom-call | flops 5000000000 | bytes 20971520 | tf_op jit(solution)/shard_map/forward_block/pallas_call | solution.py:589
  98.8 3.9 %unpack.3 = (bf16[384,2688]{1,0:T(8,128)(2,1)S(1)}, bf16[384,2688]{1,0:T(8,128)(2,1)S(1)}, bf16[1536,384]{1,0:T(8,128)(2,1)S(1)}, f32[1,5376]{1,0:T(1,128)S(1)}, f32[2,64,384]{2,1,0:T(8,128)}) custom-call(s32[3]{0:T(128)S(1)} %pad_add_fusion.place.core, bf16[4,24,3584]{2,1,0:T(8,128)(2,1)S(1)} %all-to-all-done.2.refs_0_, ...), custom_call_target="tpu_custom_call" | custom-call | tf_op jit(solution)/shard_map/unpack/pallas_call | solution.py:438
  102.7 16.0 %forward_block.3 = (f32[4,256,384]{2,1,0:T(8,128)}, f32[4,2304]{1,0:T(4,128)S(1)}, bf16[4,256,1152]{2,1,0:T(8,128)(2,1)S(1)}, bf16[4,256,384]{2,1,0:T(8,128)(2,1...) custom-call(s32[1]{0:T(128)S(6)} %copy.47.counts, ...), custom_call_target="tpu_custom_call" | custom-call | flops 5000000000 | bytes 20971520 | tf_op jit(solution)/shard_map/forward_block/pallas_call | solution.py:589
  121.3 10.1 %ffn_backward.2 = (f32[4,256,384]{2,1,0:T(8,128)S(1)}, f32[24,384]{1,0:T(8,128)S(1)}, f32[1,1920]{1,0:T(1,128)S(1)}, bf16[4,4,24,1536]{3,2,1,0:T(8,128)(2,1)S(1)}, bf16[4,4,24,1536]{3,2,1,0:T(8,128)(2,1)S(1)}) custom-call(s32[3]{0:T(128)S(1)} %pad_add_fusion.place.core, s32[1]{0:T(128)S(6)} %copy.47.counts, bf16[4,256,384]{2,1,0:T(8,128)(2,1)S(1)} %copy-done.13, ...), custom_call_target="tpu_custom_call" | custom-call | flops 8000000000 | bytes 20971520 | tf_op jit(solution)/shard_map/ffn_backward/pallas_call | solution.py:695
  131.6 2.7 %collective-permute-done.21 = bf16[4,4,24,1536]{3,2,1,0:T(8,128)(2,1)S(1)} collective-permute-done((bf16[4,4,24,1536]{3,2,1,0:T(8,128)(2,1)S(1)}, bf16[4,4,24,1536]{3,2,1,0:T(8,128)(2,1)S(1)}, u32[]{:S(2)}, u32[]{:S(2)}) %collective-permute-start.21) | collective-permute-done | bytes 1179680 | tf_op jit(solution)/shard_map/ppermute | solution.py:992
  138.3 13.1 %attention_backward.2 = (f32[4,256,384]{2,1,0:T(8,128)S(1)}, f32[4,384]{1,0:T(4,128)S(1)}, bf16[4,5,24,896]{3,2,1,0:T(8,128)(2,1)S(1)}, bf16[4,5,24,896]{3,2,1,0:T(8,128)(2,1)S(1)}) custom-call(s32[3]{0:T(128)S(1)} %pad_add_fusion.place.core, f32[4,256,384]{2,1,0:T(8,128)S(1)} %get-tuple-element.183.d_middle, f32[4,256,384]{2,1,0:T(8,128)S(1)} %copy-done.22, ...), custom_call_target="tpu_custom_call" | custom-call | flops 6000000000 | bytes 20971520 | tf_op jit(solution)/shard_map/attention_backward/pallas_call | solution.py:832
  162.8 11.0 %ffn_backward.3 = (f32[4,256,384]{2,1,0:T(8,128)S(1)}, f32[24,384]{1,0:T(8,128)S(1)}, f32[1,1920]{1,0:T(1,128)S(1)}, bf16[4,4,24,1536]{3,2,1,0:T(8,128)(2,1)S(1)}, bf16[4,4,24,1536]{3,2,1,0:T(8,128)(2,1)}) custom-call(s32[3]{0:T(128)S(1)} %pad_add_fusion.place.core, s32[1]{0:T(128)S(6)} %copy.47.counts, f32[4,256,384]{2,1,0:T(8,128)S(1)} %get-tuple-element.203.upstream, ...), custom_call_target="tpu_custom_call" | custom-call | flops 8000000000 | bytes 20971520 | tf_op jit(solution)/shard_map/ffn_backward/pallas_call | solution.py:695
  175.9 2.8 %collective-permute-done.32 = bf16[4,4,24,1536]{3,2,1,0:T(8,128)(2,1)S(1)} collective-permute-done((bf16[4,4,24,1536]{3,2,1,0:T(8,128)(2,1)}, bf16[4,4,24,1536]{3,2,1,0:T(8,128)(2,1)S(1)}, u32[]{:S(2)}, u32[]{:S(2)}) %collective-permute-start.32) | collective-permute-done | bytes 1179680 | tf_op jit(solution)/shard_map/ppermute | solution.py:992
  186.5 16.8 %attention_backward.3 = (f32[4,256,384]{2,1,0:T(8,128)}, f32[4,384]{1,0:T(4,128)}, bf16[4,5,24,896]{3,2,1,0:T(8,128)(2,1)}, bf16[4,5,24,896]{3,2,1,0:T(8,128)(2,1)}) custom-call(s32[3]{0:T(128)S(1)} %pad_add_fusion.place.core, f32[4,256,384]{2,1,0:T(8,128)} %copy-done.24, bf16[4,256,384]{2,1,0:T(8,128)(2,1)S(1)} %copy-done.15, ...), custom_call_target="tpu_custom_call" | custom-call | flops 6000000000 | bytes 20971520 | tf_op jit(solution)/shard_map/attention_backward/pallas_call | solution.py:832
  205.7 2.8 %collective-permute-start.41 = (bf16[24,1536]{1,0:T(8,128)(2,1)S(1)}, bf16[24,1536]{1,0:T(8,128)(2,1)S(1)}, u32[]{:S(2)}, u32[]{:S(2)}) collective-permute-start(bf16[24,1536]{1,0:T(8,128)(2,1)S(1)} %get-tuple-element.284), channel_id=1, source_target_pairs={{0,24},{1,25},{2,26},{3,27},{4,28},{5,29},{6,30},{7,31},{8,0},{9,1... | collective-permute-start | bytes 221192 | tf_op jit(solution)/shard_map/ppermute | solution.py:1000
  210.5 2.7 %collective-permute-done.40 = bf16[24,1536]{1,0:T(8,128)(2,1)S(1)} collective-permute-done((bf16[24,1536]{1,0:T(8,128)(2,1)S(1)}, bf16[24,1536]{1,0:T(8,128)(2,1)S(1)}, u32[]{:S(2)}, u32[]{:S(2)}) %collective-permute-start.40) | collective-permute-done | bytes 73760 | tf_op jit(solution)/shard_map/ppermute | solution.py:1000
  217.2 5.6 %collective-permute-done.45 = bf16[5,24,896]{2,1,0:T(8,128)(2,1)S(1)} collective-permute-done((bf16[5,24,896]{2,1,0:T(8,128)(2,1)S(1)}, bf16[5,24,896]{2,1,0:T(8,128)(2,1)S(1)}, u32[]{:S(2)}, u32[]{:S(2)}) %collective-permute-start.45) | collective-permute-done | bytes 215072 | tf_op jit(solution)/shard_map/ppermute | solution.py:958
  222.8 3.6 %collective-permute-done.44 = bf16[5,24,896]{2,1,0:T(8,128)(2,1)S(1)} collective-permute-done((bf16[5,24,896]{2,1,0:T(8,128)(2,1)S(1)}, bf16[5,24,896]{2,1,0:T(8,128)(2,1)S(1)}, u32[]{:S(2)}, u32[]{:S(2)}) %collective-permute-start.44) | collective-permute-done | bytes 215072 | tf_op jit(solution)/shard_map/ppermute | solution.py:958
  232.7 8.1 %collective-permute-done.47 = bf16[24,2432]{1,0:T(8,128)(2,1)S(1)} collective-permute-done((bf16[24,2432]{1,0:T(8,128)(2,1)S(1)}, bf16[24,2432]{1,0:T(8,128)(2,1)S(1)}, u32[]{:S(2)}, u32[]{:S(2)}) %collective-permute-start.47) | collective-permute-done | bytes 116768 | tf_op jit(solution)/shard_map/ppermute | solution.py:1000
  243.3 2.8 %finish.1 = (f32[2,27648]{1,0:T(2,128)}, f32[2,13824]{1,0:T(2,128)}, f32[2,4608]{1,0:T(2,128)}, f32[2,18432]{1,0:T(2,128)}, f32[2,18432]{1,0:T(2,128)}, /*index=5*/f32[2,256]{1,0:T(2,128)}) custom-call(s32[3]{0:T(128)S(1)} %pad_add_fusion.place.core, f32[2,24,1536]{2,1,0:T(8,128)S(1)} %pad_maximum_fusion.1.own_ffn, ...), custom_call_target="tpu_custom_call" | custom-call | tf_op jit(solution)/shard_map/finish/pallas_call | solution.py:934
  (202 shorter events, 74.1 us)
Async XLA Ops:
  20.5 13.2 %all-to-all-start.1 = ((bf16[4,24,1792]{2,1,0:T(8,128)(2,1)}), bf16[4,24,1792]{2,1,0:T(8,128)(2,1)S(1)}, u32[]{:S(2)}, u32[]{:S(2)}) async-start(bf16[4,24,1792]{2,1,0:T(8,128)(2,1)} %get-tuple-element.140), calls=%async_computation.1 | async-start | bytes 688128 | tf_op jit(solution)/shard_map/all_to_all | solution.py:961
  24.0 13.3 %collective-permute-start.3 = (bf16[4,24,1792]{2,1,0:T(8,128)(2,1)S(1)}, bf16[4,24,1792]{2,1,0:T(8,128)(2,1)S(1)}, u32[]{:S(2)}, u32[]{:S(2)}) collective-permute-start(bf16[4,24,1792]{2,1,0:T(8,128)(2,1)S(1)} %all_to_all.15.refs_0_), channel_id=1, source_target_pairs={{0,2},{1,3},{2,0},{3,1},{4,6},{5,7},{6,4},{7,5},{8,10},{9,11},{10,... | collective-permute-start | bytes 1032200 | tf_op jit(solution)/shard_map/ppermute | solution.py:958
  25.6 15.8 %collective-permute-start.4 = (bf16[4,24,1792]{2,1,0:T(8,128)(2,1)S(1)}, bf16[4,24,1792]{2,1,0:T(8,128)(2,1)S(1)}, u32[]{:S(2)}, u32[]{:S(2)}) collective-permute-start(bf16[4,24,1792]{2,1,0:T(8,128)(2,1)S(1)} %all_to_all.15.refs_0_), channel_id=1, source_target_pairs={{0,4},{1,5},{2,6},{3,7},{4,0},{5,1},{6,2},{7,3},{8,12},{9,13},{10,... | collective-permute-start | bytes 1032200 | tf_op jit(solution)/shard_map/ppermute | solution.py:958
  27.1 14.3 %collective-permute-start.5 = (bf16[4,24,1792]{2,1,0:T(8,128)(2,1)S(1)}, bf16[4,24,1792]{2,1,0:T(8,128)(2,1)S(1)}, u32[]{:S(2)}, u32[]{:S(2)}) collective-permute-start(bf16[4,24,1792]{2,1,0:T(8,128)(2,1)S(1)} %all_to_all.15.refs_0_), channel_id=1, source_target_pairs={{0,6},{1,7},{2,4},{3,5},{4,2},{5,3},{6,0},{7,1},{8,14},{9,15},{10,... | collective-permute-start | bytes 1032200 | tf_op jit(solution)/shard_map/ppermute | solution.py:958
  33.8 27.0 %all-to-all-start.2 = ((bf16[4,24,3584]{2,1,0:T(8,128)(2,1)}), bf16[4,24,3584]{2,1,0:T(8,128)(2,1)S(1)}, u32[]{:S(2)}, u32[]{:S(2)}) async-start(bf16[4,24,3584]{2,1,0:T(8,128)(2,1)} %get-tuple-element.142), calls=%async_computation.2 | async-start | bytes 1376256 | tf_op jit(solution)/shard_map/all_to_all | solution.py:961
  42.6 14.9 %collective-permute-start.11 = (bf16[4,24,1792]{2,1,0:T(8,128)(2,1)S(1)}, bf16[4,24,1792]{2,1,0:T(8,128)(2,1)S(1)}, u32[]{:S(2)}, u32[]{:S(2)}) collective-permute-start(bf16[4,24,1792]{2,1,0:T(8,128)(2,1)S(1)} %all-to-all-done.1.refs_8_), channel_id=1, source_target_pairs={{0,4},{1,5},{2,6},{3,7},{4,0},{5,1},{6,2},{7,3},{8,12},{9,13},{10,... | collective-permute-start | bytes 1032200 | tf_op jit(solution)/shard_map/ppermute | solution.py:958
  43.4 14.0 %collective-permute-start.12 = (bf16[4,24,1792]{2,1,0:T(8,128)(2,1)S(1)}, bf16[4,24,1792]{2,1,0:T(8,128)(2,1)S(1)}, u32[]{:S(2)}, u32[]{:S(2)}) collective-permute-start(bf16[4,24,1792]{2,1,0:T(8,128)(2,1)S(1)} %all-to-all-done.1.refs_8_), channel_id=1, source_target_pairs={{0,6},{1,7},{2,4},{3,5},{4,2},{5,3},{6,0},{7,1},{8,14},{9,15},{10,... | collective-permute-start | bytes 1032200 | tf_op jit(solution)/shard_map/ppermute | solution.py:958
  44.9 13.9 %collective-permute-start.6 = (bf16[4,24,1792]{2,1,0:T(8,128)(2,1)S(1)}, bf16[4,24,1792]{2,1,0:T(8,128)(2,1)S(1)}, u32[]{:S(2)}, u32[]{:S(2)}) collective-permute-start(bf16[4,24,1792]{2,1,0:T(8,128)(2,1)S(1)} %all_to_all.15.refs_0_), channel_id=1, source_target_pairs={{0,1},{1,0},{2,3},{3,2},{4,5},{5,4},{6,7},{7,6},{8,9},{9,8},{10,11... | collective-permute-start | bytes 1032200 | tf_op jit(solution)/shard_map/ppermute | solution.py:958
  60.8 31.1 %collective-permute-start = (bf16[4,24,3584]{2,1,0:T(8,128)(2,1)S(1)}, bf16[4,24,3584]{2,1,0:T(8,128)(2,1)S(1)}, u32[]{:S(2)}, u32[]{:S(2)}) collective-permute-start(bf16[4,24,3584]{2,1,0:T(8,128)(2,1)S(1)} %all-to-all-done.2.refs_0_), channel_id=1, source_target_pairs={{0,2},{1,3},{2,0},{3,1},{4,6},{5,7},{6,4},{7,5},{8,10},{9,11},{10,... | collective-permute-start | bytes 2064392 | tf_op jit(solution)/shard_map/ppermute | solution.py:958
  61.4 32.3 %collective-permute-start.1 = (bf16[4,24,3584]{2,1,0:T(8,128)(2,1)S(1)}, bf16[4,24,3584]{2,1,0:T(8,128)(2,1)S(1)}, u32[]{:S(2)}, u32[]{:S(2)}) collective-permute-start(bf16[4,24,3584]{2,1,0:T(8,128)(2,1)S(1)} %all-to-all-done.2.refs_0_), channel_id=1, source_target_pairs={{0,4},{1,5},{2,6},{3,7},{4,0},{5,1},{6,2},{7,3},{8,12},{9,13},{10,... | collective-permute-start | bytes 2064392 | tf_op jit(solution)/shard_map/ppermute | solution.py:958
  62.9 30.8 %collective-permute-start.2 = (bf16[4,24,3584]{2,1,0:T(8,128)(2,1)S(1)}, bf16[4,24,3584]{2,1,0:T(8,128)(2,1)S(1)}, u32[]{:S(2)}, u32[]{:S(2)}) collective-permute-start(bf16[4,24,3584]{2,1,0:T(8,128)(2,1)S(1)} %all-to-all-done.2.refs_0_), channel_id=1, source_target_pairs={{0,6},{1,7},{2,4},{3,5},{4,2},{5,3},{6,0},{7,1},{8,14},{9,15},{10,... | collective-permute-start | bytes 2064392 | tf_op jit(solution)/shard_map/ppermute | solution.py:958
  134.7 16.7 %collective-permute-start.22 = (bf16[4,24,1536]{2,1,0:T(8,128)(2,1)S(1)}, bf16[4,24,1536]{2,1,0:T(8,128)(2,1)S(1)}, u32[]{:S(2)}, u32[]{:S(2)}) collective-permute-start(bf16[4,24,1536]{2,1,0:T(8,128)(2,1)S(1)} %get-tuple-element.193), channel_id=1, source_target_pairs={{0,2},{1,3},{2,0},{3,1},{4,6},{5,7},{6,4},{7,5},{8,10},{9,11},{10,... | collective-permute-start | bytes 884744 | tf_op jit(solution)/shard_map/ppermute | solution.py:958
  136.2 15.2 %collective-permute-start.23 = (bf16[4,24,1536]{2,1,0:T(8,128)(2,1)S(1)}, bf16[4,24,1536]{2,1,0:T(8,128)(2,1)S(1)}, u32[]{:S(2)}, u32[]{:S(2)}) collective-permute-start(bf16[4,24,1536]{2,1,0:T(8,128)(2,1)S(1)} %get-tuple-element.194), channel_id=1, source_target_pairs={{0,4},{1,5},{2,6},{3,7},{4,0},{5,1},{6,2},{7,3},{8,12},{9,13},{10,... | collective-permute-start | bytes 884744 | tf_op jit(solution)/shard_map/ppermute | solution.py:958
  136.8 14.6 %collective-permute-start.24 = (bf16[4,24,1536]{2,1,0:T(8,128)(2,1)S(1)}, bf16[4,24,1536]{2,1,0:T(8,128)(2,1)S(1)}, u32[]{:S(2)}, u32[]{:S(2)}) collective-permute-start(bf16[4,24,1536]{2,1,0:T(8,128)(2,1)S(1)} %get-tuple-element.195), channel_id=1, source_target_pairs={{0,6},{1,7},{2,4},{3,5},{4,2},{5,3},{6,0},{7,1},{8,14},{9,15},{10,... | collective-permute-start | bytes 884744 | tf_op jit(solution)/shard_map/ppermute | solution.py:958
  155.4 19.5 %collective-permute-start.29 = (bf16[5,24,896]{2,1,0:T(8,128)(2,1)S(1)}, bf16[5,24,896]{2,1,0:T(8,128)(2,1)S(1)}, u32[]{:S(2)}, u32[]{:S(2)}) collective-permute-start(bf16[5,24,896]{2,1,0:T(8,128)(2,1)S(1)} %get-tuple-element.217), channel_id=1, source_target_pairs={{0,2},{1,3},{2,0},{3,1},{4,6},{5,7},{6,4},{7,5},{8,10},{9,11},{10,... | collective-permute-start | bytes 645128 | tf_op jit(solution)/shard_map/ppermute | solution.py:958
  156.9 18.1 %collective-permute-start.30 = (bf16[5,24,896]{2,1,0:T(8,128)(2,1)S(1)}, bf16[5,24,896]{2,1,0:T(8,128)(2,1)S(1)}, u32[]{:S(2)}, u32[]{:S(2)}) collective-permute-start(bf16[5,24,896]{2,1,0:T(8,128)(2,1)S(1)} %get-tuple-element.218), channel_id=1, source_target_pairs={{0,4},{1,5},{2,6},{3,7},{4,0},{5,1},{6,2},{7,3},{8,12},{9,13},{10,... | collective-permute-start | bytes 645128 | tf_op jit(solution)/shard_map/ppermute | solution.py:958
  157.5 17.6 %collective-permute-start.31 = (bf16[5,24,896]{2,1,0:T(8,128)(2,1)S(1)}, bf16[5,24,896]{2,1,0:T(8,128)(2,1)S(1)}, u32[]{:S(2)}, u32[]{:S(2)}) collective-permute-start(bf16[5,24,896]{2,1,0:T(8,128)(2,1)S(1)} %get-tuple-element.219), channel_id=1, source_target_pairs={{0,6},{1,7},{2,4},{3,5},{4,2},{5,3},{6,0},{7,1},{8,14},{9,15},{10,... | collective-permute-start | bytes 645128 | tf_op jit(solution)/shard_map/ppermute | solution.py:958
  158.9 16.0 %collective-permute-start.27 = (bf16[24,1536]{1,0:T(8,128)(2,1)S(1)}, bf16[24,1536]{1,0:T(8,128)(2,1)S(1)}, u32[]{:S(2)}, u32[]{:S(2)}) collective-permute-start(bf16[24,1536]{1,0:T(8,128)(2,1)S(1)} %get-tuple-element.214), channel_id=1, source_target_pairs={{0,16},{1,17},{2,18},{3,19},{4,20},{5,21},{6,22},{7,23},{8,24},{9,... | collective-permute-start | bytes 221192 | tf_op jit(solution)/shard_map/ppermute | solution.py:1000
  161.3 13.7 %collective-permute-start.28 = (bf16[24,1536]{1,0:T(8,128)(2,1)S(1)}, bf16[24,1536]{1,0:T(8,128)(2,1)S(1)}, u32[]{:S(2)}, u32[]{:S(2)}) collective-permute-start(bf16[24,1536]{1,0:T(8,128)(2,1)S(1)} %get-tuple-element.215), channel_id=1, source_target_pairs={{0,24},{1,25},{2,26},{3,27},{4,28},{5,29},{6,30},{7,31},{8,0},{9,1... | collective-permute-start | bytes 221192 | tf_op jit(solution)/shard_map/ppermute | solution.py:1000
  179.6 23.6 %collective-permute-start.36 = (bf16[4,24,1536]{2,1,0:T(8,128)(2,1)S(1)}, bf16[4,24,1536]{2,1,0:T(8,128)(2,1)S(1)}, u32[]{:S(2)}, u32[]{:S(2)}) collective-permute-start(bf16[4,24,1536]{2,1,0:T(8,128)(2,1)S(1)} %get-tuple-element.243), channel_id=1, source_target_pairs={{0,2},{1,3},{2,0},{3,1},{4,6},{5,7},{6,4},{7,5},{8,10},{9,11},{10,... | collective-permute-start | bytes 884744 | tf_op jit(solution)/shard_map/ppermute | solution.py:958
  181.2 22.1 %collective-permute-start.37 = (bf16[4,24,1536]{2,1,0:T(8,128)(2,1)S(1)}, bf16[4,24,1536]{2,1,0:T(8,128)(2,1)S(1)}, u32[]{:S(2)}, u32[]{:S(2)}) collective-permute-start(bf16[4,24,1536]{2,1,0:T(8,128)(2,1)S(1)} %get-tuple-element.244), channel_id=1, source_target_pairs={{0,4},{1,5},{2,6},{3,7},{4,0},{5,1},{6,2},{7,3},{8,12},{9,13},{10,... | collective-permute-start | bytes 884744 | tf_op jit(solution)/shard_map/ppermute | solution.py:958
  181.7 21.6 %collective-permute-start.38 = (bf16[4,24,1536]{2,1,0:T(8,128)(2,1)S(1)}, bf16[4,24,1536]{2,1,0:T(8,128)(2,1)S(1)}, u32[]{:S(2)}, u32[]{:S(2)}) collective-permute-start(bf16[4,24,1536]{2,1,0:T(8,128)(2,1)S(1)} %get-tuple-element.245), channel_id=1, source_target_pairs={{0,6},{1,7},{2,4},{3,5},{4,2},{5,3},{6,0},{7,1},{8,14},{9,15},{10,... | collective-permute-start | bytes 884744 | tf_op jit(solution)/shard_map/ppermute | solution.py:958
  183.2 20.1 %collective-permute-start.34 = (bf16[24,2432]{1,0:T(8,128)(2,1)S(1)}, bf16[24,2432]{1,0:T(8,128)(2,1)S(1)}, u32[]{:S(2)}, u32[]{:S(2)}) collective-permute-start(bf16[24,2432]{1,0:T(8,128)(2,1)S(1)} %get-tuple-element.240), channel_id=1, source_target_pairs={{0,16},{1,17},{2,18},{3,19},{4,20},{5,21},{6,22},{7,23},{8,24},{9,... | collective-permute-start | bytes 350216 | tf_op jit(solution)/shard_map/ppermute | solution.py:1000
  186.1 17.2 %collective-permute-start.35 = (bf16[24,2432]{1,0:T(8,128)(2,1)S(1)}, bf16[24,2432]{1,0:T(8,128)(2,1)S(1)}, u32[]{:S(2)}, u32[]{:S(2)}) collective-permute-start(bf16[24,2432]{1,0:T(8,128)(2,1)S(1)} %get-tuple-element.241), channel_id=1, source_target_pairs={{0,24},{1,25},{2,26},{3,27},{4,28},{5,29},{6,30},{7,31},{8,0},{9,1... | collective-permute-start | bytes 350216 | tf_op jit(solution)/shard_map/ppermute | solution.py:1000
  (63 other events, 500.0 us)

commit v5 on v4

--- a/solution.py
+++ b/solution.py
@@ -620,7 +620,7 @@
             per_slot(FF),
             per_slot(D),
         ),
-        compiler_params=params_of(1),
+        compiler_params=params_of(1, 36),
         cost_estimate=cost(5 * 10**9, 20 * 2**20),
         name="forward_block",
     )(counts, hidden, cond, left, right, down, bias)
@@ -722,7 +722,7 @@
             whole(4, 4, rows, 4 * D),
         ),
         scratch_shapes=[pltpu.VMEM((D, FF), F32), pltpu.VMEM((FF, D), F32)],
-        compiler_params=params_of(1),
+        compiler_params=params_of(1, 36),
         cost_estimate=cost(8 * 10**9, 20 * 2**20),
         name="ffn_backward",
     )(core, counts, upstream, branch, active, slope, middle, mod, right, down)
@@ -1028,8 +1028,8 @@
         core, d_middle, hidden[0], records[0], weights[0], d_mod, bias, condition, d_cond, chips, True
     )
     wire, attn_last, ffn_first = tie((wire, attn_last, ffn_first))
-    attn_first = in_plane(paired(*wire))
-    ffn_first = in_line(plane_sums(ffn_first))
+    both, sums = tie((paired(*wire), plane_sums(ffn_first)))
+    attn_first, ffn_first = in_plane(both), in_line(sums)
     attn_first = in_line(with_mods(attn_first))
     width = 2 * D + 128
     own_ffn = jnp.stack([total(ffn_first), total(ffn_last)])

time: 247 us -> 239 us (0.968)
  waiting for transfers between devices: 64.4 us -> 55.8 us
    ppermute x33, waiting for transfers between devices: 31.5 us -> 26 us  [along(): lax.ppermute(value, 'fsdp', [(one, one ^ bit) for one in range(devices)])]
    ppermute x12, waiting for transfers between devices: 17.4 us -> 12 us  [shifted(): lax.ppermute(value, 'fsdp', [(one, (one + 8 * step) % devices) for one in...]
  transfers between devices with their start and end apart: 53 -> 53, of which waited for: 21 -> 21; matrix products, arithmetic and copies ran while one was open for 0% -> 0% of each run, Pallas kernels for 24% -> 25%
where the time goes in v5:
time: 239 us; the launch traced here: 238 us
  Pallas kernels  95.4 us (40%)
  waiting for transfers between devices  55.8 us (23%)
  starting transfers between devices  51.5 us (22%)
  blocking collectives  17 us (7%)
  local copies, waits for them, and re-layouts  14.8 us (6%)
    pallas_call x2, Pallas kernels, forward_block(): pl.pallas_call(functools.partial(forward_kernel, last=last), grid=(SLOT /...  31.8 us
    pallas_call x2, Pallas kernels, attention_backward(): pl.pallas_call(functools.partial(attention_kernel, chips, first=first), g...  29.9 us
    ppermute x33, starting transfers between devices, along(): lax.ppermute(value, 'fsdp', [(one, one ^ bit) for one in range(devices)])  27.3 us
    ppermute x33, waiting for transfers between devices, along(): lax.ppermute(value, 'fsdp', [(one, one ^ bit) for one in range(devices)])  26 us
    pallas_call x2, Pallas kernels, ffn_backward(): pl.pallas_call(functools.partial(ffn_kernel, chips, last=last), grid=(SLO...  21.1 us
    all_to_all x1, blocking collectives, stacked(): lax.all_to_all(copies, 'fsdp', 0, 0, axis_index_groups=lines, tiled=True)  17 us
    ppermute x12, starting transfers between devices, shifted(): lax.ppermute(value, 'fsdp', [(one, (one + 8 * step) % devices) for one in...  16.3 us
    unnamed x74, local copies, waits for them, and re-layouts  14.7 us
  transfers between devices with their start and end apart: 53, of which 21 were waited for; matrix products, arithmetic and copies ran while one was open for 0% of the time, Pallas kernels for 25%

profile of v5, /device:TPU:0, one launch (start us, length us, event | category | flops | bytes accessed | tf_op | source)
XLA Modules:
  0.0 238.4 jit_solution(2366704043745566948)
XLA Ops:
  0.6 2.9 %pack.1 = (bf16[4,24,1792]{2,1,0:T(8,128)(2,1)}, bf16[4,24,1792]{2,1,0:T(8,128)(2,1)}, bf16[4,24,3584]{2,1,0:T(8,128)(2,1)}) custom-call(bf16[2,27648]{1,0:T(2,128)(2,1)} %ada_in.1, bf16[2,13824]{1,0:T(2,128)(2,1)} %qkv_in.1, bf16[2,4608]{1,0:T(2,128)(2,1)} %proj_in.1, bf16[2,18432]{1,0:T(2,128)(2,1)} %fc1_in.1, bf16[2,18432]{1,0:T(2,128)(2,1)} %fc2_in.1, ...), custom_call_target="tpu_custom_call" | custom-call | tf_op jit(solution)/shard_map/pack/pallas_call | solution.py:380
  3.6 17.0 %all_to_all.15.refs_0_ = bf16[4,24,1792]{2,1,0:T(8,128)(2,1)S(1)} all-to-all(bf16[4,24,1792]{2,1,0:T(8,128)(2,1)} %get-tuple-element.146), channel_id=1, replica_groups={{0,8,16,24},{1,9,17,25},{2,10,18,26},{3,11,19,27},{4,12,20,28},{5,13,21..., dimensions={0} | all-to-all | bytes 688128 | tf_op jit(solution)/shard_map/all_to_all | solution.py:961
  20.5 3.5 %all-to-all-start.1 = ((bf16[4,24,1792]{2,1,0:T(8,128)(2,1)}), bf16[4,24,1792]{2,1,0:T(8,128)(2,1)S(1)}, u32[]{:S(2)}, u32[]{:S(2)}) async-start(bf16[4,24,1792]{2,1,0:T(8,128)(2,1)} %get-tuple-element.148), calls=%async_computation.1 | async-start | bytes 688128 | tf_op jit(solution)/shard_map/all_to_all | solution.py:961
  27.6 6.2 %all-to-all-done.1.refs_8_ = bf16[4,24,1792]{2,1,0:T(8,128)(2,1)S(1)} async-done(((bf16[4,24,1792]{2,1,0:T(8,128)(2,1)}), bf16[4,24,1792]{2,1,0:T(8,128)(2,1)S(1)}, u32[]{:S(2)}, u32[]{:S(2)}) %all-to-all-start.1) | async-done | bytes 344096 | tf_op jit(solution)/shard_map/all_to_all | solution.py:961
  33.8 3.5 %all-to-all-start.2 = ((bf16[4,24,3584]{2,1,0:T(8,128)(2,1)}), bf16[4,24,3584]{2,1,0:T(8,128)(2,1)S(1)}, u32[]{:S(2)}, u32[]{:S(2)}) async-start(bf16[4,24,3584]{2,1,0:T(8,128)(2,1)} %get-tuple-element.150), calls=%async_computation.2 | async-start | bytes 1376256 | tf_op jit(solution)/shard_map/all_to_all | solution.py:961
  37.3 4.1 %collective-permute-done.4.refs_2_ = bf16[4,24,1792]{2,1,0:T(8,128)(2,1)S(1)} collective-permute-done((bf16[4,24,1792]{2,1,0:T(8,128)(2,1)S(1)}, bf16[4,24,1792]{2,1,0:T(8,128)(2,1)S(1)}, u32[]{:S(2)}, u32[]{:S(2)}) %collective-permute-start.4) | collective-permute-done | bytes 344096 | tf_op jit(solution)/shard_map/ppermute | solution.py:958
  45.4 7.0 %collective-permute-done.10.refs_9_ = bf16[4,24,1792]{2,1,0:T(8,128)(2,1)S(1)} collective-permute-done((bf16[4,24,1792]{2,1,0:T(8,128)(2,1)S(1)}, bf16[4,24,1792]{2,1,0:T(8,128)(2,1)S(1)}, u32[]{:S(2)}, u32[]{:S(2)}) %collective-permute-start.10) | collective-permute-done | bytes 344096 | tf_op jit(solution)/shard_map/ppermute | solution.py:958
  52.4 5.1 %collective-permute-done.11.refs_10_ = bf16[4,24,1792]{2,1,0:T(8,128)(2,1)S(1)} collective-permute-done((bf16[4,24,1792]{2,1,0:T(8,128)(2,1)S(1)}, bf16[4,24,1792]{2,1,0:T(8,128)(2,1)S(1)}, u32[]{:S(2)}, u32[]{:S(2)}) %collective-permute-start.11) | collective-permute-done | bytes 344096 | tf_op jit(solution)/shard_map/ppermute | solution.py:958
  67.9 3.1 %unpack.2 = (bf16[384,2688]{1,0:T(8,128)(2,1)S(1)}, bf16[384,2688]{1,0:T(8,128)(2,1)S(1)}, bf16[1536,384]{1,0:T(8,128)(2,1)S(1)}, f32[1,5376]{1,0:T(1,128)S(1)}, f32[2,64,384]{2,1,0:T(8,128)S(1)}) custom-call(s32[3]{0:T(128)S(1)} %pad_add_fusion.place.core, bf16[4,24,1792]{2,1,0:T(8,128)(2,1)S(1)} %all_to_all.15.refs_0_, ...), custom_call_target="tpu_custom_call" | custom-call | tf_op jit(solution)/shard_map/unpack/pallas_call | solution.py:438
  71.7 15.8 %forward_block.2 = (f32[4,256,384]{2,1,0:T(8,128)S(1)}, f32[4,2304]{1,0:T(4,128)S(1)}, bf16[4,256,1152]{2,1,0:T(8,128)(2,1)S(1)}, bf16[4,256,384]{2,1,0:T(8,128)...) custom-call(s32[1]{0:T(128)S(6)} %copy.47.counts, ...), custom_call_target="tpu_custom_call" | custom-call | flops 5000000000 | bytes 20971520 | tf_op jit(solution)/shard_map/forward_block/pallas_call | solution.py:589
  98.8 3.9 %unpack.3 = (bf16[384,2688]{1,0:T(8,128)(2,1)S(1)}, bf16[384,2688]{1,0:T(8,128)(2,1)S(1)}, bf16[1536,384]{1,0:T(8,128)(2,1)S(1)}, f32[1,5376]{1,0:T(1,128)S(1)}, f32[2,64,384]{2,1,0:T(8,128)}) custom-call(s32[3]{0:T(128)S(1)} %pad_add_fusion.place.core, bf16[4,24,3584]{2,1,0:T(8,128)(2,1)S(1)} %all-to-all-done.2.refs_0_, ...), custom_call_target="tpu_custom_call" | custom-call | tf_op jit(solution)/shard_map/unpack/pallas_call | solution.py:438
  102.7 16.0 %forward_block.3 = (f32[4,256,384]{2,1,0:T(8,128)}, f32[4,2304]{1,0:T(4,128)S(1)}, bf16[4,256,1152]{2,1,0:T(8,128)(2,1)S(1)}, bf16[4,256,384]{2,1,0:T(8,128)(2,1...) custom-call(s32[1]{0:T(128)S(6)} %copy.47.counts, ...), custom_call_target="tpu_custom_call" | custom-call | flops 5000000000 | bytes 20971520 | tf_op jit(solution)/shard_map/forward_block/pallas_call | solution.py:589
  121.3 10.1 %ffn_backward.2 = (f32[4,256,384]{2,1,0:T(8,128)S(1)}, f32[24,384]{1,0:T(8,128)S(1)}, f32[1,1920]{1,0:T(1,128)S(1)}, bf16[4,4,24,1536]{3,2,1,0:T(8,128)(2,1)S(1)}, bf16[4,4,24,1536]{3,2,1,0:T(8,128)(2,1)S(1)}) custom-call(s32[3]{0:T(128)S(1)} %pad_add_fusion.place.core, s32[1]{0:T(128)S(6)} %copy.47.counts, bf16[4,256,384]{2,1,0:T(8,128)(2,1)S(1)} %copy-done.13, ...), custom_call_target="tpu_custom_call" | custom-call | flops 8000000000 | bytes 20971520 | tf_op jit(solution)/shard_map/ffn_backward/pallas_call | solution.py:695
  131.6 2.7 %collective-permute-done.21 = bf16[4,4,24,1536]{3,2,1,0:T(8,128)(2,1)S(1)} collective-permute-done((bf16[4,4,24,1536]{3,2,1,0:T(8,128)(2,1)S(1)}, bf16[4,4,24,1536]{3,2,1,0:T(8,128)(2,1)S(1)}, u32[]{:S(2)}, u32[]{:S(2)}) %collective-permute-start.21) | collective-permute-done | bytes 1179680 | tf_op jit(solution)/shard_map/ppermute | solution.py:992
  138.3 13.1 %attention_backward.2 = (f32[4,256,384]{2,1,0:T(8,128)S(1)}, f32[4,384]{1,0:T(4,128)S(1)}, bf16[4,5,24,896]{3,2,1,0:T(8,128)(2,1)S(1)}, bf16[4,5,24,896]{3,2,1,0:T(8,128)(2,1)S(1)}) custom-call(s32[3]{0:T(128)S(1)} %pad_add_fusion.place.core, f32[4,256,384]{2,1,0:T(8,128)S(1)} %get-tuple-element.191.d_middle, f32[4,256,384]{2,1,0:T(8,128)S(1)} %copy-done.22, ...), custom_call_target="tpu_custom_call" | custom-call | flops 6000000000 | bytes 20971520 | tf_op jit(solution)/shard_map/attention_backward/pallas_call | solution.py:832
  158.9 2.4 collective-permute-start.27
  162.8 11.0 %ffn_backward.3 = (f32[4,256,384]{2,1,0:T(8,128)S(1)}, f32[24,384]{1,0:T(8,128)S(1)}, f32[1,1920]{1,0:T(1,128)S(1)}, bf16[4,4,24,1536]{3,2,1,0:T(8,128)(2,1)S(1)}, bf16[4,4,24,1536]{3,2,1,0:T(8,128)(2,1)}) custom-call(s32[3]{0:T(128)S(1)} %pad_add_fusion.place.core, s32[1]{0:T(128)S(6)} %copy.47.counts, f32[4,256,384]{2,1,0:T(8,128)S(1)} %get-tuple-element.211.upstream, ...), custom_call_target="tpu_custom_call" | custom-call | flops 8000000000 | bytes 20971520 | tf_op jit(solution)/shard_map/ffn_backward/pallas_call | solution.py:695
  175.9 2.8 %collective-permute-done.32 = bf16[4,4,24,1536]{3,2,1,0:T(8,128)(2,1)S(1)} collective-permute-done((bf16[4,4,24,1536]{3,2,1,0:T(8,128)(2,1)}, bf16[4,4,24,1536]{3,2,1,0:T(8,128)(2,1)S(1)}, u32[]{:S(2)}, u32[]{:S(2)}) %collective-permute-start.32) | collective-permute-done | bytes 1179680 | tf_op jit(solution)/shard_map/ppermute | solution.py:992
  186.5 16.8 %attention_backward.3 = (f32[4,256,384]{2,1,0:T(8,128)}, f32[4,384]{1,0:T(4,128)}, bf16[4,5,24,896]{3,2,1,0:T(8,128)(2,1)}, bf16[4,5,24,896]{3,2,1,0:T(8,128)(2,1)}) custom-call(s32[3]{0:T(128)S(1)} %pad_add_fusion.place.core, f32[4,256,384]{2,1,0:T(8,128)} %copy-done.24, bf16[4,256,384]{2,1,0:T(8,128)(2,1)S(1)} %copy-done.15, ...), custom_call_target="tpu_custom_call" | custom-call | flops 6000000000 | bytes 20971520 | tf_op jit(solution)/shard_map/attention_backward/pallas_call | solution.py:832
  211.2 2.9 %collective-permute-start.42 = (bf16[24,1536]{1,0:T(8,128)(2,1)S(1)}, bf16[24,1536]{1,0:T(8,128)(2,1)S(1)}, u32[]{:S(2)}, u32[]{:S(2)}) collective-permute-start(bf16[24,1536]{1,0:T(8,128)(2,1)S(1)} %get-tuple-element.263), channel_id=1, source_target_pairs={{0,24},{1,25},{2,26},{3,27},{4,28},{5,29},{6,30},{7,31},{8,0},{9,1... | collective-permute-start | bytes 221192 | tf_op jit(solution)/shard_map/ppermute | solution.py:1000
  219.1 2.8 %collective-permute-done.43 = bf16[5,24,896]{2,1,0:T(8,128)(2,1)S(1)} collective-permute-done((bf16[5,24,896]{2,1,0:T(8,128)(2,1)S(1)}, bf16[5,24,896]{2,1,0:T(8,128)(2,1)S(1)}, u32[]{:S(2)}, u32[]{:S(2)}) %collective-permute-start.43) | collective-permute-done | bytes 215072 | tf_op jit(solution)/shard_map/ppermute | solution.py:958
  222.2 2.6 %collective-permute-start.47 = (bf16[24,2432]{1,0:T(8,128)(2,1)S(1)}, bf16[24,2432]{1,0:T(8,128)(2,1)S(1)}, u32[]{:S(2)}, u32[]{:S(2)}) collective-permute-start(bf16[24,2432]{1,0:T(8,128)(2,1)S(1)} %get-tuple-element.315), channel_id=1, source_target_pairs={{0,16},{1,17},{2,18},{3,19},{4,20},{5,21},{6,22},{7,23},{8,24},{9,... | collective-permute-start | bytes 350216 | tf_op jit(solution)/shard_map/ppermute | solution.py:1000
  229.0 4.1 %collective-permute-done.47 = bf16[24,2432]{1,0:T(8,128)(2,1)S(1)} collective-permute-done((bf16[24,2432]{1,0:T(8,128)(2,1)S(1)}, bf16[24,2432]{1,0:T(8,128)(2,1)S(1)}, u32[]{:S(2)}, u32[]{:S(2)}) %collective-permute-start.47) | collective-permute-done | bytes 116768 | tf_op jit(solution)/shard_map/ppermute | solution.py:1000
  235.6 2.8 %finish.1 = (f32[2,27648]{1,0:T(2,128)}, f32[2,13824]{1,0:T(2,128)}, f32[2,4608]{1,0:T(2,128)}, f32[2,18432]{1,0:T(2,128)}, f32[2,18432]{1,0:T(2,128)}, /*index=5*/f32[2,256]{1,0:T(2,128)}) custom-call(s32[3]{0:T(128)S(1)} %pad_add_fusion.place.core, f32[2,24,1536]{2,1,0:T(8,128)S(1)} %pad_maximum_fusion.1.own_ffn, ...), custom_call_target="tpu_custom_call" | custom-call | tf_op jit(solution)/shard_map/finish/pallas_call | solution.py:934
  (202 shorter events, 74.5 us)
Async XLA Ops:
  20.5 13.2 %all-to-all-start.1 = ((bf16[4,24,1792]{2,1,0:T(8,128)(2,1)}), bf16[4,24,1792]{2,1,0:T(8,128)(2,1)S(1)}, u32[]{:S(2)}, u32[]{:S(2)}) async-start(bf16[4,24,1792]{2,1,0:T(8,128)(2,1)} %get-tuple-element.148), calls=%async_computation.1 | async-start | bytes 688128 | tf_op jit(solution)/shard_map/all_to_all | solution.py:961
  24.0 13.3 %collective-permute-start.3 = (bf16[4,24,1792]{2,1,0:T(8,128)(2,1)S(1)}, bf16[4,24,1792]{2,1,0:T(8,128)(2,1)S(1)}, u32[]{:S(2)}, u32[]{:S(2)}) collective-permute-start(bf16[4,24,1792]{2,1,0:T(8,128)(2,1)S(1)} %all_to_all.15.refs_0_), channel_id=1, source_target_pairs={{0,2},{1,3},{2,0},{3,1},{4,6},{5,7},{6,4},{7,5},{8,10},{9,11},{10,... | collective-permute-start | bytes 1032200 | tf_op jit(solution)/shard_map/ppermute | solution.py:958
  25.6 15.8 %collective-permute-start.4 = (bf16[4,24,1792]{2,1,0:T(8,128)(2,1)S(1)}, bf16[4,24,1792]{2,1,0:T(8,128)(2,1)S(1)}, u32[]{:S(2)}, u32[]{:S(2)}) collective-permute-start(bf16[4,24,1792]{2,1,0:T(8,128)(2,1)S(1)} %all_to_all.15.refs_0_), channel_id=1, source_target_pairs={{0,4},{1,5},{2,6},{3,7},{4,0},{5,1},{6,2},{7,3},{8,12},{9,13},{10,... | collective-permute-start | bytes 1032200 | tf_op jit(solution)/shard_map/ppermute | solution.py:958
  27.1 14.3 %collective-permute-start.5 = (bf16[4,24,1792]{2,1,0:T(8,128)(2,1)S(1)}, bf16[4,24,1792]{2,1,0:T(8,128)(2,1)S(1)}, u32[]{:S(2)}, u32[]{:S(2)}) collective-permute-start(bf16[4,24,1792]{2,1,0:T(8,128)(2,1)S(1)} %all_to_all.15.refs_0_), channel_id=1, source_target_pairs={{0,6},{1,7},{2,4},{3,5},{4,2},{5,3},{6,0},{7,1},{8,14},{9,15},{10,... | collective-permute-start | bytes 1032200 | tf_op jit(solution)/shard_map/ppermute | solution.py:958
  33.8 27.0 %all-to-all-start.2 = ((bf16[4,24,3584]{2,1,0:T(8,128)(2,1)}), bf16[4,24,3584]{2,1,0:T(8,128)(2,1)S(1)}, u32[]{:S(2)}, u32[]{:S(2)}) async-start(bf16[4,24,3584]{2,1,0:T(8,128)(2,1)} %get-tuple-element.150), calls=%async_computation.2 | async-start | bytes 1376256 | tf_op jit(solution)/shard_map/all_to_all | solution.py:961
  42.6 14.9 %collective-permute-start.11 = (bf16[4,24,1792]{2,1,0:T(8,128)(2,1)S(1)}, bf16[4,24,1792]{2,1,0:T(8,128)(2,1)S(1)}, u32[]{:S(2)}, u32[]{:S(2)}) collective-permute-start(bf16[4,24,1792]{2,1,0:T(8,128)(2,1)S(1)} %all-to-all-done.1.refs_8_), channel_id=1, source_target_pairs={{0,4},{1,5},{2,6},{3,7},{4,0},{5,1},{6,2},{7,3},{8,12},{9,13},{10,... | collective-permute-start | bytes 1032200 | tf_op jit(solution)/shard_map/ppermute | solution.py:958
  43.4 14.0 %collective-permute-start.12 = (bf16[4,24,1792]{2,1,0:T(8,128)(2,1)S(1)}, bf16[4,24,1792]{2,1,0:T(8,128)(2,1)S(1)}, u32[]{:S(2)}, u32[]{:S(2)}) collective-permute-start(bf16[4,24,1792]{2,1,0:T(8,128)(2,1)S(1)} %all-to-all-done.1.refs_8_), channel_id=1, source_target_pairs={{0,6},{1,7},{2,4},{3,5},{4,2},{5,3},{6,0},{7,1},{8,14},{9,15},{10,... | collective-permute-start | bytes 1032200 | tf_op jit(solution)/shard_map/ppermute | solution.py:958
  44.9 13.9 %collective-permute-start.6 = (bf16[4,24,1792]{2,1,0:T(8,128)(2,1)S(1)}, bf16[4,24,1792]{2,1,0:T(8,128)(2,1)S(1)}, u32[]{:S(2)}, u32[]{:S(2)}) collective-permute-start(bf16[4,24,1792]{2,1,0:T(8,128)(2,1)S(1)} %all_to_all.15.refs_0_), channel_id=1, source_target_pairs={{0,1},{1,0},{2,3},{3,2},{4,5},{5,4},{6,7},{7,6},{8,9},{9,8},{10,11... | collective-permute-start | bytes 1032200 | tf_op jit(solution)/shard_map/ppermute | solution.py:958
  60.8 31.1 %collective-permute-start = (bf16[4,24,3584]{2,1,0:T(8,128)(2,1)S(1)}, bf16[4,24,3584]{2,1,0:T(8,128)(2,1)S(1)}, u32[]{:S(2)}, u32[]{:S(2)}) collective-permute-start(bf16[4,24,3584]{2,1,0:T(8,128)(2,1)S(1)} %all-to-all-done.2.refs_0_), channel_id=1, source_target_pairs={{0,2},{1,3},{2,0},{3,1},{4,6},{5,7},{6,4},{7,5},{8,10},{9,11},{10,... | collective-permute-start | bytes 2064392 | tf_op jit(solution)/shard_map/ppermute | solution.py:958
  61.4 32.3 %collective-permute-start.1 = (bf16[4,24,3584]{2,1,0:T(8,128)(2,1)S(1)}, bf16[4,24,3584]{2,1,0:T(8,128)(2,1)S(1)}, u32[]{:S(2)}, u32[]{:S(2)}) collective-permute-start(bf16[4,24,3584]{2,1,0:T(8,128)(2,1)S(1)} %all-to-all-done.2.refs_0_), channel_id=1, source_target_pairs={{0,4},{1,5},{2,6},{3,7},{4,0},{5,1},{6,2},{7,3},{8,12},{9,13},{10,... | collective-permute-start | bytes 2064392 | tf_op jit(solution)/shard_map/ppermute | solution.py:958
  62.9 30.8 %collective-permute-start.2 = (bf16[4,24,3584]{2,1,0:T(8,128)(2,1)S(1)}, bf16[4,24,3584]{2,1,0:T(8,128)(2,1)S(1)}, u32[]{:S(2)}, u32[]{:S(2)}) collective-permute-start(bf16[4,24,3584]{2,1,0:T(8,128)(2,1)S(1)} %all-to-all-done.2.refs_0_), channel_id=1, source_target_pairs={{0,6},{1,7},{2,4},{3,5},{4,2},{5,3},{6,0},{7,1},{8,14},{9,15},{10,... | collective-permute-start | bytes 2064392 | tf_op jit(solution)/shard_map/ppermute | solution.py:958
  134.7 16.7 %collective-permute-start.22 = (bf16[4,24,1536]{2,1,0:T(8,128)(2,1)S(1)}, bf16[4,24,1536]{2,1,0:T(8,128)(2,1)S(1)}, u32[]{:S(2)}, u32[]{:S(2)}) collective-permute-start(bf16[4,24,1536]{2,1,0:T(8,128)(2,1)S(1)} %get-tuple-element.201), channel_id=1, source_target_pairs={{0,2},{1,3},{2,0},{3,1},{4,6},{5,7},{6,4},{7,5},{8,10},{9,11},{10,... | collective-permute-start | bytes 884744 | tf_op jit(solution)/shard_map/ppermute | solution.py:958
  136.2 15.2 %collective-permute-start.23 = (bf16[4,24,1536]{2,1,0:T(8,128)(2,1)S(1)}, bf16[4,24,1536]{2,1,0:T(8,128)(2,1)S(1)}, u32[]{:S(2)}, u32[]{:S(2)}) collective-permute-start(bf16[4,24,1536]{2,1,0:T(8,128)(2,1)S(1)} %get-tuple-element.202), channel_id=1, source_target_pairs={{0,4},{1,5},{2,6},{3,7},{4,0},{5,1},{6,2},{7,3},{8,12},{9,13},{10,... | collective-permute-start | bytes 884744 | tf_op jit(solution)/shard_map/ppermute | solution.py:958
  136.8 14.6 %collective-permute-start.24 = (bf16[4,24,1536]{2,1,0:T(8,128)(2,1)S(1)}, bf16[4,24,1536]{2,1,0:T(8,128)(2,1)S(1)}, u32[]{:S(2)}, u32[]{:S(2)}) collective-permute-start(bf16[4,24,1536]{2,1,0:T(8,128)(2,1)S(1)} %get-tuple-element.203), channel_id=1, source_target_pairs={{0,6},{1,7},{2,4},{3,5},{4,2},{5,3},{6,0},{7,1},{8,14},{9,15},{10,... | collective-permute-start | bytes 884744 | tf_op jit(solution)/shard_map/ppermute | solution.py:958
  155.4 19.5 %collective-permute-start.29 = (bf16[5,24,896]{2,1,0:T(8,128)(2,1)S(1)}, bf16[5,24,896]{2,1,0:T(8,128)(2,1)S(1)}, u32[]{:S(2)}, u32[]{:S(2)}) collective-permute-start(bf16[5,24,896]{2,1,0:T(8,128)(2,1)S(1)} %get-tuple-element.225), channel_id=1, source_target_pairs={{0,2},{1,3},{2,0},{3,1},{4,6},{5,7},{6,4},{7,5},{8,10},{9,11},{10,... | collective-permute-start | bytes 645128 | tf_op jit(solution)/shard_map/ppermute | solution.py:958
  156.9 18.1 %collective-permute-start.30 = (bf16[5,24,896]{2,1,0:T(8,128)(2,1)S(1)}, bf16[5,24,896]{2,1,0:T(8,128)(2,1)S(1)}, u32[]{:S(2)}, u32[]{:S(2)}) collective-permute-start(bf16[5,24,896]{2,1,0:T(8,128)(2,1)S(1)} %get-tuple-element.226), channel_id=1, source_target_pairs={{0,4},{1,5},{2,6},{3,7},{4,0},{5,1},{6,2},{7,3},{8,12},{9,13},{10,... | collective-permute-start | bytes 645128 | tf_op jit(solution)/shard_map/ppermute | solution.py:958
  157.5 17.6 %collective-permute-start.31 = (bf16[5,24,896]{2,1,0:T(8,128)(2,1)S(1)}, bf16[5,24,896]{2,1,0:T(8,128)(2,1)S(1)}, u32[]{:S(2)}, u32[]{:S(2)}) collective-permute-start(bf16[5,24,896]{2,1,0:T(8,128)(2,1)S(1)} %get-tuple-element.227), channel_id=1, source_target_pairs={{0,6},{1,7},{2,4},{3,5},{4,2},{5,3},{6,0},{7,1},{8,14},{9,15},{10,... | collective-permute-start | bytes 645128 | tf_op jit(solution)/shard_map/ppermute | solution.py:958
  158.9 16.0 %collective-permute-start.27 = (bf16[24,1536]{1,0:T(8,128)(2,1)S(1)}, bf16[24,1536]{1,0:T(8,128)(2,1)S(1)}, u32[]{:S(2)}, u32[]{:S(2)}) collective-permute-start(bf16[24,1536]{1,0:T(8,128)(2,1)S(1)} %get-tuple-element.222), channel_id=1, source_target_pairs={{0,16},{1,17},{2,18},{3,19},{4,20},{5,21},{6,22},{7,23},{8,24},{9,... | collective-permute-start | bytes 221192 | tf_op jit(solution)/shard_map/ppermute | solution.py:1000
  161.3 13.7 %collective-permute-start.28 = (bf16[24,1536]{1,0:T(8,128)(2,1)S(1)}, bf16[24,1536]{1,0:T(8,128)(2,1)S(1)}, u32[]{:S(2)}, u32[]{:S(2)}) collective-permute-start(bf16[24,1536]{1,0:T(8,128)(2,1)S(1)} %get-tuple-element.223), channel_id=1, source_target_pairs={{0,24},{1,25},{2,26},{3,27},{4,28},{5,29},{6,30},{7,31},{8,0},{9,1... | collective-permute-start | bytes 221192 | tf_op jit(solution)/shard_map/ppermute | solution.py:1000
  179.6 23.6 %collective-permute-start.36 = (bf16[4,24,1536]{2,1,0:T(8,128)(2,1)S(1)}, bf16[4,24,1536]{2,1,0:T(8,128)(2,1)S(1)}, u32[]{:S(2)}, u32[]{:S(2)}) collective-permute-start(bf16[4,24,1536]{2,1,0:T(8,128)(2,1)S(1)} %get-tuple-element.251), channel_id=1, source_target_pairs={{0,2},{1,3},{2,0},{3,1},{4,6},{5,7},{6,4},{7,5},{8,10},{9,11},{10,... | collective-permute-start | bytes 884744 | tf_op jit(solution)/shard_map/ppermute | solution.py:958
  181.2 22.1 %collective-permute-start.37 = (bf16[4,24,1536]{2,1,0:T(8,128)(2,1)S(1)}, bf16[4,24,1536]{2,1,0:T(8,128)(2,1)S(1)}, u32[]{:S(2)}, u32[]{:S(2)}) collective-permute-start(bf16[4,24,1536]{2,1,0:T(8,128)(2,1)S(1)} %get-tuple-element.252), channel_id=1, source_target_pairs={{0,4},{1,5},{2,6},{3,7},{4,0},{5,1},{6,2},{7,3},{8,12},{9,13},{10,... | collective-permute-start | bytes 884744 | tf_op jit(solution)/shard_map/ppermute | solution.py:958
  181.7 21.6 %collective-permute-start.38 = (bf16[4,24,1536]{2,1,0:T(8,128)(2,1)S(1)}, bf16[4,24,1536]{2,1,0:T(8,128)(2,1)S(1)}, u32[]{:S(2)}, u32[]{:S(2)}) collective-permute-start(bf16[4,24,1536]{2,1,0:T(8,128)(2,1)S(1)} %get-tuple-element.253), channel_id=1, source_target_pairs={{0,6},{1,7},{2,4},{3,5},{4,2},{5,3},{6,0},{7,1},{8,14},{9,15},{10,... | collective-permute-start | bytes 884744 | tf_op jit(solution)/shard_map/ppermute | solution.py:958
  183.2 20.1 %collective-permute-start.34 = (bf16[24,2432]{1,0:T(8,128)(2,1)S(1)}, bf16[24,2432]{1,0:T(8,128)(2,1)S(1)}, u32[]{:S(2)}, u32[]{:S(2)}) collective-permute-start(bf16[24,2432]{1,0:T(8,128)(2,1)S(1)} %get-tuple-element.248), channel_id=1, source_target_pairs={{0,16},{1,17},{2,18},{3,19},{4,20},{5,21},{6,22},{7,23},{8,24},{9,... | collective-permute-start | bytes 350216 | tf_op jit(solution)/shard_map/ppermute | solution.py:1000
  186.1 17.2 %collective-permute-start.35 = (bf16[24,2432]{1,0:T(8,128)(2,1)S(1)}, bf16[24,2432]{1,0:T(8,128)(2,1)S(1)}, u32[]{:S(2)}, u32[]{:S(2)}) collective-permute-start(bf16[24,2432]{1,0:T(8,128)(2,1)S(1)} %get-tuple-element.249), channel_id=1, source_target_pairs={{0,24},{1,25},{2,26},{3,27},{4,28},{5,29},{6,30},{7,31},{8,0},{9,1... | collective-permute-start | bytes 350216 | tf_op jit(solution)/shard_map/ppermute | solution.py:1000
  (63 other events, 480.4 us)

commit v6 on v5

--- a/solution.py
+++ b/solution.py
@@ -1029,7 +1029,9 @@
     )
     wire, attn_last, ffn_first = tie((wire, attn_last, ffn_first))
     both, sums = tie((paired(*wire), plane_sums(ffn_first)))
-    attn_first, ffn_first = in_plane(both), in_line(sums)
+    attn_first = in_plane(both)
+    attn_first[1], sums = tie((attn_first[1], sums))
+    ffn_first = in_line(sums)
     attn_first = in_line(with_mods(attn_first))
     width = 2 * D + 128
     own_ffn = jnp.stack([total(ffn_first), total(ffn_last)])

time: 239 us -> 244 us (1.021)
  waiting for transfers between devices: 55.8 us -> 60.3 us
    ppermute x33, waiting for transfers between devices: 26 us -> 33.1 us  [along(): lax.ppermute(value, 'fsdp', [(one, one ^ bit) for one in range(devices)])]
    ppermute x12, waiting for transfers between devices: 12 us -> 9.45 us  [shifted(): lax.ppermute(value, 'fsdp', [(one, (one + 8 * step) % devices) for one in...]
where the time goes in v6:
time: 244 us; the launch traced here: 243 us
  Pallas kernels  95.4 us (39%)
  waiting for transfers between devices  60.3 us (25%)
  starting transfers between devices  52.1 us (21%)
  blocking collectives  17 us (7%)
  local copies, waits for them, and re-layouts  14.8 us (6%)
    ppermute x33, waiting for transfers between devices, along(): lax.ppermute(value, 'fsdp', [(one, one ^ bit) for one in range(devices)])  33.1 us
    pallas_call x2, Pallas kernels, forward_block(): pl.pallas_call(functools.partial(forward_kernel, last=last), grid=(SLOT /...  31.8 us
    pallas_call x2, Pallas kernels, attention_backward(): pl.pallas_call(functools.partial(attention_kernel, chips, first=first), g...  29.9 us
    ppermute x33, starting transfers between devices, along(): lax.ppermute(value, 'fsdp', [(one, one ^ bit) for one in range(devices)])  27.3 us
    pallas_call x2, Pallas kernels, ffn_backward(): pl.pallas_call(functools.partial(ffn_kernel, chips, last=last), grid=(SLO...  21.1 us
    all_to_all x1, blocking collectives, stacked(): lax.all_to_all(copies, 'fsdp', 0, 0, axis_index_groups=lines, tiled=True)  17 us
    ppermute x12, starting transfers between devices, shifted(): lax.ppermute(value, 'fsdp', [(one, (one + 8 * step) % devices) for one in...  16.9 us
    unnamed x74, local copies, waits for them, and re-layouts  14.7 us
  transfers between devices with their start and end apart: 53, of which 21 were waited for; matrix products, arithmetic and copies ran while one was open for 0% of the time, Pallas kernels for 25%

profile of v6, /device:TPU:0, one launch (start us, length us, event | category | flops | bytes accessed | tf_op | source)
XLA Modules:
  0.0 243.5 jit_solution(8493630794011180785)
XLA Ops:
  0.6 2.9 %pack.1 = (bf16[4,24,1792]{2,1,0:T(8,128)(2,1)}, bf16[4,24,1792]{2,1,0:T(8,128)(2,1)}, bf16[4,24,3584]{2,1,0:T(8,128)(2,1)}) custom-call(bf16[2,27648]{1,0:T(2,128)(2,1)} %ada_in.1, bf16[2,13824]{1,0:T(2,128)(2,1)} %qkv_in.1, bf16[2,4608]{1,0:T(2,128)(2,1)} %proj_in.1, bf16[2,18432]{1,0:T(2,128)(2,1)} %fc1_in.1, bf16[2,18432]{1,0:T(2,128)(2,1)} %fc2_in.1, ...), custom_call_target="tpu_custom_call" | custom-call | tf_op jit(solution)/shard_map/pack/pallas_call | solution.py:380
  3.6 17.0 %all_to_all.15.refs_0_ = bf16[4,24,1792]{2,1,0:T(8,128)(2,1)S(1)} all-to-all(bf16[4,24,1792]{2,1,0:T(8,128)(2,1)} %get-tuple-element.151), channel_id=1, replica_groups={{0,8,16,24},{1,9,17,25},{2,10,18,26},{3,11,19,27},{4,12,20,28},{5,13,21..., dimensions={0} | all-to-all | bytes 688128 | tf_op jit(solution)/shard_map/all_to_all | solution.py:961
  20.5 3.5 %all-to-all-start.1 = ((bf16[4,24,1792]{2,1,0:T(8,128)(2,1)}), bf16[4,24,1792]{2,1,0:T(8,128)(2,1)S(1)}, u32[]{:S(2)}, u32[]{:S(2)}) async-start(bf16[4,24,1792]{2,1,0:T(8,128)(2,1)} %get-tuple-element.153), calls=%async_computation.1 | async-start | bytes 688128 | tf_op jit(solution)/shard_map/all_to_all | solution.py:961
  27.6 6.2 %all-to-all-done.1.refs_8_ = bf16[4,24,1792]{2,1,0:T(8,128)(2,1)S(1)} async-done(((bf16[4,24,1792]{2,1,0:T(8,128)(2,1)}), bf16[4,24,1792]{2,1,0:T(8,128)(2,1)S(1)}, u32[]{:S(2)}, u32[]{:S(2)}) %all-to-all-start.1) | async-done | bytes 344096 | tf_op jit(solution)/shard_map/all_to_all | solution.py:961
  33.8 3.5 %all-to-all-start.2 = ((bf16[4,24,3584]{2,1,0:T(8,128)(2,1)}), bf16[4,24,3584]{2,1,0:T(8,128)(2,1)S(1)}, u32[]{:S(2)}, u32[]{:S(2)}) async-start(bf16[4,24,3584]{2,1,0:T(8,128)(2,1)} %get-tuple-element.155), calls=%async_computation.2 | async-start | bytes 1376256 | tf_op jit(solution)/shard_map/all_to_all | solution.py:961
  37.3 4.1 %collective-permute-done.4.refs_2_ = bf16[4,24,1792]{2,1,0:T(8,128)(2,1)S(1)} collective-permute-done((bf16[4,24,1792]{2,1,0:T(8,128)(2,1)S(1)}, bf16[4,24,1792]{2,1,0:T(8,128)(2,1)S(1)}, u32[]{:S(2)}, u32[]{:S(2)}) %collective-permute-start.4) | collective-permute-done | bytes 344096 | tf_op jit(solution)/shard_map/ppermute | solution.py:958
  45.4 7.0 %collective-permute-done.10.refs_9_ = bf16[4,24,1792]{2,1,0:T(8,128)(2,1)S(1)} collective-permute-done((bf16[4,24,1792]{2,1,0:T(8,128)(2,1)S(1)}, bf16[4,24,1792]{2,1,0:T(8,128)(2,1)S(1)}, u32[]{:S(2)}, u32[]{:S(2)}) %collective-permute-start.10) | collective-permute-done | bytes 344096 | tf_op jit(solution)/shard_map/ppermute | solution.py:958
  52.4 5.1 %collective-permute-done.11.refs_10_ = bf16[4,24,1792]{2,1,0:T(8,128)(2,1)S(1)} collective-permute-done((bf16[4,24,1792]{2,1,0:T(8,128)(2,1)S(1)}, bf16[4,24,1792]{2,1,0:T(8,128)(2,1)S(1)}, u32[]{:S(2)}, u32[]{:S(2)}) %collective-permute-start.11) | collective-permute-done | bytes 344096 | tf_op jit(solution)/shard_map/ppermute | solution.py:958
  67.9 3.1 %unpack.2 = (bf16[384,2688]{1,0:T(8,128)(2,1)S(1)}, bf16[384,2688]{1,0:T(8,128)(2,1)S(1)}, bf16[1536,384]{1,0:T(8,128)(2,1)S(1)}, f32[1,5376]{1,0:T(1,128)S(1)}, f32[2,64,384]{2,1,0:T(8,128)S(1)}) custom-call(s32[3]{0:T(128)S(1)} %pad_add_fusion.place.core, bf16[4,24,1792]{2,1,0:T(8,128)(2,1)S(1)} %all_to_all.15.refs_0_, ...), custom_call_target="tpu_custom_call" | custom-call | tf_op jit(solution)/shard_map/unpack/pallas_call | solution.py:438
  71.7 15.8 %forward_block.2 = (f32[4,256,384]{2,1,0:T(8,128)S(1)}, f32[4,2304]{1,0:T(4,128)S(1)}, bf16[4,256,1152]{2,1,0:T(8,128)(2,1)S(1)}, bf16[4,256,384]{2,1,0:T(8,128)...) custom-call(s32[1]{0:T(128)S(6)} %copy.47.counts, ...), custom_call_target="tpu_custom_call" | custom-call | flops 5000000000 | bytes 20971520 | tf_op jit(solution)/shard_map/forward_block/pallas_call | solution.py:589
  98.8 3.9 %unpack.3 = (bf16[384,2688]{1,0:T(8,128)(2,1)S(1)}, bf16[384,2688]{1,0:T(8,128)(2,1)S(1)}, bf16[1536,384]{1,0:T(8,128)(2,1)S(1)}, f32[1,5376]{1,0:T(1,128)S(1)}, f32[2,64,384]{2,1,0:T(8,128)}) custom-call(s32[3]{0:T(128)S(1)} %pad_add_fusion.place.core, bf16[4,24,3584]{2,1,0:T(8,128)(2,1)S(1)} %all-to-all-done.2.refs_0_, ...), custom_call_target="tpu_custom_call" | custom-call | tf_op jit(solution)/shard_map/unpack/pallas_call | solution.py:438
  102.7 16.0 %forward_block.3 = (f32[4,256,384]{2,1,0:T(8,128)}, f32[4,2304]{1,0:T(4,128)S(1)}, bf16[4,256,1152]{2,1,0:T(8,128)(2,1)S(1)}, bf16[4,256,384]{2,1,0:T(8,128)(2,1...) custom-call(s32[1]{0:T(128)S(6)} %copy.47.counts, ...), custom_call_target="tpu_custom_call" | custom-call | flops 5000000000 | bytes 20971520 | tf_op jit(solution)/shard_map/forward_block/pallas_call | solution.py:589
  121.3 10.1 %ffn_backward.2 = (f32[4,256,384]{2,1,0:T(8,128)S(1)}, f32[24,384]{1,0:T(8,128)S(1)}, f32[1,1920]{1,0:T(1,128)S(1)}, bf16[4,4,24,1536]{3,2,1,0:T(8,128)(2,1)S(1)}, bf16[4,4,24,1536]{3,2,1,0:T(8,128)(2,1)S(1)}) custom-call(s32[3]{0:T(128)S(1)} %pad_add_fusion.place.core, s32[1]{0:T(128)S(6)} %copy.47.counts, bf16[4,256,384]{2,1,0:T(8,128)(2,1)S(1)} %copy-done.13, ...), custom_call_target="tpu_custom_call" | custom-call | flops 8000000000 | bytes 20971520 | tf_op jit(solution)/shard_map/ffn_backward/pallas_call | solution.py:695
  131.6 2.7 %collective-permute-done.21 = bf16[4,4,24,1536]{3,2,1,0:T(8,128)(2,1)S(1)} collective-permute-done((bf16[4,4,24,1536]{3,2,1,0:T(8,128)(2,1)S(1)}, bf16[4,4,24,1536]{3,2,1,0:T(8,128)(2,1)S(1)}, u32[]{:S(2)}, u32[]{:S(2)}) %collective-permute-start.21) | collective-permute-done | bytes 1179680 | tf_op jit(solution)/shard_map/ppermute | solution.py:992
  138.3 13.1 %attention_backward.2 = (f32[4,256,384]{2,1,0:T(8,128)S(1)}, f32[4,384]{1,0:T(4,128)S(1)}, bf16[4,5,24,896]{3,2,1,0:T(8,128)(2,1)S(1)}, bf16[4,5,24,896]{3,2,1,0:T(8,128)(2,1)S(1)}) custom-call(s32[3]{0:T(128)S(1)} %pad_add_fusion.place.core, f32[4,256,384]{2,1,0:T(8,128)S(1)} %get-tuple-element.196.d_middle, f32[4,256,384]{2,1,0:T(8,128)S(1)} %copy-done.22, ...), custom_call_target="tpu_custom_call" | custom-call | flops 6000000000 | bytes 20971520 | tf_op jit(solution)/shard_map/attention_backward/pallas_call | solution.py:832
  158.9 2.4 collective-permute-start.27
  162.8 11.0 %ffn_backward.3 = (f32[4,256,384]{2,1,0:T(8,128)S(1)}, f32[24,384]{1,0:T(8,128)S(1)}, f32[1,1920]{1,0:T(1,128)S(1)}, bf16[4,4,24,1536]{3,2,1,0:T(8,128)(2,1)S(1)}, bf16[4,4,24,1536]{3,2,1,0:T(8,128)(2,1)}) custom-call(s32[3]{0:T(128)S(1)} %pad_add_fusion.place.core, s32[1]{0:T(128)S(6)} %copy.47.counts, f32[4,256,384]{2,1,0:T(8,128)S(1)} %get-tuple-element.216.upstream, ...), custom_call_target="tpu_custom_call" | custom-call | flops 8000000000 | bytes 20971520 | tf_op jit(solution)/shard_map/ffn_backward/pallas_call | solution.py:695
  175.9 2.8 %collective-permute-done.32 = bf16[4,4,24,1536]{3,2,1,0:T(8,128)(2,1)S(1)} collective-permute-done((bf16[4,4,24,1536]{3,2,1,0:T(8,128)(2,1)}, bf16[4,4,24,1536]{3,2,1,0:T(8,128)(2,1)S(1)}, u32[]{:S(2)}, u32[]{:S(2)}) %collective-permute-start.32) | collective-permute-done | bytes 1179680 | tf_op jit(solution)/shard_map/ppermute | solution.py:992
  186.5 16.8 %attention_backward.3 = (f32[4,256,384]{2,1,0:T(8,128)}, f32[4,384]{1,0:T(4,128)}, bf16[4,5,24,896]{3,2,1,0:T(8,128)(2,1)}, bf16[4,5,24,896]{3,2,1,0:T(8,128)(2,1)}) custom-call(s32[3]{0:T(128)S(1)} %pad_add_fusion.place.core, f32[4,256,384]{2,1,0:T(8,128)} %copy-done.24, bf16[4,256,384]{2,1,0:T(8,128)(2,1)S(1)} %copy-done.15, ...), custom_call_target="tpu_custom_call" | custom-call | flops 6000000000 | bytes 20971520 | tf_op jit(solution)/shard_map/attention_backward/pallas_call | solution.py:832
  209.7 4.6 %collective-permute-done.40 = bf16[5,24,896]{2,1,0:T(8,128)(2,1)S(1)} collective-permute-done((bf16[5,24,896]{2,1,0:T(8,128)(2,1)S(1)}, bf16[5,24,896]{2,1,0:T(8,128)(2,1)S(1)}, u32[]{:S(2)}, u32[]{:S(2)}) %collective-permute-start.40) | collective-permute-done | bytes 215072 | tf_op jit(solution)/shard_map/ppermute | solution.py:958
  214.4 4.9 %collective-permute-done.45 = bf16[5,24,896]{2,1,0:T(8,128)(2,1)S(1)} collective-permute-done((bf16[5,24,896]{2,1,0:T(8,128)(2,1)S(1)}, bf16[5,24,896]{2,1,0:T(8,128)(2,1)S(1)}, u32[]{:S(2)}, u32[]{:S(2)}) %collective-permute-start.45) | collective-permute-done | bytes 215072 | tf_op jit(solution)/shard_map/ppermute | solution.py:958
  227.9 3.6 %collective-permute-done.41 = bf16[24,1536]{1,0:T(8,128)(2,1)S(1)} collective-permute-done((bf16[24,1536]{1,0:T(8,128)(2,1)S(1)}, bf16[24,1536]{1,0:T(8,128)(2,1)S(1)}, u32[]{:S(2)}, u32[]{:S(2)}) %collective-permute-start.41) | collective-permute-done | bytes 73760 | tf_op jit(solution)/shard_map/ppermute | solution.py:1000
  231.4 3.1 %collective-permute-start.46 = (bf16[24,2432]{1,0:T(8,128)(2,1)S(1)}, bf16[24,2432]{1,0:T(8,128)(2,1)S(1)}, u32[]{:S(2)}, u32[]{:S(2)}) collective-permute-start(bf16[24,2432]{1,0:T(8,128)(2,1)S(1)} %get-tuple-element.324), channel_id=1, source_target_pairs={{0,8},{1,9},{2,10},{3,11},{4,12},{5,13},{6,14},{7,15},{8,16},{9,17... | collective-permute-start | bytes 350216 | tf_op jit(solution)/shard_map/ppermute | solution.py:1000
  240.7 2.8 %finish.1 = (f32[2,27648]{1,0:T(2,128)}, f32[2,13824]{1,0:T(2,128)}, f32[2,4608]{1,0:T(2,128)}, f32[2,18432]{1,0:T(2,128)}, f32[2,18432]{1,0:T(2,128)}, /*index=5*/f32[2,256]{1,0:T(2,128)}) custom-call(s32[3]{0:T(128)S(1)} %pad_add_fusion.place.core, f32[2,24,1536]{2,1,0:T(8,128)S(1)} %pad_maximum_fusion.1.own_ffn, ...), custom_call_target="tpu_custom_call" | custom-call | tf_op jit(solution)/shard_map/finish/pallas_call | solution.py:934
  (202 shorter events, 75.8 us)
Async XLA Ops:
  25.6 15.8 %collective-permute-start.4 = (bf16[4,24,1792]{2,1,0:T(8,128)(2,1)S(1)}, bf16[4,24,1792]{2,1,0:T(8,128)(2,1)S(1)}, u32[]{:S(2)}, u32[]{:S(2)}) collective-permute-start(bf16[4,24,1792]{2,1,0:T(8,128)(2,1)S(1)} %all_to_all.15.refs_0_), channel_id=1, source_target_pairs={{0,4},{1,5},{2,6},{3,7},{4,0},{5,1},{6,2},{7,3},{8,12},{9,13},{10,... | collective-permute-start | bytes 1032200 | tf_op jit(solution)/shard_map/ppermute | solution.py:958
  27.1 14.3 %collective-permute-start.5 = (bf16[4,24,1792]{2,1,0:T(8,128)(2,1)S(1)}, bf16[4,24,1792]{2,1,0:T(8,128)(2,1)S(1)}, u32[]{:S(2)}, u32[]{:S(2)}) collective-permute-start(bf16[4,24,1792]{2,1,0:T(8,128)(2,1)S(1)} %all_to_all.15.refs_0_), channel_id=1, source_target_pairs={{0,6},{1,7},{2,4},{3,5},{4,2},{5,3},{6,0},{7,1},{8,14},{9,15},{10,... | collective-permute-start | bytes 1032200 | tf_op jit(solution)/shard_map/ppermute | solution.py:958
  33.8 27.0 %all-to-all-start.2 = ((bf16[4,24,3584]{2,1,0:T(8,128)(2,1)}), bf16[4,24,3584]{2,1,0:T(8,128)(2,1)S(1)}, u32[]{:S(2)}, u32[]{:S(2)}) async-start(bf16[4,24,3584]{2,1,0:T(8,128)(2,1)} %get-tuple-element.155), calls=%async_computation.2 | async-start | bytes 1376256 | tf_op jit(solution)/shard_map/all_to_all | solution.py:961
  42.6 14.9 %collective-permute-start.11 = (bf16[4,24,1792]{2,1,0:T(8,128)(2,1)S(1)}, bf16[4,24,1792]{2,1,0:T(8,128)(2,1)S(1)}, u32[]{:S(2)}, u32[]{:S(2)}) collective-permute-start(bf16[4,24,1792]{2,1,0:T(8,128)(2,1)S(1)} %all-to-all-done.1.refs_8_), channel_id=1, source_target_pairs={{0,4},{1,5},{2,6},{3,7},{4,0},{5,1},{6,2},{7,3},{8,12},{9,13},{10,... | collective-permute-start | bytes 1032200 | tf_op jit(solution)/shard_map/ppermute | solution.py:958
  43.4 14.0 %collective-permute-start.12 = (bf16[4,24,1792]{2,1,0:T(8,128)(2,1)S(1)}, bf16[4,24,1792]{2,1,0:T(8,128)(2,1)S(1)}, u32[]{:S(2)}, u32[]{:S(2)}) collective-permute-start(bf16[4,24,1792]{2,1,0:T(8,128)(2,1)S(1)} %all-to-all-done.1.refs_8_), channel_id=1, source_target_pairs={{0,6},{1,7},{2,4},{3,5},{4,2},{5,3},{6,0},{7,1},{8,14},{9,15},{10,... | collective-permute-start | bytes 1032200 | tf_op jit(solution)/shard_map/ppermute | solution.py:958
  44.9 13.9 %collective-permute-start.6 = (bf16[4,24,1792]{2,1,0:T(8,128)(2,1)S(1)}, bf16[4,24,1792]{2,1,0:T(8,128)(2,1)S(1)}, u32[]{:S(2)}, u32[]{:S(2)}) collective-permute-start(bf16[4,24,1792]{2,1,0:T(8,128)(2,1)S(1)} %all_to_all.15.refs_0_), channel_id=1, source_target_pairs={{0,1},{1,0},{2,3},{3,2},{4,5},{5,4},{6,7},{7,6},{8,9},{9,8},{10,11... | collective-permute-start | bytes 1032200 | tf_op jit(solution)/shard_map/ppermute | solution.py:958
  60.8 31.1 %collective-permute-start = (bf16[4,24,3584]{2,1,0:T(8,128)(2,1)S(1)}, bf16[4,24,3584]{2,1,0:T(8,128)(2,1)S(1)}, u32[]{:S(2)}, u32[]{:S(2)}) collective-permute-start(bf16[4,24,3584]{2,1,0:T(8,128)(2,1)S(1)} %all-to-all-done.2.refs_0_), channel_id=1, source_target_pairs={{0,2},{1,3},{2,0},{3,1},{4,6},{5,7},{6,4},{7,5},{8,10},{9,11},{10,... | collective-permute-start | bytes 2064392 | tf_op jit(solution)/shard_map/ppermute | solution.py:958
  61.4 32.3 %collective-permute-start.1 = (bf16[4,24,3584]{2,1,0:T(8,128)(2,1)S(1)}, bf16[4,24,3584]{2,1,0:T(8,128)(2,1)S(1)}, u32[]{:S(2)}, u32[]{:S(2)}) collective-permute-start(bf16[4,24,3584]{2,1,0:T(8,128)(2,1)S(1)} %all-to-all-done.2.refs_0_), channel_id=1, source_target_pairs={{0,4},{1,5},{2,6},{3,7},{4,0},{5,1},{6,2},{7,3},{8,12},{9,13},{10,... | collective-permute-start | bytes 2064392 | tf_op jit(solution)/shard_map/ppermute | solution.py:958
  62.9 30.8 %collective-permute-start.2 = (bf16[4,24,3584]{2,1,0:T(8,128)(2,1)S(1)}, bf16[4,24,3584]{2,1,0:T(8,128)(2,1)S(1)}, u32[]{:S(2)}, u32[]{:S(2)}) collective-permute-start(bf16[4,24,3584]{2,1,0:T(8,128)(2,1)S(1)} %all-to-all-done.2.refs_0_), channel_id=1, source_target_pairs={{0,6},{1,7},{2,4},{3,5},{4,2},{5,3},{6,0},{7,1},{8,14},{9,15},{10,... | collective-permute-start | bytes 2064392 | tf_op jit(solution)/shard_map/ppermute | solution.py:958
  134.7 16.7 %collective-permute-start.22 = (bf16[4,24,1536]{2,1,0:T(8,128)(2,1)S(1)}, bf16[4,24,1536]{2,1,0:T(8,128)(2,1)S(1)}, u32[]{:S(2)}, u32[]{:S(2)}) collective-permute-start(bf16[4,24,1536]{2,1,0:T(8,128)(2,1)S(1)} %get-tuple-element.206), channel_id=1, source_target_pairs={{0,2},{1,3},{2,0},{3,1},{4,6},{5,7},{6,4},{7,5},{8,10},{9,11},{10,... | collective-permute-start | bytes 884744 | tf_op jit(solution)/shard_map/ppermute | solution.py:958
  136.2 15.2 %collective-permute-start.23 = (bf16[4,24,1536]{2,1,0:T(8,128)(2,1)S(1)}, bf16[4,24,1536]{2,1,0:T(8,128)(2,1)S(1)}, u32[]{:S(2)}, u32[]{:S(2)}) collective-permute-start(bf16[4,24,1536]{2,1,0:T(8,128)(2,1)S(1)} %get-tuple-element.207), channel_id=1, source_target_pairs={{0,4},{1,5},{2,6},{3,7},{4,0},{5,1},{6,2},{7,3},{8,12},{9,13},{10,... | collective-permute-start | bytes 884744 | tf_op jit(solution)/shard_map/ppermute | solution.py:958
  136.8 14.6 %collective-permute-start.24 = (bf16[4,24,1536]{2,1,0:T(8,128)(2,1)S(1)}, bf16[4,24,1536]{2,1,0:T(8,128)(2,1)S(1)}, u32[]{:S(2)}, u32[]{:S(2)}) collective-permute-start(bf16[4,24,1536]{2,1,0:T(8,128)(2,1)S(1)} %get-tuple-element.208), channel_id=1, source_target_pairs={{0,6},{1,7},{2,4},{3,5},{4,2},{5,3},{6,0},{7,1},{8,14},{9,15},{10,... | collective-permute-start | bytes 884744 | tf_op jit(solution)/shard_map/ppermute | solution.py:958
  155.4 19.5 %collective-permute-start.29 = (bf16[5,24,896]{2,1,0:T(8,128)(2,1)S(1)}, bf16[5,24,896]{2,1,0:T(8,128)(2,1)S(1)}, u32[]{:S(2)}, u32[]{:S(2)}) collective-permute-start(bf16[5,24,896]{2,1,0:T(8,128)(2,1)S(1)} %get-tuple-element.230), channel_id=1, source_target_pairs={{0,2},{1,3},{2,0},{3,1},{4,6},{5,7},{6,4},{7,5},{8,10},{9,11},{10,... | collective-permute-start | bytes 645128 | tf_op jit(solution)/shard_map/ppermute | solution.py:958
  156.9 18.1 %collective-permute-start.30 = (bf16[5,24,896]{2,1,0:T(8,128)(2,1)S(1)}, bf16[5,24,896]{2,1,0:T(8,128)(2,1)S(1)}, u32[]{:S(2)}, u32[]{:S(2)}) collective-permute-start(bf16[5,24,896]{2,1,0:T(8,128)(2,1)S(1)} %get-tuple-element.231), channel_id=1, source_target_pairs={{0,4},{1,5},{2,6},{3,7},{4,0},{5,1},{6,2},{7,3},{8,12},{9,13},{10,... | collective-permute-start | bytes 645128 | tf_op jit(solution)/shard_map/ppermute | solution.py:958
  157.5 17.6 %collective-permute-start.31 = (bf16[5,24,896]{2,1,0:T(8,128)(2,1)S(1)}, bf16[5,24,896]{2,1,0:T(8,128)(2,1)S(1)}, u32[]{:S(2)}, u32[]{:S(2)}) collective-permute-start(bf16[5,24,896]{2,1,0:T(8,128)(2,1)S(1)} %get-tuple-element.232), channel_id=1, source_target_pairs={{0,6},{1,7},{2,4},{3,5},{4,2},{5,3},{6,0},{7,1},{8,14},{9,15},{10,... | collective-permute-start | bytes 645128 | tf_op jit(solution)/shard_map/ppermute | solution.py:958
  158.9 16.0 %collective-permute-start.27 = (bf16[24,1536]{1,0:T(8,128)(2,1)S(1)}, bf16[24,1536]{1,0:T(8,128)(2,1)S(1)}, u32[]{:S(2)}, u32[]{:S(2)}) collective-permute-start(bf16[24,1536]{1,0:T(8,128)(2,1)S(1)} %get-tuple-element.227), channel_id=1, source_target_pairs={{0,16},{1,17},{2,18},{3,19},{4,20},{5,21},{6,22},{7,23},{8,24},{9,... | collective-permute-start | bytes 221192 | tf_op jit(solution)/shard_map/ppermute | solution.py:1000
  161.3 13.7 %collective-permute-start.28 = (bf16[24,1536]{1,0:T(8,128)(2,1)S(1)}, bf16[24,1536]{1,0:T(8,128)(2,1)S(1)}, u32[]{:S(2)}, u32[]{:S(2)}) collective-permute-start(bf16[24,1536]{1,0:T(8,128)(2,1)S(1)} %get-tuple-element.228), channel_id=1, source_target_pairs={{0,24},{1,25},{2,26},{3,27},{4,28},{5,29},{6,30},{7,31},{8,0},{9,1... | collective-permute-start | bytes 221192 | tf_op jit(solution)/shard_map/ppermute | solution.py:1000
  179.6 23.6 %collective-permute-start.36 = (bf16[4,24,1536]{2,1,0:T(8,128)(2,1)S(1)}, bf16[4,24,1536]{2,1,0:T(8,128)(2,1)S(1)}, u32[]{:S(2)}, u32[]{:S(2)}) collective-permute-start(bf16[4,24,1536]{2,1,0:T(8,128)(2,1)S(1)} %get-tuple-element.256), channel_id=1, source_target_pairs={{0,2},{1,3},{2,0},{3,1},{4,6},{5,7},{6,4},{7,5},{8,10},{9,11},{10,... | collective-permute-start | bytes 884744 | tf_op jit(solution)/shard_map/ppermute | solution.py:958
  181.2 22.1 %collective-permute-start.37 = (bf16[4,24,1536]{2,1,0:T(8,128)(2,1)S(1)}, bf16[4,24,1536]{2,1,0:T(8,128)(2,1)S(1)}, u32[]{:S(2)}, u32[]{:S(2)}) collective-permute-start(bf16[4,24,1536]{2,1,0:T(8,128)(2,1)S(1)} %get-tuple-element.257), channel_id=1, source_target_pairs={{0,4},{1,5},{2,6},{3,7},{4,0},{5,1},{6,2},{7,3},{8,12},{9,13},{10,... | collective-permute-start | bytes 884744 | tf_op jit(solution)/shard_map/ppermute | solution.py:958
  181.7 21.6 %collective-permute-start.38 = (bf16[4,24,1536]{2,1,0:T(8,128)(2,1)S(1)}, bf16[4,24,1536]{2,1,0:T(8,128)(2,1)S(1)}, u32[]{:S(2)}, u32[]{:S(2)}) collective-permute-start(bf16[4,24,1536]{2,1,0:T(8,128)(2,1)S(1)} %get-tuple-element.258), channel_id=1, source_target_pairs={{0,6},{1,7},{2,4},{3,5},{4,2},{5,3},{6,0},{7,1},{8,14},{9,15},{10,... | collective-permute-start | bytes 884744 | tf_op jit(solution)/shard_map/ppermute | solution.py:958
  183.2 20.1 %collective-permute-start.34 = (bf16[24,2432]{1,0:T(8,128)(2,1)S(1)}, bf16[24,2432]{1,0:T(8,128)(2,1)S(1)}, u32[]{:S(2)}, u32[]{:S(2)}) collective-permute-start(bf16[24,2432]{1,0:T(8,128)(2,1)S(1)} %get-tuple-element.253), channel_id=1, source_target_pairs={{0,16},{1,17},{2,18},{3,19},{4,20},{5,21},{6,22},{7,23},{8,24},{9,... | collective-permute-start | bytes 350216 | tf_op jit(solution)/shard_map/ppermute | solution.py:1000
  186.1 17.2 %collective-permute-start.35 = (bf16[24,2432]{1,0:T(8,128)(2,1)S(1)}, bf16[24,2432]{1,0:T(8,128)(2,1)S(1)}, u32[]{:S(2)}, u32[]{:S(2)}) collective-permute-start(bf16[24,2432]{1,0:T(8,128)(2,1)S(1)} %get-tuple-element.254), channel_id=1, source_target_pairs={{0,24},{1,25},{2,26},{3,27},{4,28},{5,29},{6,30},{7,31},{8,0},{9,1... | collective-permute-start | bytes 350216 | tf_op jit(solution)/shard_map/ppermute | solution.py:1000
  220.8 16.0 %collective-permute-start.48 = (bf16[24,2432]{1,0:T(8,128)(2,1)S(1)}, bf16[24,2432]{1,0:T(8,128)(2,1)S(1)}, u32[]{:S(2)}, u32[]{:S(2)}) collective-permute-start(bf16[24,2432]{1,0:T(8,128)(2,1)S(1)} %get-tuple-element.326), channel_id=1, source_target_pairs={{0,24},{1,25},{2,26},{3,27},{4,28},{5,29},{6,30},{7,31},{8,0},{9,1... | collective-permute-start | bytes 350216 | tf_op jit(solution)/shard_map/ppermute | solution.py:1000
  222.0 14.8 %collective-permute-start.47 = (bf16[24,2432]{1,0:T(8,128)(2,1)S(1)}, bf16[24,2432]{1,0:T(8,128)(2,1)S(1)}, u32[]{:S(2)}, u32[]{:S(2)}) collective-permute-start(bf16[24,2432]{1,0:T(8,128)(2,1)S(1)} %get-tuple-element.325), channel_id=1, source_target_pairs={{0,16},{1,17},{2,18},{3,19},{4,20},{5,21},{6,22},{7,23},{8,24},{9,... | collective-permute-start | bytes 350216 | tf_op jit(solution)/shard_map/ppermute | solution.py:1000
  (63 other events, 498.7 us)
